TPU v7x, 32 devices: a whole 2x2x4 slice. The times are simulated.
32 devices in a mesh: shot: 4 (over y, core), gx: 4 (over z), gy: 2 (over x).
Axes of the slice: x: 2, y: 2, z: 4, core: 2. Of those that a mesh axis runs over, the one named last changes fastest.
Arguments:
- model_tiles: float32 [256, 64, 128], P(('shot', 'gx'), 'gy'), may hold values from 0.2 to 0.45
- owner_map: int32 [16], replicated, may hold values from 0 to 15, each once
- offsets: int32 [4], P('shot'), may hold values from 0 to 12
- field_now: float32 [4, 2, 64, 64, 128], P('shot', None, 'gx', 'gy'), may hold values from -6 to 6
- field_prev: float32 [4, 2, 64, 64, 128], P('shot', None, 'gx', 'gy'), may hold values from -6 to 6
- sources: int32 [4, 2, 3], P('shot'), may hold values from 0 to 127, as said below
- wavelet: float32 [4, 2, 8], P('shot'), may hold values from -6 to 6
- receivers: int32 [4, 256, 3], P('shot'), may hold values from 0 to 127, as said below
Outputs:
- out_now: float32 [4, 2, 64, 64, 128], P('shot', None, 'gx', 'gy')
- out_prev: float32 [4, 2, 64, 64, 128], P('shot', None, 'gx', 'gy')
- traces: float32 [4, 2, 256, 8], P('shot')
Inputs may be any that keep to these rules, and one draw needn't show every extreme that they name: `sources`: each row is a cell of the group's aperture: first entry below 64, second below 64, third below 128. `receivers`: each row is a cell of the group's aperture: first entry below 64, second below 64, third below 128.
All inputs are finite; a program needn't handle non-finite values.
Results may differ from a plain program's by a relative error of at most 0.0003.
Values sent between devices are 32-bit elements; how exact they have to be, the bound alone decides.
No kernel may reach another device: no remote copies, remote signals or barrier semaphores. Data moves between devices by JAX's collectives and lax.ppermute only.
A program may use at most 128 MiB of HBM per device.

v0:
```python
import jax
import jax.numpy as jnp
from jax import lax
from jax.sharding import PartitionSpec as P

STEPS = 8


center_weight = -2.5
near_weight = 4.0 / 3.0
far_weight = -1.0 / 12.0
damp_peak = 0.3


def extended_2(cells, sides, width):
    for axis, dim in sides:
        count = lax.axis_size(axis)
        ends = count - 1
        head = lax.slice_in_dim(cells, 0, width, axis=dim)
        tail = lax.slice_in_dim(cells, cells.shape[dim] - width, cells.shape[dim], axis=dim)
        cells = jnp.concatenate(
            [
                lax.ppermute(tail, axis, [(i, (i + 1) % count) for i in range(ends)]),
                cells,
                lax.ppermute(head, axis, [((i + 1) % count, i) for i in range(ends)]),
            ],
            axis=dim,
        )
    return cells


def depth_ahead(field, reach):
    filler = jnp.zeros(field.shape[:-1] + (reach,), field.dtype)
    return jnp.concatenate([field[..., reach:], filler], axis=-1)


def depth_behind(field, reach):
    filler = jnp.zeros(field.shape[:-1] + (reach,), field.dtype)
    return jnp.concatenate([filler, field[..., :-reach]], axis=-1)


def laplace(extended):
    middle = extended[:, 2:-2, 2:-2]
    along_x = (
        center_weight * middle
        + near_weight * (extended[:, 3:-1, 2:-2] + extended[:, 1:-3, 2:-2])
        + far_weight * (extended[:, 4:, 2:-2] + extended[:, :-4, 2:-2])
    )
    along_y = (
        center_weight * middle
        + near_weight * (extended[:, 2:-2, 3:-1] + extended[:, 2:-2, 1:-3])
        + far_weight * (extended[:, 2:-2, 4:] + extended[:, 2:-2, :-4])
    )
    along_z = (
        center_weight * middle
        + near_weight * (depth_ahead(middle, 1) + depth_behind(middle, 1))
        + far_weight * (depth_ahead(middle, 2) + depth_behind(middle, 2))
    )
    return along_x + along_y + along_z


def damping(x_cells, y_cells, width, x_total, y_total):
    x_depth = (
        jnp.maximum(width - jnp.minimum(x_cells + 1, x_total - x_cells), 0).astype(jnp.float32)
        / width
    )
    y_depth = (
        jnp.maximum(width - jnp.minimum(y_cells + 1, y_total - y_cells), 0).astype(jnp.float32)
        / width
    )
    return damp_peak * (x_depth[:, None] * x_depth[:, None] + y_depth[None, :] * y_depth[None, :])


def injection(x_cells, y_cells, z_cells, source_cells, amplitude):
    on_x = (x_cells[None, :] == source_cells[:, 0:1]).astype(jnp.float32)
    on_y = (y_cells[None, :] == source_cells[:, 1:2]).astype(jnp.float32)
    on_z = (z_cells[None, :] == source_cells[:, 2:3]).astype(jnp.float32)
    return (
        amplitude[:, None, None, None]
        * on_x[:, :, None, None]
        * on_y[:, None, :, None]
        * on_z[:, None, None, :]
    )


def advance(extended, previous, coef, damp, inject):
    middle = extended[:, 2:-2, 2:-2]
    return (2.0 * middle - (1.0 - damp) * previous + coef * laplace(extended) + inject) / (
        1.0 + damp
    )


def sample(field, receiver_cells, x_start, y_start):
    size_x, size_y = (field.shape[1], field.shape[2])
    local_x = receiver_cells[:, 0] - x_start
    local_y = receiver_cells[:, 1] - y_start
    inside = (local_x >= 0) & (local_x < size_x) & (local_y >= 0) & (local_y < size_y)
    values = field[
        :, jnp.clip(local_x, 0, size_x - 1), jnp.clip(local_y, 0, size_y - 1), receiver_cells[:, 2]
    ]
    return jnp.where(inside[None, :], values, 0.0)


def local(model_tiles, owner_map, offsets, field_now, field_prev, sources, wavelet, receivers):
    block_x, block_y, depth = model_tiles.shape
    column_index = lax.axis_index("gx")
    row_index = lax.axis_index("gy")
    across = lax.axis_size("gx")
    total_x = block_x * across
    total_y = block_y * lax.axis_size("gy")
    shift_x = offsets[0]
    tile_total = owner_map.shape[0]
    column_ids = jnp.arange(tile_total, dtype=jnp.int32)
    group_total = lax.axis_size("shot")
    stacked = lax.all_gather(model_tiles, "shot", axis=0, tiled=True)
    stored = jnp.arange(group_total, dtype=jnp.int32) * across + column_index
    column_of = jnp.sum(
        jnp.where(owner_map[None, :] == stored[:, None], column_ids[None, :], 0), axis=1
    )
    target = column_of - shift_x
    selector = (target[None, :] == jnp.arange(across, dtype=jnp.int32)[:, None]).astype(jnp.float32)
    outgoing = jnp.dot(selector, stacked.reshape(group_total, -1), precision=lax.Precision.HIGHEST)
    outgoing = outgoing.reshape(across * block_x, block_y, depth)
    incoming = lax.all_to_all(outgoing, "gx", split_axis=0, concat_axis=0, tiled=True)
    speed = jnp.sum(incoming.reshape(across, block_x, block_y, depth), axis=0)
    coef = speed * speed
    current = field_now[0]
    previous = field_prev[0]
    source_cells = sources[0]
    amplitudes = wavelet[0]
    receiver_cells = receivers[0]
    x_start = column_index * block_x
    y_start = row_index * block_y
    x_here = x_start + jnp.arange(block_x, dtype=jnp.int32)
    y_here = y_start + jnp.arange(block_y, dtype=jnp.int32)
    z_cells = jnp.arange(depth, dtype=jnp.int32)
    damp = damping(x_here, y_here, block_x, total_x, total_y)[:, :, None]
    recorded = []
    for step in range(STEPS):
        extended = extended_2(current, (("gx", 1), ("gy", 2)), 2)
        inject = injection(x_here, y_here, z_cells, source_cells, amplitudes[:, step])
        fresh = advance(extended, previous, coef, damp, inject)
        recorded.append(sample(fresh, receiver_cells, x_start, y_start))
        previous = current
        current = fresh
    traces = lax.psum(jnp.stack(recorded, axis=-1), ("gx", "gy"))
    return (current[None], previous[None], traces[None])


def solution(mesh):
    return jax.shard_map(
        local,
        mesh=mesh,
        in_specs=(
            P(("shot", "gx"), "gy", None),
            P(),
            P("shot"),
            P("shot", None, "gx", "gy", None),
            P("shot", None, "gx", "gy", None),
            P("shot", None, None),
            P("shot", None, None),
            P("shot", None, None),
        ),
        out_specs=(
            P("shot", None, "gx", "gy", None),
            P("shot", None, "gx", "gy", None),
            P("shot", None, None, None),
        ),
        check_vma=False,
    )
```

profile of v0, /device:TPU:0, one launch (start us, length us, event | category | flops | bytes accessed | tf_op | source)
XLA Modules:
  0.0 392.2 jit_solution(7513996289417220753)
XLA Ops:
  10.1 5.6 %collective-permute-start.1 = (f32[2,2,32,128]{3,2,1,0:T(8,128)S(1)}, f32[2,2,32,128]{3,2,1,0:T(8,128)S(1)}, u32[]{:S(2)}, u32[]{:S(2)}) collective-permute-start(f32[2,2,32,128]{3,2,1,0:T(8,128)S(1)} %get-tuple-element.105), channel_id=1, source_target_pairs={{0,2},{2,4},{4,6},{1,3},{3,5},{5,7},{8,10},{10,12},{12,14},{9,11},... | collective-permute-start | bytes 196616 | tf_op jit(solution)/shard_map/ppermute | solution.py:23
  20.4 8.7 %all-gather.2.cloned.1.call-done = f32[64,32,128]{2,1,0:T(8,128)} async-done(((f32[16,32,128]{2,1,0:T(8,128)}), f32[64,32,128]{2,1,0:T(8,128)}) %all-gather.2.cloned.1.call-update) | async-done | bytes 1048592 | tf_op jit(solution)/shard_map/all_gather | solution.py:115
  33.6 4.5 %all-to-all-start = ((f32[64,32,128]{2,1,0:T(8,128)}), f32[64,32,128]{2,1,0:T(8,128)S(1)}, u32[]{:S(2)}, u32[]{:S(2)}) async-start(f32[64,32,128]{2,1,0:T(8,128)} %reshape.845), calls=%async_computation | async-start | bytes 2097152 | tf_op jit(solution)/shard_map/all_to_all | solution.py:124
  46.0 4.5 %collective-permute-start.3 = (f32[2,20,2,128]{3,2,1,0:T(2,128)S(1)}, f32[2,20,2,128]{3,2,1,0:T(2,128)S(1)}, u32[]{:S(2)}, u32[]{:S(2)}) collective-permute-start(f32[2,20,2,128]{3,2,1,0:T(2,128)S(1)} %get-tuple-element.57), channel_id=1, source_target_pairs={{0,1},{2,3},{4,5},{6,7},{8,9},{10,11},{12,13},{14,15},{16,17},{18,... | collective-permute-start | bytes 122888 | tf_op jit(solution)/shard_map/ppermute | solution.py:23
  53.6 10.6 %all-to-all-done = f32[64,32,128]{2,1,0:T(8,128)S(1)} async-done(((f32[64,32,128]{2,1,0:T(8,128)}), f32[64,32,128]{2,1,0:T(8,128)S(1)}, u32[]{:S(2)}, u32[]{:S(2)}) %all-to-all-start) | async-done | bytes 1048608 | tf_op jit(solution)/shard_map/all_to_all | solution.py:124
  66.1 3.2 fusion.94
  70.7 4.5 %collective-permute-start.5 = (f32[2,2,32,128]{3,2,1,0:T(8,128)S(1)}, f32[2,2,32,128]{3,2,1,0:T(8,128)S(1)}, u32[]{:S(2)}, u32[]{:S(2)}) collective-permute-start(f32[2,2,32,128]{3,2,1,0:T(8,128)S(1)} %get-tuple-element.99), channel_id=1, source_target_pairs={{0,2},{2,4},{4,6},{1,3},{3,5},{5,7},{8,10},{10,12},{12,14},{9,11},... | collective-permute-start | bytes 196616 | tf_op jit(solution)/shard_map/ppermute | solution.py:23
  78.4 4.5 %collective-permute-start.7 = (f32[2,20,2,128]{3,2,1,0:T(2,128)S(1)}, f32[2,20,2,128]{3,2,1,0:T(2,128)S(1)}, u32[]{:S(2)}, u32[]{:S(2)}) collective-permute-start(f32[2,20,2,128]{3,2,1,0:T(2,128)S(1)} %get-tuple-element.53), channel_id=1, source_target_pairs={{0,1},{2,3},{4,5},{6,7},{8,9},{10,11},{12,13},{14,15},{16,17},{18,... | collective-permute-start | bytes 122888 | tf_op jit(solution)/shard_map/ppermute | solution.py:23
  83.9 16.6 %copy.515 = f32[2,16,32,128]{0,3,2,1:T(8,128)} copy(f32[2,16,32,128]{3,2,1,0:T(8,128)S(1)} %fusion.94) | data formatting | bytes 1048576 | tf_op jit(solution)/shard_map/div | solution.py:88
  100.6 3.0 gather_fusion
  107.1 4.9 %collective-permute-start.9 = (f32[2,2,32,128]{3,2,1,0:T(8,128)S(1)}, f32[2,2,32,128]{3,2,1,0:T(8,128)S(1)}, u32[]{:S(2)}, u32[]{:S(2)}) collective-permute-start(f32[2,2,32,128]{3,2,1,0:T(8,128)S(1)} %get-tuple-element.93), channel_id=1, source_target_pairs={{0,2},{2,4},{4,6},{1,3},{3,5},{5,7},{8,10},{10,12},{12,14},{9,11},... | collective-permute-start | bytes 196616 | tf_op jit(solution)/shard_map/ppermute | solution.py:23
  115.2 4.5 %collective-permute-start.11 = (f32[2,20,2,128]{3,2,1,0:T(2,128)S(1)}, f32[2,20,2,128]{3,2,1,0:T(2,128)S(1)}, u32[]{:S(2)}, u32[]{:S(2)}) collective-permute-start(f32[2,20,2,128]{3,2,1,0:T(2,128)S(1)} %get-tuple-element.49), channel_id=1, source_target_pairs={{0,1},{2,3},{4,5},{6,7},{8,9},{10,11},{12,13},{14,15},{16,17},{18,... | collective-permute-start | bytes 122888 | tf_op jit(solution)/shard_map/ppermute | solution.py:23
  120.7 16.6 %copy.516 = f32[2,16,32,128]{0,3,2,1:T(8,128)} copy(f32[2,16,32,128]{3,2,1,0:T(8,128)S(1)} %fusion.82) | data formatting | bytes 1048576 | tf_op jit(solution)/shard_map/div | solution.py:88
  143.8 4.9 %collective-permute-start.13 = (f32[2,2,32,128]{3,2,1,0:T(8,128)S(1)}, f32[2,2,32,128]{3,2,1,0:T(8,128)S(1)}, u32[]{:S(2)}, u32[]{:S(2)}) collective-permute-start(f32[2,2,32,128]{3,2,1,0:T(8,128)S(1)} %get-tuple-element.87), channel_id=1, source_target_pairs={{0,2},{2,4},{4,6},{1,3},{3,5},{5,7},{8,10},{10,12},{12,14},{9,11},... | collective-permute-start | bytes 196616 | tf_op jit(solution)/shard_map/ppermute | solution.py:23
  151.9 4.7 %collective-permute-start.15 = (f32[2,20,2,128]{3,2,1,0:T(2,128)S(1)}, f32[2,20,2,128]{3,2,1,0:T(2,128)S(1)}, u32[]{:S(2)}, u32[]{:S(2)}) collective-permute-start(f32[2,20,2,128]{3,2,1,0:T(2,128)S(1)} %get-tuple-element.45), channel_id=1, source_target_pairs={{0,1},{2,3},{4,5},{6,7},{8,9},{10,11},{12,13},{14,15},{16,17},{18,... | collective-permute-start | bytes 122888 | tf_op jit(solution)/shard_map/ppermute | solution.py:23
  157.6 16.6 %copy.517 = f32[2,16,32,128]{0,3,2,1:T(8,128)} copy(f32[2,16,32,128]{3,2,1,0:T(8,128)S(1)} %fusion.70) | data formatting | bytes 1048576 | tf_op jit(solution)/shard_map/div | solution.py:88
  174.2 3.0 gather_fusion.2
  180.7 4.9 %collective-permute-start.17 = (f32[2,2,32,128]{3,2,1,0:T(8,128)S(1)}, f32[2,2,32,128]{3,2,1,0:T(8,128)S(1)}, u32[]{:S(2)}, u32[]{:S(2)}) collective-permute-start(f32[2,2,32,128]{3,2,1,0:T(8,128)S(1)} %get-tuple-element.81), channel_id=1, source_target_pairs={{0,2},{2,4},{4,6},{1,3},{3,5},{5,7},{8,10},{10,12},{12,14},{9,11},... | collective-permute-start | bytes 196616 | tf_op jit(solution)/shard_map/ppermute | solution.py:23
  188.8 4.5 %collective-permute-start.19 = (f32[2,20,2,128]{3,2,1,0:T(2,128)S(1)}, f32[2,20,2,128]{3,2,1,0:T(2,128)S(1)}, u32[]{:S(2)}, u32[]{:S(2)}) collective-permute-start(f32[2,20,2,128]{3,2,1,0:T(2,128)S(1)} %get-tuple-element.41), channel_id=1, source_target_pairs={{0,1},{2,3},{4,5},{6,7},{8,9},{10,11},{12,13},{14,15},{16,17},{18,... | collective-permute-start | bytes 122888 | tf_op jit(solution)/shard_map/ppermute | solution.py:23
  194.3 16.6 %copy.518 = f32[2,16,32,128]{0,3,2,1:T(8,128)} copy(f32[2,16,32,128]{3,2,1,0:T(8,128)S(1)} %fusion.58) | data formatting | bytes 1048576 | tf_op jit(solution)/shard_map/div | solution.py:88
  217.4 4.9 %collective-permute-start.21 = (f32[2,2,32,128]{3,2,1,0:T(8,128)S(1)}, f32[2,2,32,128]{3,2,1,0:T(8,128)S(1)}, u32[]{:S(2)}, u32[]{:S(2)}) collective-permute-start(f32[2,2,32,128]{3,2,1,0:T(8,128)S(1)} %get-tuple-element.75), channel_id=1, source_target_pairs={{0,2},{2,4},{4,6},{1,3},{3,5},{5,7},{8,10},{10,12},{12,14},{9,11},... | collective-permute-start | bytes 196616 | tf_op jit(solution)/shard_map/ppermute | solution.py:23
  225.5 4.5 %collective-permute-start.23 = (f32[2,20,2,128]{3,2,1,0:T(2,128)S(1)}, f32[2,20,2,128]{3,2,1,0:T(2,128)S(1)}, u32[]{:S(2)}, u32[]{:S(2)}) collective-permute-start(f32[2,20,2,128]{3,2,1,0:T(2,128)S(1)} %get-tuple-element.37), channel_id=1, source_target_pairs={{0,1},{2,3},{4,5},{6,7},{8,9},{10,11},{12,13},{14,15},{16,17},{18,... | collective-permute-start | bytes 122888 | tf_op jit(solution)/shard_map/ppermute | solution.py:23
  231.0 16.6 %copy.519 = f32[2,16,32,128]{0,3,2,1:T(8,128)} copy(f32[2,16,32,128]{3,2,1,0:T(8,128)S(1)} %fusion.46) | data formatting | bytes 1048576 | tf_op jit(solution)/shard_map/div | solution.py:88
  254.2 4.9 %collective-permute-start.25 = (f32[2,2,32,128]{3,2,1,0:T(8,128)S(1)}, f32[2,2,32,128]{3,2,1,0:T(8,128)S(1)}, u32[]{:S(2)}, u32[]{:S(2)}) collective-permute-start(f32[2,2,32,128]{3,2,1,0:T(8,128)S(1)} %get-tuple-element.69), channel_id=1, source_target_pairs={{0,2},{2,4},{4,6},{1,3},{3,5},{5,7},{8,10},{10,12},{12,14},{9,11},... | collective-permute-start | bytes 196616 | tf_op jit(solution)/shard_map/ppermute | solution.py:23
  262.3 4.5 %collective-permute-start.27 = (f32[2,20,2,128]{3,2,1,0:T(2,128)S(1)}, f32[2,20,2,128]{3,2,1,0:T(2,128)S(1)}, u32[]{:S(2)}, u32[]{:S(2)}) collective-permute-start(f32[2,20,2,128]{3,2,1,0:T(2,128)S(1)} %get-tuple-element.33), channel_id=1, source_target_pairs={{0,1},{2,3},{4,5},{6,7},{8,9},{10,11},{12,13},{14,15},{16,17},{18,... | collective-permute-start | bytes 122888 | tf_op jit(solution)/shard_map/ppermute | solution.py:23
  267.8 16.6 %copy.520 = f32[2,16,32,128]{0,3,2,1:T(8,128)} copy(f32[2,16,32,128]{3,2,1,0:T(8,128)S(1)} %fusion.34) | data formatting | bytes 1048576 | tf_op jit(solution)/shard_map/div | solution.py:88
  290.9 4.9 %collective-permute-start.29 = (f32[2,2,32,128]{3,2,1,0:T(8,128)S(1)}, f32[2,2,32,128]{3,2,1,0:T(8,128)S(1)}, u32[]{:S(2)}, u32[]{:S(2)}) collective-permute-start(f32[2,2,32,128]{3,2,1,0:T(8,128)S(1)} %get-tuple-element.63), channel_id=1, source_target_pairs={{0,2},{2,4},{4,6},{1,3},{3,5},{5,7},{8,10},{10,12},{12,14},{9,11},... | collective-permute-start | bytes 196616 | tf_op jit(solution)/shard_map/ppermute | solution.py:23
  299.0 4.8 %collective-permute-start.31 = (f32[2,20,2,128]{3,2,1,0:T(2,128)S(1)}, f32[2,20,2,128]{3,2,1,0:T(2,128)S(1)}, u32[]{:S(2)}, u32[]{:S(2)}) collective-permute-start(f32[2,20,2,128]{3,2,1,0:T(2,128)S(1)} %get-tuple-element.29), channel_id=1, source_target_pairs={{0,1},{2,3},{4,5},{6,7},{8,9},{10,11},{12,13},{14,15},{16,17},{18,... | collective-permute-start | bytes 122888 | tf_op jit(solution)/shard_map/ppermute | solution.py:23
  304.7 16.6 %copy.521 = f32[2,16,32,128]{0,3,2,1:T(8,128)} copy(f32[2,16,32,128]{3,2,1,0:T(8,128)S(1)} %fusion.22) | data formatting | bytes 1048576 | tf_op jit(solution)/shard_map/div | solution.py:88
  321.4 3.0 gather_fusion.6
  326.6 16.7 %copy.522 = f32[2,16,32,128]{0,3,2,1:T(8,128)} copy(f32[2,16,32,128]{3,2,1,0:T(8,128)S(1)} %fusion.10) | data formatting | bytes 1048576 | tf_op jit(solution)/shard_map/div | solution.py:88
  347.8 37.5 %psum.7 = f32[1,2,256,8]{2,3,1,0:T(8,128)} all-reduce(f32[1,2,256,8]{2,3,1,0:T(8,128)S(1)} %bitcast.71), channel_id=1, replica_groups=mesh['shot'=4,'gx'=4,'gy'=2] {'gx','gy'}, use_global_device_ids=true, to_apply=%region_2.3 | all-reduce | flops 4096 | bytes 32768 | tf_op jit(solution)/shard_map/psum | solution.py:146
  (160 shorter events, 93.8 us)
Async XLA Ops:
  7.2 21.9 %all-gather.2.cloned.1.call-start = ((), (), s32[]{:S(2)}) async-start(), calls=%async_computation.1 | async-start | bytes 1310720 | tf_op jit(solution)/shard_map/all_gather | solution.py:115
  8.8 34.8 %collective-permute-start = (f32[2,2,32,128]{3,2,1,0:T(8,128)S(1)}, f32[2,2,32,128]{3,2,1,0:T(8,128)S(1)}, u32[]{:S(2)}, u32[]{:S(2)}) collective-permute-start(f32[2,2,32,128]{3,2,1,0:T(8,128)S(1)} %get-tuple-element.104), channel_id=1, source_target_pairs={{2,0},{4,2},{6,4},{3,1},{5,3},{7,5},{10,8},{12,10},{14,12},{11,9},... | collective-permute-start | bytes 196616 | tf_op jit(solution)/shard_map/ppermute | solution.py:25
  10.1 33.5 %collective-permute-start.1 = (f32[2,2,32,128]{3,2,1,0:T(8,128)S(1)}, f32[2,2,32,128]{3,2,1,0:T(8,128)S(1)}, u32[]{:S(2)}, u32[]{:S(2)}) collective-permute-start(f32[2,2,32,128]{3,2,1,0:T(8,128)S(1)} %get-tuple-element.105), channel_id=1, source_target_pairs={{0,2},{2,4},{4,6},{1,3},{3,5},{5,7},{8,10},{10,12},{12,14},{9,11},... | collective-permute-start | bytes 196616 | tf_op jit(solution)/shard_map/ppermute | solution.py:23
  33.6 30.7 %all-to-all-start = ((f32[64,32,128]{2,1,0:T(8,128)}), f32[64,32,128]{2,1,0:T(8,128)S(1)}, u32[]{:S(2)}, u32[]{:S(2)}) async-start(f32[64,32,128]{2,1,0:T(8,128)} %reshape.845), calls=%async_computation | async-start | bytes 2097152 | tf_op jit(solution)/shard_map/all_to_all | solution.py:124
  46.0 6.2 %collective-permute-start.3 = (f32[2,20,2,128]{3,2,1,0:T(2,128)S(1)}, f32[2,20,2,128]{3,2,1,0:T(2,128)S(1)}, u32[]{:S(2)}, u32[]{:S(2)}) collective-permute-start(f32[2,20,2,128]{3,2,1,0:T(2,128)S(1)} %get-tuple-element.57), channel_id=1, source_target_pairs={{0,1},{2,3},{4,5},{6,7},{8,9},{10,11},{12,13},{14,15},{16,17},{18,... | collective-permute-start | bytes 122888 | tf_op jit(solution)/shard_map/ppermute | solution.py:23
  70.7 6.4 %collective-permute-start.5 = (f32[2,2,32,128]{3,2,1,0:T(8,128)S(1)}, f32[2,2,32,128]{3,2,1,0:T(8,128)S(1)}, u32[]{:S(2)}, u32[]{:S(2)}) collective-permute-start(f32[2,2,32,128]{3,2,1,0:T(8,128)S(1)} %get-tuple-element.99), channel_id=1, source_target_pairs={{0,2},{2,4},{4,6},{1,3},{3,5},{5,7},{8,10},{10,12},{12,14},{9,11},... | collective-permute-start | bytes 196616 | tf_op jit(solution)/shard_map/ppermute | solution.py:23
  77.1 26.5 %collective-permute-start.6 = (f32[2,20,2,128]{3,2,1,0:T(2,128)S(1)}, f32[2,20,2,128]{3,2,1,0:T(2,128)S(1)}, u32[]{:S(2)}, u32[]{:S(2)}) collective-permute-start(f32[2,20,2,128]{3,2,1,0:T(2,128)S(1)} %get-tuple-element.52), channel_id=1, source_target_pairs={{1,0},{3,2},{5,4},{7,6},{9,8},{11,10},{13,12},{15,14},{17,16},{19,... | collective-permute-start | bytes 122888 | tf_op jit(solution)/shard_map/ppermute | solution.py:25
  78.4 25.2 %collective-permute-start.7 = (f32[2,20,2,128]{3,2,1,0:T(2,128)S(1)}, f32[2,20,2,128]{3,2,1,0:T(2,128)S(1)}, u32[]{:S(2)}, u32[]{:S(2)}) collective-permute-start(f32[2,20,2,128]{3,2,1,0:T(2,128)S(1)} %get-tuple-element.53), channel_id=1, source_target_pairs={{0,1},{2,3},{4,5},{6,7},{8,9},{10,11},{12,13},{14,15},{16,17},{18,... | collective-permute-start | bytes 122888 | tf_op jit(solution)/shard_map/ppermute | solution.py:23
  105.8 6.5 %collective-permute-start.8 = (f32[2,2,32,128]{3,2,1,0:T(8,128)S(1)}, f32[2,2,32,128]{3,2,1,0:T(8,128)S(1)}, u32[]{:S(2)}, u32[]{:S(2)}) collective-permute-start(f32[2,2,32,128]{3,2,1,0:T(8,128)S(1)} %get-tuple-element.92), channel_id=1, source_target_pairs={{2,0},{4,2},{6,4},{3,1},{5,3},{7,5},{10,8},{12,10},{14,12},{11,9},... | collective-permute-start | bytes 196616 | tf_op jit(solution)/shard_map/ppermute | solution.py:25
  107.1 6.8 %collective-permute-start.9 = (f32[2,2,32,128]{3,2,1,0:T(8,128)S(1)}, f32[2,2,32,128]{3,2,1,0:T(8,128)S(1)}, u32[]{:S(2)}, u32[]{:S(2)}) collective-permute-start(f32[2,2,32,128]{3,2,1,0:T(8,128)S(1)} %get-tuple-element.93), channel_id=1, source_target_pairs={{0,2},{2,4},{4,6},{1,3},{3,5},{5,7},{8,10},{10,12},{12,14},{9,11},... | collective-permute-start | bytes 196616 | tf_op jit(solution)/shard_map/ppermute | solution.py:23
  113.9 26.5 %collective-permute-start.10 = (f32[2,20,2,128]{3,2,1,0:T(2,128)S(1)}, f32[2,20,2,128]{3,2,1,0:T(2,128)S(1)}, u32[]{:S(2)}, u32[]{:S(2)}) collective-permute-start(f32[2,20,2,128]{3,2,1,0:T(2,128)S(1)} %get-tuple-element.48), channel_id=1, source_target_pairs={{1,0},{3,2},{5,4},{7,6},{9,8},{11,10},{13,12},{15,14},{17,16},{19,... | collective-permute-start | bytes 122888 | tf_op jit(solution)/shard_map/ppermute | solution.py:25
  115.2 25.2 %collective-permute-start.11 = (f32[2,20,2,128]{3,2,1,0:T(2,128)S(1)}, f32[2,20,2,128]{3,2,1,0:T(2,128)S(1)}, u32[]{:S(2)}, u32[]{:S(2)}) collective-permute-start(f32[2,20,2,128]{3,2,1,0:T(2,128)S(1)} %get-tuple-element.49), channel_id=1, source_target_pairs={{0,1},{2,3},{4,5},{6,7},{8,9},{10,11},{12,13},{14,15},{16,17},{18,... | collective-permute-start | bytes 122888 | tf_op jit(solution)/shard_map/ppermute | solution.py:23
  142.5 6.5 %collective-permute-start.12 = (f32[2,2,32,128]{3,2,1,0:T(8,128)S(1)}, f32[2,2,32,128]{3,2,1,0:T(8,128)S(1)}, u32[]{:S(2)}, u32[]{:S(2)}) collective-permute-start(f32[2,2,32,128]{3,2,1,0:T(8,128)S(1)} %get-tuple-element.86), channel_id=1, source_target_pairs={{2,0},{4,2},{6,4},{3,1},{5,3},{7,5},{10,8},{12,10},{14,12},{11,9},... | collective-permute-start | bytes 196616 | tf_op jit(solution)/shard_map/ppermute | solution.py:25
  143.8 6.8 %collective-permute-start.13 = (f32[2,2,32,128]{3,2,1,0:T(8,128)S(1)}, f32[2,2,32,128]{3,2,1,0:T(8,128)S(1)}, u32[]{:S(2)}, u32[]{:S(2)}) collective-permute-start(f32[2,2,32,128]{3,2,1,0:T(8,128)S(1)} %get-tuple-element.87), channel_id=1, source_target_pairs={{0,2},{2,4},{4,6},{1,3},{3,5},{5,7},{8,10},{10,12},{12,14},{9,11},... | collective-permute-start | bytes 196616 | tf_op jit(solution)/shard_map/ppermute | solution.py:23
  150.6 26.7 %collective-permute-start.14 = (f32[2,20,2,128]{3,2,1,0:T(2,128)S(1)}, f32[2,20,2,128]{3,2,1,0:T(2,128)S(1)}, u32[]{:S(2)}, u32[]{:S(2)}) collective-permute-start(f32[2,20,2,128]{3,2,1,0:T(2,128)S(1)} %get-tuple-element.44), channel_id=1, source_target_pairs={{1,0},{3,2},{5,4},{7,6},{9,8},{11,10},{13,12},{15,14},{17,16},{19,... | collective-permute-start | bytes 122888 | tf_op jit(solution)/shard_map/ppermute | solution.py:25
  151.9 25.4 %collective-permute-start.15 = (f32[2,20,2,128]{3,2,1,0:T(2,128)S(1)}, f32[2,20,2,128]{3,2,1,0:T(2,128)S(1)}, u32[]{:S(2)}, u32[]{:S(2)}) collective-permute-start(f32[2,20,2,128]{3,2,1,0:T(2,128)S(1)} %get-tuple-element.45), channel_id=1, source_target_pairs={{0,1},{2,3},{4,5},{6,7},{8,9},{10,11},{12,13},{14,15},{16,17},{18,... | collective-permute-start | bytes 122888 | tf_op jit(solution)/shard_map/ppermute | solution.py:23
  179.4 6.5 %collective-permute-start.16 = (f32[2,2,32,128]{3,2,1,0:T(8,128)S(1)}, f32[2,2,32,128]{3,2,1,0:T(8,128)S(1)}, u32[]{:S(2)}, u32[]{:S(2)}) collective-permute-start(f32[2,2,32,128]{3,2,1,0:T(8,128)S(1)} %get-tuple-element.80), channel_id=1, source_target_pairs={{2,0},{4,2},{6,4},{3,1},{5,3},{7,5},{10,8},{12,10},{14,12},{11,9},... | collective-permute-start | bytes 196616 | tf_op jit(solution)/shard_map/ppermute | solution.py:25
  180.7 6.8 %collective-permute-start.17 = (f32[2,2,32,128]{3,2,1,0:T(8,128)S(1)}, f32[2,2,32,128]{3,2,1,0:T(8,128)S(1)}, u32[]{:S(2)}, u32[]{:S(2)}) collective-permute-start(f32[2,2,32,128]{3,2,1,0:T(8,128)S(1)} %get-tuple-element.81), channel_id=1, source_target_pairs={{0,2},{2,4},{4,6},{1,3},{3,5},{5,7},{8,10},{10,12},{12,14},{9,11},... | collective-permute-start | bytes 196616 | tf_op jit(solution)/shard_map/ppermute | solution.py:23
  187.5 26.5 %collective-permute-start.18 = (f32[2,20,2,128]{3,2,1,0:T(2,128)S(1)}, f32[2,20,2,128]{3,2,1,0:T(2,128)S(1)}, u32[]{:S(2)}, u32[]{:S(2)}) collective-permute-start(f32[2,20,2,128]{3,2,1,0:T(2,128)S(1)} %get-tuple-element.40), channel_id=1, source_target_pairs={{1,0},{3,2},{5,4},{7,6},{9,8},{11,10},{13,12},{15,14},{17,16},{19,... | collective-permute-start | bytes 122888 | tf_op jit(solution)/shard_map/ppermute | solution.py:25
  188.8 25.2 %collective-permute-start.19 = (f32[2,20,2,128]{3,2,1,0:T(2,128)S(1)}, f32[2,20,2,128]{3,2,1,0:T(2,128)S(1)}, u32[]{:S(2)}, u32[]{:S(2)}) collective-permute-start(f32[2,20,2,128]{3,2,1,0:T(2,128)S(1)} %get-tuple-element.41), channel_id=1, source_target_pairs={{0,1},{2,3},{4,5},{6,7},{8,9},{10,11},{12,13},{14,15},{16,17},{18,... | collective-permute-start | bytes 122888 | tf_op jit(solution)/shard_map/ppermute | solution.py:23
  216.1 6.5 %collective-permute-start.20 = (f32[2,2,32,128]{3,2,1,0:T(8,128)S(1)}, f32[2,2,32,128]{3,2,1,0:T(8,128)S(1)}, u32[]{:S(2)}, u32[]{:S(2)}) collective-permute-start(f32[2,2,32,128]{3,2,1,0:T(8,128)S(1)} %get-tuple-element.74), channel_id=1, source_target_pairs={{2,0},{4,2},{6,4},{3,1},{5,3},{7,5},{10,8},{12,10},{14,12},{11,9},... | collective-permute-start | bytes 196616 | tf_op jit(solution)/shard_map/ppermute | solution.py:25
  217.4 6.8 %collective-permute-start.21 = (f32[2,2,32,128]{3,2,1,0:T(8,128)S(1)}, f32[2,2,32,128]{3,2,1,0:T(8,128)S(1)}, u32[]{:S(2)}, u32[]{:S(2)}) collective-permute-start(f32[2,2,32,128]{3,2,1,0:T(8,128)S(1)} %get-tuple-element.75), channel_id=1, source_target_pairs={{0,2},{2,4},{4,6},{1,3},{3,5},{5,7},{8,10},{10,12},{12,14},{9,11},... | collective-permute-start | bytes 196616 | tf_op jit(solution)/shard_map/ppermute | solution.py:23
  224.2 26.5 %collective-permute-start.22 = (f32[2,20,2,128]{3,2,1,0:T(2,128)S(1)}, f32[2,20,2,128]{3,2,1,0:T(2,128)S(1)}, u32[]{:S(2)}, u32[]{:S(2)}) collective-permute-start(f32[2,20,2,128]{3,2,1,0:T(2,128)S(1)} %get-tuple-element.36), channel_id=1, source_target_pairs={{1,0},{3,2},{5,4},{7,6},{9,8},{11,10},{13,12},{15,14},{17,16},{19,... | collective-permute-start | bytes 122888 | tf_op jit(solution)/shard_map/ppermute | solution.py:25
  225.5 25.2 %collective-permute-start.23 = (f32[2,20,2,128]{3,2,1,0:T(2,128)S(1)}, f32[2,20,2,128]{3,2,1,0:T(2,128)S(1)}, u32[]{:S(2)}, u32[]{:S(2)}) collective-permute-start(f32[2,20,2,128]{3,2,1,0:T(2,128)S(1)} %get-tuple-element.37), channel_id=1, source_target_pairs={{0,1},{2,3},{4,5},{6,7},{8,9},{10,11},{12,13},{14,15},{16,17},{18,... | collective-permute-start | bytes 122888 | tf_op jit(solution)/shard_map/ppermute | solution.py:23
  252.9 6.5 %collective-permute-start.24 = (f32[2,2,32,128]{3,2,1,0:T(8,128)S(1)}, f32[2,2,32,128]{3,2,1,0:T(8,128)S(1)}, u32[]{:S(2)}, u32[]{:S(2)}) collective-permute-start(f32[2,2,32,128]{3,2,1,0:T(8,128)S(1)} %get-tuple-element.68), channel_id=1, source_target_pairs={{2,0},{4,2},{6,4},{3,1},{5,3},{7,5},{10,8},{12,10},{14,12},{11,9},... | collective-permute-start | bytes 196616 | tf_op jit(solution)/shard_map/ppermute | solution.py:25
  254.2 6.8 %collective-permute-start.25 = (f32[2,2,32,128]{3,2,1,0:T(8,128)S(1)}, f32[2,2,32,128]{3,2,1,0:T(8,128)S(1)}, u32[]{:S(2)}, u32[]{:S(2)}) collective-permute-start(f32[2,2,32,128]{3,2,1,0:T(8,128)S(1)} %get-tuple-element.69), channel_id=1, source_target_pairs={{0,2},{2,4},{4,6},{1,3},{3,5},{5,7},{8,10},{10,12},{12,14},{9,11},... | collective-permute-start | bytes 196616 | tf_op jit(solution)/shard_map/ppermute | solution.py:23
  261.0 26.5 %collective-permute-start.26 = (f32[2,20,2,128]{3,2,1,0:T(2,128)S(1)}, f32[2,20,2,128]{3,2,1,0:T(2,128)S(1)}, u32[]{:S(2)}, u32[]{:S(2)}) collective-permute-start(f32[2,20,2,128]{3,2,1,0:T(2,128)S(1)} %get-tuple-element.32), channel_id=1, source_target_pairs={{1,0},{3,2},{5,4},{7,6},{9,8},{11,10},{13,12},{15,14},{17,16},{19,... | collective-permute-start | bytes 122888 | tf_op jit(solution)/shard_map/ppermute | solution.py:25
  262.3 25.2 %collective-permute-start.27 = (f32[2,20,2,128]{3,2,1,0:T(2,128)S(1)}, f32[2,20,2,128]{3,2,1,0:T(2,128)S(1)}, u32[]{:S(2)}, u32[]{:S(2)}) collective-permute-start(f32[2,20,2,128]{3,2,1,0:T(2,128)S(1)} %get-tuple-element.33), channel_id=1, source_target_pairs={{0,1},{2,3},{4,5},{6,7},{8,9},{10,11},{12,13},{14,15},{16,17},{18,... | collective-permute-start | bytes 122888 | tf_op jit(solution)/shard_map/ppermute | solution.py:23
  289.6 6.5 %collective-permute-start.28 = (f32[2,2,32,128]{3,2,1,0:T(8,128)S(1)}, f32[2,2,32,128]{3,2,1,0:T(8,128)S(1)}, u32[]{:S(2)}, u32[]{:S(2)}) collective-permute-start(f32[2,2,32,128]{3,2,1,0:T(8,128)S(1)} %get-tuple-element.62), channel_id=1, source_target_pairs={{2,0},{4,2},{6,4},{3,1},{5,3},{7,5},{10,8},{12,10},{14,12},{11,9},... | collective-permute-start | bytes 196616 | tf_op jit(solution)/shard_map/ppermute | solution.py:25
  290.9 6.8 %collective-permute-start.29 = (f32[2,2,32,128]{3,2,1,0:T(8,128)S(1)}, f32[2,2,32,128]{3,2,1,0:T(8,128)S(1)}, u32[]{:S(2)}, u32[]{:S(2)}) collective-permute-start(f32[2,2,32,128]{3,2,1,0:T(8,128)S(1)} %get-tuple-element.63), channel_id=1, source_target_pairs={{0,2},{2,4},{4,6},{1,3},{3,5},{5,7},{8,10},{10,12},{12,14},{9,11},... | collective-permute-start | bytes 196616 | tf_op jit(solution)/shard_map/ppermute | solution.py:23
  297.7 26.7 %collective-permute-start.30 = (f32[2,20,2,128]{3,2,1,0:T(2,128)S(1)}, f32[2,20,2,128]{3,2,1,0:T(2,128)S(1)}, u32[]{:S(2)}, u32[]{:S(2)}) collective-permute-start(f32[2,20,2,128]{3,2,1,0:T(2,128)S(1)} %get-tuple-element.28), channel_id=1, source_target_pairs={{1,0},{3,2},{5,4},{7,6},{9,8},{11,10},{13,12},{15,14},{17,16},{19,... | collective-permute-start | bytes 122888 | tf_op jit(solution)/shard_map/ppermute | solution.py:25
  299.0 25.4 %collective-permute-start.31 = (f32[2,20,2,128]{3,2,1,0:T(2,128)S(1)}, f32[2,20,2,128]{3,2,1,0:T(2,128)S(1)}, u32[]{:S(2)}, u32[]{:S(2)}) collective-permute-start(f32[2,20,2,128]{3,2,1,0:T(2,128)S(1)} %get-tuple-element.29), channel_id=1, source_target_pairs={{0,1},{2,3},{4,5},{6,7},{8,9},{10,11},{12,13},{14,15},{16,17},{18,... | collective-permute-start | bytes 122888 | tf_op jit(solution)/shard_map/ppermute | solution.py:23
  (15 other events, 441.1 us)
Sparse Core Ops, SparseCore 0:
  9.6 19.4 all-gather.1
where the time goes:
time: 394 us; the launch traced here: 392 us
  local copies, waits for them, and re-layouts  178 us (45%)
  starting transfers between devices  101 us (26%)
  blocking collectives  37.5 us (10%)
  waiting for transfers between devices  33.4 us (8%)
  other arithmetic  25.8 us (7%)
  between operations  15.4 us (4%)
    div x8, local copies, waits for them, and re-layouts, advance(): (2.0 * middle - (1.0 - damp) * previous + coef * laplace(extended) + inje...  133 us
    ppermute x16, starting transfers between devices, extended_2(): lax.ppermute(tail, axis, [(i, (i + 1) % count) for i in range(ends)])  76.2 us
    psum x1, blocking collectives, local(): traces = lax.psum(jnp.stack(recorded, axis=-1), ('gx', 'gy'))  37.5 us
    gather x8, local copies, waits for them, and re-layouts, sample(): field[:, jnp.clip(local_x, 0, size_x - 1), jnp.clip(local_y, 0, size_y -...  23.6 us
    ppermute x16, starting transfers between devices, extended_2(): lax.ppermute(head, axis, [((i + 1) % count, i) for i in range(ends)])  20.7 us
    div x8, other arithmetic, advance(): (2.0 * middle - (1.0 - damp) * previous + coef * laplace(extended) + inje...  17.1 us
    slice x16, local copies, waits for them, and re-layouts, depth_ahead(): return jnp.concatenate([field[..., reach:], filler], axis=-1)  12.7 us
    ppermute x16, waiting for transfers between devices, extended_2(): lax.ppermute(tail, axis, [(i, (i + 1) % count) for i in range(ends)])  12.7 us
  transfers between devices with their start and end apart: 34, of which 17 were waited for; matrix products, arithmetic and copies ran while one was open for 42% of the time, Pallas kernels for 0%

commit v1 on v0

v1 whole, which is shorter than its diff:
```python
import functools

import jax
import jax.numpy as jnp
from jax import lax
from jax.experimental import pallas as pl
from jax.experimental.pallas import tpu as pltpu
from jax.sharding import Mesh
from jax.sharding import PartitionSpec as P

STEPS = 8
HALO = 2 * STEPS
PAD = 8

near_weight = 4.0 / 3.0
centre_ratio = 7.5 * 3.0 / 4.0
far_ratio = 1.0 / 16.0
damp_peak = 0.3

SMEM = pl.BlockSpec(memory_space=pltpu.SMEM)
ANY = pl.BlockSpec(memory_space=pl.ANY)
VMEM = pl.BlockSpec(memory_space=pltpu.VMEM)


def pairs(count, parity):
    return [
        pair
        for i in range(parity, count - 1, 2)
        for pair in ((i, i + 1), (i + 1, i))
    ]


def joint(first, second, count):
    return [(a * count + b, c * count + d) for a, c in first for b, d in second]


def pick_kernel(columns, where, stored, other, out, sems):
    targets = out.shape[0]
    across = where[1]
    core = where[0]
    copies = []
    for t in range(targets):
        block = columns[t]
        owner_core = (block // across) % 2
        row = (block // (2 * across)) * across + block % across
        here = pltpu.make_async_copy(stored.at[row], out.at[t], sems.at[t])
        there = pltpu.make_async_copy(other.at[row], out.at[t], sems.at[t])
        pl.when(owner_core == core)(here.start)
        pl.when(owner_core != core)(there.start)
        copies.append(here)
    for copy in copies:
        copy.wait()


def pick(columns, where, stored, other):
    targets = stored.shape[0]
    return pl.pallas_call(
        pick_kernel,
        out_shape=jax.ShapeDtypeStruct(stored.shape, stored.dtype),
        in_specs=[SMEM, SMEM, ANY, ANY],
        out_specs=ANY,
        scratch_shapes=[pltpu.SemaphoreType.DMA((targets,))],
        name="pick_slices",
    )(columns, where, stored, other)


def list_kernel(block_x, block_y, starts, receivers, out):
    total = receivers.shape[0] // 3

    def body(r, count):
        x = receivers[3 * r] - starts[0]
        y = receivers[3 * r + 1] - starts[1]
        inside = (x >= 0) & (x < block_x) & (y >= 0) & (y < block_y)
        out[1 + 2 * count] = r
        out[2 + 2 * count] = x * block_y + y
        return count + inside.astype(jnp.int32)

    out[0] = lax.fori_loop(0, total, body, jnp.int32(0))


def list_receivers(block_x, block_y, starts, receivers):
    total = receivers.shape[0]
    return pl.pallas_call(
        functools.partial(list_kernel, block_x, block_y),
        out_shape=jax.ShapeDtypeStruct((2 * total + 8,), jnp.int32),
        in_specs=[SMEM, SMEM],
        out_specs=SMEM,
        name="list_receivers",
    )(starts, receivers.reshape(-1))


def window_kernel(
    sizes,
    starts,
    sources,
    amplitudes,
    local_list,
    lanes,
    now,
    prev,
    now_x,
    prev_x,
    sides,
    corners,
    speed,
    speed_x,
    speed_y,
    speed_xy,
    out_now,
    out_prev,
    partial,
    now_ext,
    prev_ext,
    near,
    twice,
    samples,
    sems,
    out_sems,
):
    block_x, block_y, total_x, total_y, ny = sizes
    rows = now_ext.shape[2]
    planes = now_ext.shape[1]
    shots = now_ext.shape[0]
    column, row = starts[0], starts[1]
    odd_x, odd_y = column % 2, row % 2
    own = pl.multiple_of(PAD + (HALO * odd_y if ny == 2 else HALO), 8)
    high_x = [odd_x == 0, odd_x == 1]
    high_y = [odd_y == 0, odd_y == 1]
    x_at = [jnp.where(h, HALO + block_x, 0) for h in high_x]
    y_at = [
        pl.multiple_of(jnp.where(h, own + block_y, own - HALO), 8) for h in high_y
    ]
    near_x = [jnp.where(h, 0, HALO // 2) for h in high_x]
    near_y = [
        pl.multiple_of(jnp.where(h, own + block_y, own - HALO // 2), 8) for h in high_y
    ]
    far_y = [
        pl.multiple_of(jnp.where(h, own + block_y + HALO // 2, own - HALO), 8)
        for h in high_y
    ]
    half = HALO // 2
    copies = []

    def fetch(src, dst):
        copy = pltpu.make_async_copy(src, dst, sems.at[len(copies)])
        copy.start()
        copies.append(copy)

    y_count = speed_y.shape[0]
    own_rows = pl.ds(own, block_y)
    fetch(now, now_ext.at[:, pl.ds(HALO, block_x), own_rows])
    fetch(prev, prev_ext.at[:, pl.ds(HALO, block_x), own_rows])
    for e in range(2):
        at = pl.ds(x_at[e], block_x)
        fetch(now_x[e], now_ext.at[:, at, own_rows])
        fetch(prev_x[e], prev_ext.at[:, at, own_rows])
    for f in range(y_count):
        at = pl.ds(y_at[f], HALO)
        fetch(sides.at[f, 0], now_ext.at[:, pl.ds(HALO, block_x), at])
        fetch(sides.at[f, 1], prev_ext.at[:, pl.ds(HALO, block_x), at])
        for e in range(2):
            at_near = pl.ds(x_at[e] + near_x[e], half)
            at_far = pl.ds(x_at[e] + half - near_x[e], half)
            for k, ext in enumerate((now_ext, prev_ext)):
                fetch(
                    corners.at[f, e, k, :, :, pl.ds(0, HALO)],
                    ext.at[:, at_near, at],
                )
                fetch(
                    corners.at[f, e, k, :, :, pl.ds(HALO, half)],
                    ext.at[:, at_far, pl.ds(near_y[f], half)],
                )
    field_copies = len(copies)
    fetch(speed, near.at[pl.ds(HALO, block_x), own_rows])
    for e in range(2):
        fetch(speed_x[e], near.at[pl.ds(x_at[e], block_x), own_rows])
    for f in range(y_count):
        at = pl.ds(y_at[f], HALO)
        fetch(speed_y.at[f], near.at[pl.ds(HALO, block_x), at])
        for e in range(2):
            fetch(speed_xy.at[f, e], near.at[pl.ds(x_at[e], block_x), at])

    blank = jnp.zeros((PAD, now_ext.shape[3]), jnp.float32)
    for ext in (now_ext, prev_ext):
        for s in range(shots):

            def clear(x, _):
                ext[s, x, pl.ds(0, PAD)] = blank
                ext[s, x, pl.ds(rows - PAD, PAD)] = blank
                return 0

            lax.fori_loop(0, planes, clear, 0)
            for f in range(y_count):
                for e in range(2):

                    def clear_far(x, _):
                        ext[s, x_at[e] + half - near_x[e] + x, pl.ds(far_y[f], half)] = blank
                        return 0

                    lax.fori_loop(0, half, clear_far, 0)

    def depth_in(cell, total):
        inside = (cell >= 0) & (cell < total)
        depth = jnp.maximum(
            block_x - jnp.minimum(cell + 1, total - cell), 0
        ).astype(jnp.float32) / block_x
        return inside, depth

    x_first = column * block_x - HALO
    y_first = row * block_y - own
    shape = (rows, now_ext.shape[3])
    y_in, y_depth = depth_in(lax.broadcasted_iota(jnp.int32, shape, 0) + y_first, total_y)
    y_part = y_depth * y_depth

    for copy in copies:
        copy.wait()

    def prepare(x, _):
        x_in, x_depth = depth_in(jnp.full(shape, x + x_first, jnp.int32), total_x)
        inverse = 1.0 / (1.0 + damp_peak * (x_depth * x_depth + y_part))
        inverse = jnp.where(x_in & y_in, inverse, 0.0)
        v = near[x]
        near[x] = jnp.where(x_in & y_in, inverse * (v * v) * near_weight, 0.0)
        twice[x] = 2.0 * inverse
        return 0

    lax.fori_loop(2, planes - 2, prepare, 0)

    depth = now_ext.shape[3]
    lane = lax.broadcasted_iota(jnp.int32, (8, depth), 1)
    ahead_1, ahead_2 = lane < depth - 1, lane < depth - 2
    behind_1, behind_2 = lane >= 1, lane >= 2
    lane_row = lax.broadcasted_iota(jnp.int32, (1, depth), 1)

    cur, old = now_ext, prev_ext
    for step in range(1, STEPS + 1):
        reach = 2 * (STEPS - step)
        side = -(-reach // 8)
        if ny == 2:
            first = pl.multiple_of(own - 8 * side * odd_y, 8)
            tiles = block_y // 8 + side
        else:
            first = pl.multiple_of(own - 8 * side, 8)
            tiles = block_y // 8 + 2 * side

        def plane(x, _, cur=cur, old=old, first=first, tiles=tiles):
            for j in range(tiles):
                base = first + 8 * j
                at = pl.ds(pl.multiple_of(base, 8), 8)
                n, a = near[x, at], twice[x, at]
                for s in range(shots):
                    c = cur[s, x, at]
                    close = cur[s, x - 1, at] + cur[s, x + 1, at]
                    wide = cur[s, x - 2, at] + cur[s, x + 2, at]
                    close += cur[s, x, pl.ds(base - 1, 8)] + cur[s, x, pl.ds(base + 1, 8)]
                    wide += cur[s, x, pl.ds(base - 2, 8)] + cur[s, x, pl.ds(base + 2, 8)]
                    close += jnp.where(ahead_1, pltpu.roll(c, depth - 1, 1), 0.0)
                    close += jnp.where(behind_1, pltpu.roll(c, 1, 1), 0.0)
                    wide += jnp.where(ahead_2, pltpu.roll(c, depth - 2, 1), 0.0)
                    wide += jnp.where(behind_2, pltpu.roll(c, 2, 1), 0.0)
                    p = old[s, x, at]
                    lap = close - far_ratio * wide - centre_ratio * c
                    old[s, x, at] = p + a * (c - p) + n * lap
            return 0

        lax.fori_loop(2 * step, planes - 2 * step, plane, 0)

        for s in range(shots):
            sx = sources[3 * s] - x_first
            sy = sources[3 * s + 1] - y_first
            sz = sources[3 * s + 2]
            amplitude = amplitudes[s * STEPS + step - 1]
            inside = (
                (sx >= 2 * step)
                & (sx < planes - 2 * step)
                & (sy >= first)
                & (sy < first + 8 * tiles)
            )

            @pl.when(inside)
            def _(old=old, s=s, sx=sx, sy=sy, sz=sz, amplitude=amplitude):
                at = pl.ds(sy, 1)
                old[s, sx, at] += jnp.where(lane_row == sz, amplitude, 0.0)

        cur, old = old, cur

        def take(k, _, cur=cur, step=step):
            r = local_list[1 + 2 * k]
            cell = local_list[2 + 2 * k]
            x = HALO + cell // block_y
            y = own + cell % block_y
            for s in range(shots):
                samples[s * STEPS + step - 1, pl.ds(r, 1)] = cur[s, x, pl.ds(y, 1)]
            return 0

        lax.fori_loop(0, local_list[0], take, 0)
        if step >= STEPS - 1:
            out = out_prev if step == STEPS - 1 else out_now
            copy = pltpu.make_async_copy(
                cur.at[:, pl.ds(HALO, block_x), own_rows],
                out,
                out_sems.at[step - STEPS + 1],
            )
            copy.start()
            if step == STEPS - 1:
                first_out = copy
            else:
                last_out = copy

    total = lanes.shape[0]
    mask = lanes[...] == lax.broadcasted_iota(jnp.int32, (total, depth), 1)
    for k in range(shots * STEPS):
        taken = jnp.where(mask, samples[k], 0.0)
        values = jnp.sum(taken, axis=1)
        for copy_to in range(partial.shape[0]):
            partial[copy_to, k] = values
    first_out.wait()
    last_out.wait()


def window(sizes, starts, sources, amplitudes, local_list, lanes, now, prev, now_x, prev_x, sides, corners, speed, speed_x, speed_y, speed_xy, copies):
    block_x, block_y, total_x, total_y, ny = sizes
    shots, _, _, depth = now.shape
    planes = block_x + 2 * HALO
    rows = block_y + (HALO if ny == 2 else 2 * HALO) + 2 * PAD
    recs = lanes.shape[0]

    def kernel(starts, sources, amplitudes, local_list, lanes, now, prev, n0, n1, p0, p1, sides, corners, speed, v0, v1, *rest):
        window_kernel(
            sizes, starts, sources, amplitudes, local_list, lanes, now, prev,
            (n0, n1), (p0, p1), sides, corners, speed, (v0, v1), *rest,
        )

    return pl.pallas_call(
        kernel,
        out_shape=(
            jax.ShapeDtypeStruct(now.shape, now.dtype),
            jax.ShapeDtypeStruct(now.shape, now.dtype),
            jax.ShapeDtypeStruct((copies, shots * STEPS, recs), now.dtype),
        ),
        in_specs=[SMEM, SMEM, SMEM, SMEM, VMEM] + [ANY] * 13,
        out_specs=(ANY, ANY, VMEM),
        scratch_shapes=[
            pltpu.VMEM((shots, planes, rows, depth), jnp.float32),
            pltpu.VMEM((shots, planes, rows, depth), jnp.float32),
            pltpu.VMEM((planes, rows, depth), jnp.float32),
            pltpu.VMEM((planes, rows, depth), jnp.float32),
            pltpu.VMEM((shots * STEPS, recs, depth), jnp.float32),
            pltpu.SemaphoreType.DMA((48,)),
            pltpu.SemaphoreType.DMA((2,)),
        ],
        compiler_params=pltpu.CompilerParams(vmem_limit_bytes=40 * 2**20),
        name="wave_window",
    )(
        starts, sources, amplitudes, local_list, lanes, now, prev, *now_x, *prev_x,
        sides, corners, speed, *speed_x, speed_y, speed_xy,
    )


def local(model_tiles, owner_map, offsets, field_now, field_prev, sources, wavelet, receivers):
    block_x, block_y, depth = model_tiles.shape
    nx, ny, groups = lax.axis_size("gx"), lax.axis_size("gy"), lax.axis_size("sy")
    column, row, core = lax.axis_index("gx"), lax.axis_index("gy"), lax.axis_index("core")
    shot_row = lax.axis_index("sy")
    total_x, total_y = block_x * nx, block_y * ny
    now, prev = field_now[0], field_prev[0]
    x_perms = [pairs(nx, 0), pairs(nx, 1)]
    y_perms = [pairs(ny, f) for f in range(2 if ny > 2 else 1)]
    odd_x, odd_y = column % 2, row % 2
    low_rows, high_rows = 0, block_y - HALO
    half = HALO // 2

    spread = lax.all_to_all(model_tiles, ("sy", "gx"), 0, 0, tiled=True)
    other = lax.ppermute(spread, "core", [(0, 1), (1, 0)])

    now_x = [lax.ppermute(now, "gx", perm) for perm in x_perms]
    prev_x = [lax.ppermute(prev, "gx", perm) for perm in x_perms]

    def sent_rows(f):
        return jnp.where(odd_y == f, high_rows, low_rows)

    def near_planes(e):
        return jnp.where(odd_x == e, 0, half)

    sides, corners = [], []
    for f, perm in enumerate(y_perms):
        start = sent_rows(f)
        cut = jnp.stack(
            [lax.dynamic_slice_in_dim(v, start, HALO, axis=2) for v in (now, prev)]
        )
        sides.append(lax.ppermute(cut, "gy", perm))
        near_start = jnp.where(odd_y == f, block_y - half, 0)
        cut = []
        for e in range(2):
            for v in (now_x[e], prev_x[e]):
                close = lax.dynamic_slice_in_dim(v, near_planes(e), half, axis=1)
                close = lax.dynamic_slice_in_dim(close, start, HALO, axis=2)
                wide = lax.dynamic_slice_in_dim(v, half - near_planes(e), half, axis=1)
                wide = lax.dynamic_slice_in_dim(wide, near_start, half, axis=2)
                cut.append(jnp.concatenate([close, wide], axis=2))
        cut = jnp.stack(cut).reshape((2, 2) + cut[0].shape)
        corners.append(lax.ppermute(cut, "gy", perm))
    sides, corners = jnp.stack(sides), jnp.stack(corners)

    shifts = jnp.zeros((groups,), jnp.int32)
    for turn in range(groups):
        came = offsets if turn == 0 else lax.ppermute(
            offsets, "sy", [(i, (i + turn) % groups) for i in range(groups)]
        )
        at = (shot_row - turn) % groups
        shifts = jnp.where(jnp.arange(groups) == at, came, shifts)
    columns = (shifts[:, None] + jnp.arange(nx, dtype=jnp.int32)[None, :]).reshape(-1)
    stored_in = jnp.sum(
        jnp.where(
            columns[:, None] == jnp.arange(owner_map.shape[0], dtype=jnp.int32)[None, :],
            owner_map[None, :],
            0,
        ),
        axis=1,
    )
    targets = groups * nx
    slice_shape = (targets, block_x // targets, block_y, depth)
    picked = pick(
        stored_in,
        jnp.stack([core, jnp.int32(nx)]),
        spread.reshape(slice_shape),
        other.reshape(slice_shape),
    )
    speed = lax.all_to_all(picked.reshape(model_tiles.shape), ("sy", "gx"), 0, 0, tiled=True)
    speed_x = [lax.ppermute(speed, "gx", perm) for perm in x_perms]
    speed_y, speed_xy = [], []
    for f, perm in enumerate(y_perms):
        cut = lax.dynamic_slice_in_dim(speed, sent_rows(f), HALO, axis=1)
        speed_y.append(lax.ppermute(cut, "gy", perm))
        speed_xy.append(
            jnp.stack([lax.ppermute(cut, ("gx", "gy"), joint(x_perm, perm, ny)) for x_perm in x_perms])
        )

    starts = jnp.stack([column, row]).astype(jnp.int32)
    cells = receivers[0]
    local_list = list_receivers(
        block_x, block_y, starts * jnp.array([block_x, block_y], jnp.int32), cells
    )
    local_x, local_y = cells[:, 0] - column * block_x, cells[:, 1] - row * block_y
    inside = (local_x >= 0) & (local_x < block_x) & (local_y >= 0) & (local_y < block_y)
    lanes = jnp.broadcast_to(jnp.where(inside, cells[:, 2], -1)[:, None], (cells.shape[0], depth))
    place = sources[0]
    x_depth = jnp.maximum(block_x - jnp.minimum(place[:, 0] + 1, total_x - place[:, 0]), 0).astype(jnp.float32) / block_x
    y_depth = jnp.maximum(block_x - jnp.minimum(place[:, 1] + 1, total_y - place[:, 1]), 0).astype(jnp.float32) / block_x
    damp = damp_peak * (x_depth * x_depth + y_depth * y_depth)
    amplitudes = wavelet[0] / (1.0 + damp)[:, None]

    out_now, out_prev, partial = window(
        (block_x, block_y, total_x, total_y, ny),
        starts, place.reshape(-1), amplitudes.reshape(-1), local_list, lanes,
        now, prev, now_x, prev_x, sides, corners,
        speed, speed_x, jnp.stack(speed_y), jnp.stack(speed_xy), nx * ny,
    )
    gathered = lax.all_to_all(partial, ("gx", "gy"), 0, 0, tiled=True)
    shots = now.shape[0]
    traces = jnp.sum(gathered, axis=0).reshape(shots, STEPS, -1).transpose(0, 2, 1)
    return (out_now[None], out_prev[None], traces[None])


def solution(mesh):
    shape = dict(zip(mesh.axis_names, mesh.devices.shape))
    cores = 2 if shape["shot"] % 2 == 0 else 1
    fine = Mesh(
        mesh.devices.reshape(shape["shot"] // cores, cores, shape["gx"], shape["gy"]),
        ("sy", "core", "gx", "gy"),
    )
    shot = ("sy", "core")
    field = P(shot, None, "gx", "gy", None)
    return jax.shard_map(
        local,
        mesh=fine,
        in_specs=(
            P(("sy", "core", "gx"), "gy", None),
            P(),
            P(shot),
            field,
            field,
            P(shot, None, None),
            P(shot, None, None),
            P(shot, None, None),
        ),
        out_specs=(field, field, P(shot, None, None, None)),
        check_vma=False,
    )
```

time: 394 us -> 142 us (0.36)
  local copies, waits for them, and re-layouts: 178 us -> 16.3 us
  starting transfers between devices: 101 us -> 32.4 us
  Pallas kernels: 0 us -> 52 us
  blocking collectives: 37.5 us -> 12.9 us
  waiting for transfers between devices: 33.4 us -> 16.7 us
  other arithmetic: 25.8 us -> 9.95 us
  between operations: 15.4 us -> 1.56 us
    div x8 -> x2, local copies, waits for them, and re-layouts: 133 us -> 1.98 us  [local(): amplitudes = wavelet[0] / (1.0 + damp)[:, None]]
    ppermute x32 -> x13, starting transfers between devices: 96.9 us -> 24.3 us  [the longest x2 6.7 us: local(): now_x = [lax.ppermute(now, 'gx', perm) for perm in x_perms]]
    pallas_call x0 -> x3, Pallas kernels: none -> 52 us  [the longest x1 37.5 us: window(): pl.pallas_call(kernel, out_shape=(jax.ShapeDtypeStruct(now.shape, now.dty...]
    psum x1 -> x0, blocking collectives: 37.5 us -> none  [local(): traces = lax.psum(jnp.stack(recorded, axis=-1), ('gx', 'gy'))]
    gather x8 -> x0, local copies, waits for them, and re-layouts: 23.6 us -> none  [sample(): field[:, jnp.clip(local_x, 0, size_x - 1), jnp.clip(local_y, 0, size_y -...]
    div x8 -> x1, other arithmetic: 17.1 us -> 0.68 us  [local(): amplitudes = wavelet[0] / (1.0 + damp)[:, None]]
    slice x26 -> x0, local copies, waits for them, and re-layouts: 16 us -> none  [the longest x16 12.7 us: depth_ahead(): return jnp.concatenate([field[..., reach:], filler], axis=-1)]
    ppermute x32 -> x13, waiting for transfers between devices: 13.4 us -> 0.03 us  [the longest x2 0.01 us: local(): now_x = [lax.ppermute(now, 'gx', perm) for perm in x_perms]]
  transfers between devices with their start and end apart: 34 -> 15, of which waited for: 17 -> 2; matrix products, arithmetic and copies ran while one was open for 42% -> 14% of each run, Pallas kernels for 0% -> 10%
where the time goes in v1:
time: 142 us
  Pallas kernels  52 us (37%)
  starting transfers between devices  32.4 us (23%)
  waiting for transfers between devices  16.7 us (12%)
  local copies, waits for them, and re-layouts  16.3 us (11%)
  blocking collectives  12.9 us (9%)
  other arithmetic  9.95 us (7%)
  between operations  1.56 us (1%)
    pallas_call x1, Pallas kernels, window(): pl.pallas_call(kernel, out_shape=(jax.ShapeDtypeStruct(now.shape, now.dty...  37.5 us
    all_to_all x1, blocking collectives, local(): gathered = lax.all_to_all(partial, ('gx', 'gy'), 0, 0, tiled=True)  12.9 us
    all_to_all x1, waiting for transfers between devices, local(): spread = lax.all_to_all(model_tiles, ('sy', 'gx'), 0, 0, tiled=True)  11.3 us
    pallas_call x1, Pallas kernels, pick(): pl.pallas_call(pick_kernel, out_shape=jax.ShapeDtypeStruct(stored.shape,...  9.81 us
    unnamed x34, local copies, waits for them, and re-layouts  6.81 us
    ppermute x2, starting transfers between devices, local(): now_x = [lax.ppermute(now, 'gx', perm) for perm in x_perms]  6.7 us
    all_to_all x1, waiting for transfers between devices, local(): lax.all_to_all(picked.reshape(model_tiles.shape), ('sy', 'gx'), 0, 0, til...  5.36 us
    ppermute x2, starting transfers between devices, local(): speed_x = [lax.ppermute(speed, 'gx', perm) for perm in x_perms]  5.01 us
  transfers between devices with their start and end apart: 15, of which 2 were waited for; matrix products, arithmetic and copies ran while one was open for 14% of the time, Pallas kernels for 10%

profile of v1, /device:TPU:0, one launch (start us, length us, event | category | flops | bytes accessed | tf_op | source)
XLA Modules:
  0.0 141.7 jit_solution(446452652071364137)
XLA Ops:
  0.6 0.8 collective-permute-start.1
  1.5 5.9 %collective-permute-start = (f32[2,16,32,128]{3,2,1,0:T(8,128)}, f32[2,16,32,128]{3,2,1,0:T(8,128)S(1)}, u32[]{:S(2)}, u32[]{:S(2)}) collective-permute-start(f32[2,16,32,128]{3,2,1,0:T(8,128)} %bitcast.40), channel_id=1, source_target_pairs={{0,2},{2,0},{4,6},{6,4},{1,3},{3,1},{5,7},{7,5},{8,10},{10,8},{12,... | collective-permute-start | bytes 1572872 | tf_op jit(solution)/shard_map/ppermute | solution.py:376
  7.4 0.8 collective-permute-start.3
  8.2 1.8 %collective-permute-start.2 = (f32[2,16,32,128]{3,2,1,0:T(8,128)}, f32[2,16,32,128]{3,2,1,0:T(8,128)S(1)}, u32[]{:S(2)}, u32[]{:S(2)}) collective-permute-start(f32[2,16,32,128]{3,2,1,0:T(8,128)} %bitcast.43), channel_id=1, source_target_pairs={{0,2},{2,0},{4,6},{6,4},{1,3},{3,1},{5,7},{7,5},{8,10},{10,8},{12,... | collective-permute-start | bytes 1572872 | tf_op jit(solution)/shard_map/ppermute | solution.py:377
  9.9 4.7 %all-to-all-start = ((f32[16,32,128]{2,1,0:T(8,128)}), f32[16,32,128]{2,1,0:T(8,128)S(1)}, u32[]{:S(2)}, u32[]{:S(2)}) async-start(f32[16,32,128]{2,1,0:T(8,128)} %param.9), calls=%async_computation | async-start | bytes 524288 | tf_op jit(solution)/shard_map/all_to_all | solution.py:373
  14.6 2.0 %collective-permute-start.6 = (s32[1]{0:T(128)}, s32[1]{0:T(128)}, u32[]{:S(2)}, u32[]{:S(2)}) collective-permute-start(s32[1]{0:T(128)} %param.11), channel_id=1, source_target_pairs={{0,16},{16,0},{1,17},{17,1},{2,18},{18,2},{3,19},{19,3},{4,20},{20... | collective-permute-start | bytes 20 | tf_op jit(solution)/shard_map/ppermute | solution.py:407
  16.7 0.7 constant_dynamic-slice_fusion.10
  18.1 1.9 %pad_maximum_fusion.1 = f32[2,2,16,16,128]{4,3,2,1,0:T(8,128)} fusion(f32[1,2,16,16,128]{4,3,2,1,0:T(8,128)} %constant_dynamic-slice_fusion.9, f32[1,2,16,16,128]{4,3,2,1,0:T(8,128)} %constant_dynamic-slice_fusion.10), kind=kLoop, calls=%fused_computation.1 | loop fusion | flops 131072 | bytes 1048576 | tf_op jit(solution)/shard_map/stack | solution.py:388
  21.9 1.5 %collective-permute-start.4 = (f32[2,2,16,16,128]{4,3,2,1,0:T(8,128)}, f32[2,2,16,16,128]{4,3,2,1,0:T(8,128)}, u32[]{:S(2)}, u32[]{:S(2)}) collective-permute-start(f32[2,2,16,16,128]{4,3,2,1,0:T(8,128)} %pad_maximum_fusion.1), channel_id=1, source_target_pairs={{0,1},{1,0},{2,3},{3,2},{4,5},{5,4},{6,7},{7,6},{8,9},{9,8},{10,11... | collective-permute-start | bytes 1572872 | tf_op jit(solution)/shard_map/ppermute | solution.py:391
  24.8 0.7 select_reduce_fusion.columns
  25.5 11.3 %all-to-all-done = f32[16,32,128]{2,1,0:T(8,128)S(1)} async-done(((f32[16,32,128]{2,1,0:T(8,128)}), f32[16,32,128]{2,1,0:T(8,128)S(1)}, u32[]{:S(2)}, u32[]{:S(2)}) %all-to-all-start) | async-done | bytes 262176 | tf_op jit(solution)/shard_map/all_to_all | solution.py:373
  40.4 9.8 %pick_slices.1 = f32[8,2,32,128]{3,2,1,0:T(8,128)} custom-call(s32[8]{0:T(128)} %select_reduce_fusion.columns, s32[2]{0:T(128)} %pad_add_fusion.1.where, f32[8,2,32,128]{3,2,1,0:T(8,128)} %bitcast.46, f32[8,2,32,128]{3,2,1,0:T(8,128)} %bitcast.48), custom_call_target="tpu_custom_call" | custom-call | tf_op jit(solution)/shard_map/pick_slices/pallas_call | solution.py:57
  50.3 3.4 %all-to-all-start.1 = ((f32[16,32,128]{2,1,0:T(8,128)}), f32[16,32,128]{2,1,0:T(8,128)S(1)}, u32[]{:S(2)}, u32[]{:S(2)}) async-start(f32[16,32,128]{2,1,0:T(8,128)} %bitcast.47), calls=%async_computation.1 | async-start | bytes 524288 | tf_op jit(solution)/shard_map/all_to_all | solution.py:429
  53.7 0.8 copy-done.8
  54.6 0.9 copy-done.6
  55.5 0.9 copy-done.4
  56.5 1.0 pad_maximum_fusion
  57.5 1.5 %collective-permute-start.5 = (f32[2,2,2,8,24,128]{5,4,3,2,1,0:T(8,128)}, f32[2,2,2,8,24,128]{5,4,3,2,1,0:T(8,128)}, u32[]{:S(2)}, u32[]{:S(2)}) collective-permute-start(f32[2,2,2,8,24,128]{5,4,3,2,1,0:T(8,128)} %bitcast.11), channel_id=1, source_target_pairs={{0,1},{1,0},{2,3},{3,2},{4,5},{5,4},{6,7},{7,6},{8,9},{9,8},{10,11... | collective-permute-start | bytes 2359304 | tf_op jit(solution)/shard_map/ppermute | solution.py:402
  59.0 5.4 %all-to-all-done.1.speed = f32[16,32,128]{2,1,0:T(8,128)S(1)} async-done(((f32[16,32,128]{2,1,0:T(8,128)}), f32[16,32,128]{2,1,0:T(8,128)S(1)}, u32[]{:S(2)}, u32[]{:S(2)}) %all-to-all-start.1) | async-done | bytes 262176 | tf_op jit(solution)/shard_map/all_to_all | solution.py:429
  65.7 2.7 %collective-permute-start.11 = (f32[16,16,128]{2,1,0:T(8,128)}, f32[16,16,128]{2,1,0:T(8,128)S(1)}, u32[]{:S(2)}, u32[]{:S(2)}) collective-permute-start(f32[16,16,128]{2,1,0:T(8,128)} %constant_dynamic-slice_fusion), channel_id=1, source_target_pairs={{0,3},{1,2},{2,1},{3,0},{4,7},{5,6},{6,5},{7,4},{8,11},{9,10},{10,... | collective-permute-start | bytes 393224 | tf_op jit(solution)/shard_map/ppermute | solution.py:436
  68.3 1.4 collective-permute-start.9
  69.7 3.6 %collective-permute-start.8 = (f32[16,32,128]{2,1,0:T(8,128)S(1)}, f32[16,32,128]{2,1,0:T(8,128)}, u32[]{:S(2)}, u32[]{:S(2)}) collective-permute-start(f32[16,32,128]{2,1,0:T(8,128)S(1)} %all-to-all-done.1.speed), channel_id=1, source_target_pairs={{0,2},{2,0},{4,6},{6,4},{1,3},{3,1},{5,7},{7,5},{8,10},{10,8},{12,... | collective-permute-start | bytes 786440 | tf_op jit(solution)/shard_map/ppermute | solution.py:430
  74.7 1.7 %collective-permute-start.10 = (f32[16,16,128]{2,1,0:T(8,128)}, f32[16,16,128]{2,1,0:T(8,128)S(1)}, u32[]{:S(2)}, u32[]{:S(2)}) collective-permute-start(f32[16,16,128]{2,1,0:T(8,128)} %constant_dynamic-slice_fusion), channel_id=1, source_target_pairs={{0,1},{1,0},{2,3},{3,2},{4,5},{5,4},{6,7},{7,6},{8,9},{9,8},{10,11... | collective-permute-start | bytes 393224 | tf_op jit(solution)/shard_map/ppermute | solution.py:434
  77.0 0.8 reshape_squeeze.6.sources
  77.8 0.8 copy.13
  78.6 1.3 squeeze.10
  80.5 1.3 div.23
  81.8 1.7 %reshape_squeeze.7.receivers = s32[768]{0:T(1024)} reshape(s32[1,256,3]{2,1,0:T(8,128)} %copy.13) | data formatting | bytes 6144 | tf_op jit(solution)/shard_map/reshape;squeeze | solution.py:89
  84.2 4.7 %list_receivers.1.local_list = s32[520]{0:T(1024)} custom-call(s32[2]{0:T(128)} %get-tuple-element.9.starts, s32[768]{0:T(1024)} %reshape_squeeze.7.receivers), custom_call_target="tpu_custom_call" | custom-call | tf_op jit(solution)/shard_map/list_receivers/pallas_call | solution.py:83
  88.9 1.0 maximum_bitcast_fusion.rest_1_
  90.7 37.5 %wave_window.1 = (f32[2,16,32,128]{3,2,1,0:T(8,128)}, f32[2,16,32,128]{3,2,1,0:T(8,128)}, f32[8,16,256]{2,1,0:T(8,128)S(1)}) custom-call(s32[2]{0:T(128)S(1)} %get-tuple-element.10.starts, s32[6]{0:T(128)S(1)} %reshape_squeeze.6.sources, f32[16]{0:T(128)S(1)} %div.24.amplitudes, s32[520]{0:T(1024)S(1)} %copy-done.2, s32[256,128]{1,0:T(8,128)S(1)} %broadcast_in_dim.57.lanes, ...), custom_call_target="tpu_custom_call" | custom-call | tf_op jit(solution)/shard_map/wave_window/pallas_call | solution.py:334
  128.2 12.9 %all_to_all.15 = f32[8,16,256]{2,1,0:T(8,128)S(1)} all-to-all(f32[8,16,256]{2,1,0:T(8,128)S(1)} %get-tuple-element.8), channel_id=1, replica_groups=mesh['sy'=2,'core'=2,'gx'=4,'gy'=2] {'gx','gy'}, dimensions={0} | all-to-all | bytes 262144 | tf_op jit(solution)/shard_map/all_to_all | solution.py:459
  (70 shorter events, 13.2 us)
Async XLA Ops:
  0.6 16.0 %copy-start = (f32[1,2,16,32,128]{4,3,2,1,0:T(8,128)S(1)}, f32[1,2,16,32,128]{4,3,2,1,0:T(8,128)}, u32[]{:S(2)}) copy-start(f32[1,2,16,32,128]{4,3,2,1,0:T(8,128)} %param.12) | copy-start | bytes 1572868
  0.6 36.2 %collective-permute-start.1 = (f32[2,16,32,128]{3,2,1,0:T(8,128)}, f32[2,16,32,128]{3,2,1,0:T(8,128)S(1)}, u32[]{:S(2)}, u32[]{:S(2)}) collective-permute-start(f32[2,16,32,128]{3,2,1,0:T(8,128)} %bitcast.39), channel_id=1, source_target_pairs={{2,4},{4,2},{3,5},{5,3},{10,12},{12,10},{11,13},{13,11},{18,20},{2... | collective-permute-start | bytes 1572872 | tf_op jit(solution)/shard_map/ppermute | solution.py:376
  1.5 36.1 %collective-permute-start = (f32[2,16,32,128]{3,2,1,0:T(8,128)}, f32[2,16,32,128]{3,2,1,0:T(8,128)S(1)}, u32[]{:S(2)}, u32[]{:S(2)}) collective-permute-start(f32[2,16,32,128]{3,2,1,0:T(8,128)} %bitcast.40), channel_id=1, source_target_pairs={{0,2},{2,0},{4,6},{6,4},{1,3},{3,1},{5,7},{7,5},{8,10},{10,8},{12,... | collective-permute-start | bytes 1572872 | tf_op jit(solution)/shard_map/ppermute | solution.py:376
  7.4 10.0 %copy-start.1 = (f32[1,2,16,32,128]{4,3,2,1,0:T(8,128)S(1)}, f32[1,2,16,32,128]{4,3,2,1,0:T(8,128)}, u32[]{:S(2)}) copy-start(f32[1,2,16,32,128]{4,3,2,1,0:T(8,128)} %param.13) | copy-start | bytes 1572868
  7.4 29.5 %collective-permute-start.3 = (f32[2,16,32,128]{3,2,1,0:T(8,128)}, f32[2,16,32,128]{3,2,1,0:T(8,128)S(1)}, u32[]{:S(2)}, u32[]{:S(2)}) collective-permute-start(f32[2,16,32,128]{3,2,1,0:T(8,128)} %bitcast.42), channel_id=1, source_target_pairs={{2,4},{4,2},{3,5},{5,3},{10,12},{12,10},{11,13},{13,11},{18,20},{2... | collective-permute-start | bytes 1572872 | tf_op jit(solution)/shard_map/ppermute | solution.py:377
  8.2 29.5 %collective-permute-start.2 = (f32[2,16,32,128]{3,2,1,0:T(8,128)}, f32[2,16,32,128]{3,2,1,0:T(8,128)S(1)}, u32[]{:S(2)}, u32[]{:S(2)}) collective-permute-start(f32[2,16,32,128]{3,2,1,0:T(8,128)} %bitcast.43), channel_id=1, source_target_pairs={{0,2},{2,0},{4,6},{6,4},{1,3},{3,1},{5,7},{7,5},{8,10},{10,8},{12,... | collective-permute-start | bytes 1572872 | tf_op jit(solution)/shard_map/ppermute | solution.py:377
  9.9 26.9 %all-to-all-start = ((f32[16,32,128]{2,1,0:T(8,128)}), f32[16,32,128]{2,1,0:T(8,128)S(1)}, u32[]{:S(2)}, u32[]{:S(2)}) async-start(f32[16,32,128]{2,1,0:T(8,128)} %param.9), calls=%async_computation | async-start | bytes 524288 | tf_op jit(solution)/shard_map/all_to_all | solution.py:373
  14.6 7.3 %collective-permute-start.6 = (s32[1]{0:T(128)}, s32[1]{0:T(128)}, u32[]{:S(2)}, u32[]{:S(2)}) collective-permute-start(s32[1]{0:T(128)} %param.11), channel_id=1, source_target_pairs={{0,16},{16,0},{1,17},{17,1},{2,18},{18,2},{3,19},{19,3},{4,20},{20... | collective-permute-start | bytes 20 | tf_op jit(solution)/shard_map/ppermute | solution.py:407
  21.2 0.7 copy-start.11
  21.9 68.0 %collective-permute-start.4 = (f32[2,2,16,16,128]{4,3,2,1,0:T(8,128)}, f32[2,2,16,16,128]{4,3,2,1,0:T(8,128)}, u32[]{:S(2)}, u32[]{:S(2)}) collective-permute-start(f32[2,2,16,16,128]{4,3,2,1,0:T(8,128)} %pad_maximum_fusion.1), channel_id=1, source_target_pairs={{0,1},{1,0},{2,3},{3,2},{4,5},{5,4},{6,7},{7,6},{8,9},{9,8},{10,11... | collective-permute-start | bytes 1572872 | tf_op jit(solution)/shard_map/ppermute | solution.py:391
  24.1 0.7 copy-start.15
  36.8 0.7 copy-start.3
  36.8 2.9 %collective-permute-start.7 = (f32[16,32,128]{2,1,0:T(8,128)S(1)}, f32[16,32,128]{2,1,0:T(8,128)S(1)}, u32[]{:S(2)}, u32[]{:S(2)}) collective-permute-start(f32[16,32,128]{2,1,0:T(8,128)S(1)} %all-to-all-done), channel_id=1, source_target_pairs={{0,8},{8,0},{1,9},{9,1},{2,10},{10,2},{3,11},{11,3},{4,12},{12,4},... | collective-permute-start | bytes 786440 | tf_op jit(solution)/shard_map/ppermute | solution.py:374
  39.7 0.7 copy-start.7
  50.3 14.1 %all-to-all-start.1 = ((f32[16,32,128]{2,1,0:T(8,128)}), f32[16,32,128]{2,1,0:T(8,128)S(1)}, u32[]{:S(2)}, u32[]{:S(2)}) async-start(f32[16,32,128]{2,1,0:T(8,128)} %bitcast.47), calls=%async_computation.1 | async-start | bytes 524288 | tf_op jit(solution)/shard_map/all_to_all | solution.py:429
  53.7 0.8 copy-start.8
  54.5 0.9 copy-start.6
  55.4 0.9 copy-start.4
  55.4 1.0 copy-start.5
  57.5 32.5 %collective-permute-start.5 = (f32[2,2,2,8,24,128]{5,4,3,2,1,0:T(8,128)}, f32[2,2,2,8,24,128]{5,4,3,2,1,0:T(8,128)}, u32[]{:S(2)}, u32[]{:S(2)}) collective-permute-start(f32[2,2,2,8,24,128]{5,4,3,2,1,0:T(8,128)} %bitcast.11), channel_id=1, source_target_pairs={{0,1},{1,0},{2,3},{3,2},{4,5},{5,4},{6,7},{7,6},{8,9},{9,8},{10,11... | collective-permute-start | bytes 2359304 | tf_op jit(solution)/shard_map/ppermute | solution.py:402
  65.0 4.7 %collective-permute-start.12 = (f32[16,16,128]{2,1,0:T(8,128)}, f32[16,16,128]{2,1,0:T(8,128)S(1)}, u32[]{:S(2)}, u32[]{:S(2)}) collective-permute-start(f32[16,16,128]{2,1,0:T(8,128)} %constant_dynamic-slice_fusion), channel_id=1, source_target_pairs={{2,5},{3,4},{4,3},{5,2},{10,13},{11,12},{12,11},{13,10},{18,21},{1... | collective-permute-start | bytes 393224 | tf_op jit(solution)/shard_map/ppermute | solution.py:436
  65.7 9.0 %collective-permute-start.11 = (f32[16,16,128]{2,1,0:T(8,128)}, f32[16,16,128]{2,1,0:T(8,128)S(1)}, u32[]{:S(2)}, u32[]{:S(2)}) collective-permute-start(f32[16,16,128]{2,1,0:T(8,128)} %constant_dynamic-slice_fusion), channel_id=1, source_target_pairs={{0,3},{1,2},{2,1},{3,0},{4,7},{5,6},{6,5},{7,4},{8,11},{9,10},{10,... | collective-permute-start | bytes 393224 | tf_op jit(solution)/shard_map/ppermute | solution.py:436
  68.3 21.6 %collective-permute-start.9 = (f32[16,32,128]{2,1,0:T(8,128)S(1)}, f32[16,32,128]{2,1,0:T(8,128)}, u32[]{:S(2)}, u32[]{:S(2)}) collective-permute-start(f32[16,32,128]{2,1,0:T(8,128)S(1)} %all-to-all-done.1.speed), channel_id=1, source_target_pairs={{2,4},{4,2},{3,5},{5,3},{10,12},{12,10},{11,13},{13,11},{18,20},{2... | collective-permute-start | bytes 786440 | tf_op jit(solution)/shard_map/ppermute | solution.py:430
  69.7 6.6 %copy-start.9 = (f32[16,16,128]{2,1,0:T(8,128)}, f32[16,16,128]{2,1,0:T(8,128)S(1)}, u32[]{:S(2)}) copy-start(f32[16,16,128]{2,1,0:T(8,128)S(1)} %collective-permute-done.12) | copy-start | bytes 393220
  69.7 20.2 %collective-permute-start.8 = (f32[16,32,128]{2,1,0:T(8,128)S(1)}, f32[16,32,128]{2,1,0:T(8,128)}, u32[]{:S(2)}, u32[]{:S(2)}) collective-permute-start(f32[16,32,128]{2,1,0:T(8,128)S(1)} %all-to-all-done.1.speed), channel_id=1, source_target_pairs={{0,2},{2,0},{4,6},{6,4},{1,3},{3,1},{5,7},{7,5},{8,10},{10,8},{12,... | collective-permute-start | bytes 786440 | tf_op jit(solution)/shard_map/ppermute | solution.py:430
  73.3 0.7 copy-start.13
  74.7 1.7 %copy-start.12 = (s32[1,2,3]{2,1,0:T(2,128)S(1)}, s32[1,2,3]{2,1,0:T(2,128)}, u32[]{:S(2)}) copy-start(s32[1,2,3]{2,1,0:T(2,128)} %param.14) | copy-start | bytes 76
  74.7 1.7 %copy-start.10 = (f32[16,16,128]{2,1,0:T(8,128)}, f32[16,16,128]{2,1,0:T(8,128)S(1)}, u32[]{:S(2)}) copy-start(f32[16,16,128]{2,1,0:T(8,128)S(1)} %collective-permute-done.11) | copy-start | bytes 393220
  74.7 15.2 %collective-permute-start.10 = (f32[16,16,128]{2,1,0:T(8,128)}, f32[16,16,128]{2,1,0:T(8,128)S(1)}, u32[]{:S(2)}, u32[]{:S(2)}) collective-permute-start(f32[16,16,128]{2,1,0:T(8,128)} %constant_dynamic-slice_fusion), channel_id=1, source_target_pairs={{0,1},{1,0},{2,3},{3,2},{4,5},{5,4},{6,7},{7,6},{8,9},{9,8},{10,11... | collective-permute-start | bytes 393224 | tf_op jit(solution)/shard_map/ppermute | solution.py:434
  78.6 1.3 copy-start.14
  90.0 0.7 copy-start.2

commit v2 on v1

v2 whole, which is shorter than its diff:
```python
import functools

import jax
import jax.numpy as jnp
from jax import lax
from jax.experimental import pallas as pl
from jax.experimental.pallas import tpu as pltpu
from jax.sharding import Mesh
from jax.sharding import PartitionSpec as P

STEPS = 8
HALO = 2 * STEPS
PAD = 8
GROUP = 4
BATCH = 4

near_weight = 4.0 / 3.0
centre_part = -7.5 * 0.75
far_part = -1.0 / 16.0
damp_peak = 0.3

SMEM = pl.BlockSpec(memory_space=pltpu.SMEM)
ANY = pl.BlockSpec(memory_space=pl.ANY)
VMEM = pl.BlockSpec(memory_space=pltpu.VMEM)


def pairs(count, parity):
    return [
        pair
        for i in range(parity, count - 1, 2)
        for pair in ((i, i + 1), (i + 1, i))
    ]


def joint(first, second, count):
    return [(a * count + b, c * count + d) for a, c in first for b, d in second]


def prepare_kernel(block_x, block_y, places, owner_map, shifts, receivers, stored_in, local_list):
    column, row, across = places[0], places[1], places[2]
    targets = stored_in.shape[0]
    for t in range(targets):
        stored_in[t] = owner_map[shifts[t]]
    x_first, y_first = column * block_x, row * block_y
    total = receivers.shape[1]
    batch = 8

    def body(g, count):
        for i in range(batch):
            r = g * batch + i
            x = receivers[0, r] - x_first
            y = receivers[1, r] - y_first
            inside = (x >= 0) & (x < block_x) & (y >= 0) & (y < block_y)
            local_list[1 + 3 * count] = r
            local_list[2 + 3 * count] = x * block_y + y
            local_list[3 + 3 * count] = receivers[2, r]
            count = count + inside.astype(jnp.int32)
        return count

    count = lax.fori_loop(0, total // batch, body, jnp.int32(0))
    local_list[0] = count
    for i in range(BATCH):
        local_list[1 + 3 * (count + i)] = total
        local_list[2 + 3 * (count + i)] = 0
        local_list[3 + 3 * (count + i)] = 0


def prepare(block_x, block_y, places, owner_map, shifts, receivers):
    total = receivers.shape[1]
    return pl.pallas_call(
        functools.partial(prepare_kernel, block_x, block_y),
        out_shape=(
            jax.ShapeDtypeStruct(shifts.shape, jnp.int32),
            jax.ShapeDtypeStruct((3 * (total + BATCH) + 8,), jnp.int32),
        ),
        in_specs=[SMEM] * 4,
        out_specs=(SMEM, SMEM),
        name="prepare_lists",
    )(places, owner_map, shifts, receivers)


def pick_kernel(stored_in, places, stored, other, out, sems):
    targets = out.shape[0]
    across, core = places[2], places[3]
    copies = []
    for t in range(targets):
        block = stored_in[t]
        owner_core = (block // across) % 2
        row = (block // (2 * across)) * across + block % across
        here = pltpu.make_async_copy(stored.at[row], out.at[t], sems.at[t])
        there = pltpu.make_async_copy(other.at[row], out.at[t], sems.at[t])
        pl.when(owner_core == core)(here.start)
        pl.when(owner_core != core)(there.start)
        copies.append(here)
    for copy in copies:
        copy.wait()


def pick(stored_in, places, stored, other):
    targets = stored.shape[0]
    return pl.pallas_call(
        pick_kernel,
        out_shape=jax.ShapeDtypeStruct(stored.shape, stored.dtype),
        in_specs=[SMEM, SMEM, ANY, ANY],
        out_specs=VMEM,
        scratch_shapes=[pltpu.SemaphoreType.DMA((targets,))],
        name="pick_slices",
    )(stored_in, places, stored, other)


def corner_kernel(block_y, parity_y, places, first, second, out, sems):
    half = HALO // 2
    odd_x, odd_y = places[0] % 2, places[1] % 2
    above = odd_y == parity_y
    start = pl.multiple_of(jnp.where(above, block_y - HALO, 0), 8)
    near_start = pl.multiple_of(jnp.where(above, block_y - half, 0), 8)
    copies = []
    for e, block in enumerate((first, second)):
        near = jnp.where(odd_x == e, 0, half)
        copies.append(
            pltpu.make_async_copy(
                block.at[:, pl.ds(near, half), pl.ds(start, HALO)],
                out.at[e, :, :, pl.ds(0, HALO)],
                sems.at[2 * e],
            )
        )
        copies.append(
            pltpu.make_async_copy(
                block.at[:, pl.ds(half - near, half), pl.ds(near_start, half)],
                out.at[e, :, :, pl.ds(HALO, half)],
                sems.at[2 * e + 1],
            )
        )
    for copy in copies:
        copy.start()
    for copy in copies:
        copy.wait()


def pack_corners(parity_y, places, blocks):
    shots, _, block_y, depth = blocks[0].shape
    half = HALO // 2
    return pl.pallas_call(
        functools.partial(corner_kernel, block_y, parity_y),
        out_shape=jax.ShapeDtypeStruct((2, shots, half, HALO + half, depth), jnp.float32),
        in_specs=[SMEM, ANY, ANY],
        out_specs=VMEM,
        scratch_shapes=[pltpu.SemaphoreType.DMA((4,))],
        name="pack_corners",
    )(places, *blocks)


def side_kernel(block_y, parity_y, places, now, prev, out, sems):
    start = pl.multiple_of(jnp.where(places[1] % 2 == parity_y, block_y - HALO, 0), 8)
    copies = [
        pltpu.make_async_copy(block.at[:, :, pl.ds(start, HALO)], out.at[k], sems.at[k])
        for k, block in enumerate((now, prev))
    ]
    for copy in copies:
        copy.start()
    for copy in copies:
        copy.wait()


def pack_sides(parity_y, places, now, prev):
    shots, block_x, block_y, depth = now.shape
    return pl.pallas_call(
        functools.partial(side_kernel, block_y, parity_y),
        out_shape=jax.ShapeDtypeStruct((2, shots, block_x, HALO, depth), jnp.float32),
        in_specs=[SMEM, ANY, ANY],
        out_specs=VMEM,
        scratch_shapes=[pltpu.SemaphoreType.DMA((2,))],
        name="pack_sides",
    )(places, now, prev)


def window_kernel(
    sizes,
    starts,
    sources,
    amplitudes,
    local_list,
    now,
    prev,
    now_x,
    prev_x,
    sides,
    corners_now,
    corners_prev,
    speed,
    speed_x,
    speed_y,
    speed_xy,
    out_now,
    out_prev,
    partial,
    ext_all,
    samples,
    sems,
    out_sems,
):
    block_x, block_y, total_x, total_y, ny = sizes
    half_way = (ext_all.shape[0] - 2) // 2
    now_ext, prev_ext = ext_all.at[pl.ds(0, half_way)], ext_all.at[pl.ds(half_way, half_way)]
    near, twice = ext_all.at[2 * half_way], ext_all.at[2 * half_way + 1]
    rows = now_ext.shape[2]
    planes = now_ext.shape[1]
    shots = now_ext.shape[0]
    column, row = starts[0], starts[1]
    odd_x, odd_y = column % 2, row % 2
    own = pl.multiple_of(PAD + (HALO * odd_y if ny == 2 else HALO), 8)
    high_x = [odd_x == 0, odd_x == 1]
    high_y = [odd_y == 0, odd_y == 1]
    x_at = [jnp.where(h, HALO + block_x, 0) for h in high_x]
    y_at = [
        pl.multiple_of(jnp.where(h, own + block_y, own - HALO), 8) for h in high_y
    ]
    near_x = [jnp.where(h, 0, HALO // 2) for h in high_x]
    near_y = [
        pl.multiple_of(jnp.where(h, own + block_y, own - HALO // 2), 8) for h in high_y
    ]
    far_y = [
        pl.multiple_of(jnp.where(h, own + block_y + HALO // 2, own - HALO), 8)
        for h in high_y
    ]
    half = HALO // 2
    copies = []

    def fetch(src, dst):
        copy = pltpu.make_async_copy(src, dst, sems.at[len(copies)])
        copy.start()
        copies.append(copy)

    y_count = speed_y.shape[0]
    corners = (corners_now, corners_prev)
    own_rows = pl.ds(own, block_y)
    fetch(speed, near.at[pl.ds(HALO, block_x), own_rows])
    for e in range(2):
        fetch(speed_x[e], near.at[pl.ds(x_at[e], block_x), own_rows])
    for f in range(y_count):
        at = pl.ds(y_at[f], HALO)
        fetch(speed_y.at[f], near.at[pl.ds(HALO, block_x), at])
        for e in range(2):
            fetch(speed_xy.at[f, e], near.at[pl.ds(x_at[e], block_x), at])
    speed_copies = len(copies)
    fetch(now, now_ext.at[:, pl.ds(HALO, block_x), own_rows])
    fetch(prev, prev_ext.at[:, pl.ds(HALO, block_x), own_rows])
    for e in range(2):
        at = pl.ds(x_at[e], block_x)
        fetch(now_x[e], now_ext.at[:, at, own_rows])
        fetch(prev_x[e], prev_ext.at[:, at, own_rows])
    for f in range(y_count):
        at = pl.ds(y_at[f], HALO)
        fetch(sides.at[f, 0], now_ext.at[:, pl.ds(HALO, block_x), at])
        fetch(sides.at[f, 1], prev_ext.at[:, pl.ds(HALO, block_x), at])
        for e in range(2):
            at_near = pl.ds(x_at[e] + near_x[e], half)
            at_far = pl.ds(x_at[e] + half - near_x[e], half)
            for k, ext in enumerate((now_ext, prev_ext)):
                fetch(
                    corners[k].at[f, e, :, :, pl.ds(0, HALO)],
                    ext.at[:, at_near, at],
                )
                fetch(
                    corners[k].at[f, e, :, :, pl.ds(HALO, half)],
                    ext.at[:, at_far, pl.ds(near_y[f], half)],
                )

    blank = jnp.zeros((PAD, now_ext.shape[3]), jnp.float32)
    for ext in (now_ext, prev_ext):
        for s in range(shots):

            def clear(x, _):
                ext[s, x, pl.ds(0, PAD)] = blank
                ext[s, x, pl.ds(rows - PAD, PAD)] = blank
                return 0

            lax.fori_loop(0, planes, clear, 0)
            for f in range(y_count):
                for e in range(2):

                    def clear_far(x, _):
                        ext[s, x_at[e] + half - near_x[e] + x, pl.ds(far_y[f], half)] = blank
                        return 0

                    lax.fori_loop(0, half, clear_far, 0)

    def depth_in(cell, total):
        inside = (cell >= 0) & (cell < total)
        depth = jnp.maximum(
            block_x - jnp.minimum(cell + 1, total - cell), 0
        ).astype(jnp.float32) / block_x
        return inside, depth

    x_first = column * block_x - HALO
    y_first = row * block_y - own
    shape = (rows, now_ext.shape[3])
    y_in, y_depth = depth_in(lax.broadcasted_iota(jnp.int32, shape, 0) + y_first, total_y)
    y_part = y_depth * y_depth

    for k in range(shots * STEPS):
        samples[k] = jnp.zeros(samples.shape[1:], jnp.float32)
    for copy in copies[:speed_copies]:
        copy.wait()

    def prepare(x, _):
        x_in, x_depth = depth_in(jnp.full(shape, x + x_first, jnp.int32), total_x)
        inverse = 1.0 / (1.0 + damp_peak * (x_depth * x_depth + y_part))
        inverse = jnp.where(x_in & y_in, inverse, 0.0)
        v = near[x]
        near[x] = jnp.where(x_in & y_in, inverse * (v * v) * near_weight, 0.0)
        twice[x] = 2.0 * inverse
        return 0

    lax.fori_loop(2, planes - 2, prepare, 0, unroll=2)
    for copy in copies[speed_copies:]:
        copy.wait()

    depth = now_ext.shape[3]
    gap = lax.broadcasted_iota(jnp.int32, (depth, depth), 0) - lax.broadcasted_iota(jnp.int32, (depth, depth), 1)
    gap = jnp.abs(gap)
    band = jnp.where(gap == 0, centre_part, jnp.where(gap == 1, 1.0, jnp.where(gap == 2, far_part, 0.0)))
    band = band.astype(jnp.bfloat16)
    band = jnp.concatenate([band, band], axis=0)
    lane_row = lax.broadcasted_iota(jnp.int32, (1, depth), 1)

    cur, old = now_ext, prev_ext
    for step in range(1, STEPS + 1):
        reach = 2 * (STEPS - step)
        side = -(-reach // 8)
        if ny == 2:
            first = pl.multiple_of(own - 8 * side * odd_y, 8)
            tiles = block_y // 8 + side
        else:
            first = pl.multiple_of(own - 8 * side, 8)
            tiles = block_y // 8 + 2 * side

        size = 8 * tiles

        def plane(g, _, cur=cur, old=old, first=first, tiles=tiles, size=size, step=step):
            x = 2 * step + GROUP * g
            along = []
            for s in range(shots):
                c = cur[s, pl.ds(x, GROUP), pl.ds(first, size)].reshape(GROUP * size, depth)
                head = c.astype(jnp.bfloat16)
                rest = (c - head.astype(jnp.float32)).astype(jnp.bfloat16)
                parts = jnp.concatenate([head, rest], axis=1)
                out = jnp.dot(parts, band, preferred_element_type=jnp.float32)
                along.append(out.reshape(GROUP, size, depth))
            for s in range(shots):
                for j in range(tiles):
                    base = first + 8 * j
                    at = pl.ds(pl.multiple_of(base, 8), 8)
                    n = [near[x + i, at] for i in range(GROUP)]
                    a = [twice[x + i, at] for i in range(GROUP)]
                    c = [cur[s, x + i - 2, at] for i in range(GROUP + 4)]
                    out = []
                    for i in range(GROUP):
                        m = c[i + 2]
                        close = (c[i + 1] + c[i + 3]) + (cur[s, x + i, pl.ds(base - 1, 8)] + cur[s, x + i, pl.ds(base + 1, 8)])
                        wide = (c[i] + c[i + 4]) + (cur[s, x + i, pl.ds(base - 2, 8)] + cur[s, x + i, pl.ds(base + 2, 8)])
                        p = old[s, x + i, at]
                        lap = along[s][i, 8 * j : 8 * j + 8] + close + far_part * wide
                        out.append(p + a[i] * (m - p) + n[i] * lap)
                    for i in range(GROUP):
                        old[s, x + i, at] = out[i]
            return 0

        lax.fori_loop(0, (planes - 4 * step) // GROUP, plane, 0)

        for s in range(shots):
            sx = sources[s, 0] - x_first
            sy = sources[s, 1] - y_first
            sz = sources[s, 2]
            amplitude = amplitudes[s, step - 1]
            inside = (
                (sx >= 2 * step)
                & (sx < planes - 2 * step)
                & (sy >= first)
                & (sy < first + 8 * tiles)
            )

            @pl.when(inside)
            def _(old=old, s=s, sx=sx, sy=sy, sz=sz, amplitude=amplitude):
                at = pl.ds(sy, 1)
                old[s, sx, at] += jnp.where(lane_row == sz, (0.5 * amplitude) * twice[sx, at], 0.0)

        cur, old = old, cur

        def take(g, _, cur=cur, step=step):
            found = []
            for i in range(BATCH):
                at = 1 + 3 * (BATCH * g + i)
                cell, z = local_list[at + 1], local_list[at + 2]
                x = HALO + cell // block_y
                y = own + cell % block_y
                for s in range(shots):
                    found.append(jnp.where(lane_row == z, cur[s, x, pl.ds(y, 1)], 0.0))
            for i in range(BATCH):
                r = local_list[1 + 3 * (BATCH * g + i)]
                for s in range(shots):
                    samples[s * STEPS + step - 1, pl.ds(r, 1)] = found[i * shots + s]
            return 0

        lax.fori_loop(0, (local_list[0] + BATCH - 1) // BATCH, take, 0)
        if step >= STEPS - 1:
            out = out_prev if step == STEPS - 1 else out_now
            copy = pltpu.make_async_copy(
                cur.at[:, pl.ds(HALO, block_x), own_rows],
                out,
                out_sems.at[step - STEPS + 1],
            )
            copy.start()
            if step == STEPS - 1:
                first_out = copy
            else:
                last_out = copy

    total = partial.shape[2]
    for k in range(shots * STEPS):
        values = jnp.sum(samples[k, pl.ds(0, total)], axis=1)
        for copy_to in range(partial.shape[0]):
            partial[copy_to, k] = values
    first_out.wait()
    last_out.wait()


def window(sizes, starts, sources, amplitudes, local_list, recs, now, prev, now_x, prev_x, sides, corners, speed, speed_x, speed_y, speed_xy, copies):
    block_x, block_y, total_x, total_y, ny = sizes
    shots, _, _, depth = now.shape
    planes = block_x + 2 * HALO
    rows = block_y + (HALO if ny == 2 else 2 * HALO) + 2 * PAD

    def kernel(starts, sources, amplitudes, local_list, now, prev, n0, n1, p0, p1, sides, corners_now, corners_prev, speed, v0, v1, *rest):
        window_kernel(
            sizes, starts, sources, amplitudes, local_list, now, prev,
            (n0, n1), (p0, p1), sides, corners_now, corners_prev, speed, (v0, v1), *rest,
        )

    return pl.pallas_call(
        kernel,
        out_shape=(
            jax.ShapeDtypeStruct(now.shape, now.dtype),
            jax.ShapeDtypeStruct(now.shape, now.dtype),
            jax.ShapeDtypeStruct((copies, shots * STEPS, recs), now.dtype),
        ),
        in_specs=[SMEM] * 4 + [ANY] * 14,
        out_specs=(ANY, ANY, VMEM),
        scratch_shapes=[
            pltpu.VMEM((2 * shots + 2, planes, rows, depth), jnp.float32),
            pltpu.VMEM((shots * STEPS, recs + 8, depth), jnp.float32),
            pltpu.SemaphoreType.DMA((48,)),
            pltpu.SemaphoreType.DMA((2,)),
        ],
        compiler_params=pltpu.CompilerParams(vmem_limit_bytes=40 * 2**20),
        name="wave_window",
    )(
        starts, sources, amplitudes, local_list, now, prev, *now_x, *prev_x,
        sides, *corners, speed, *speed_x, speed_y, speed_xy,
    )


def local(model_tiles, owner_map, offsets, field_now, field_prev, sources, wavelet, receivers):
    block_x, block_y, depth = model_tiles.shape
    nx, ny, groups = lax.axis_size("gx"), lax.axis_size("gy"), lax.axis_size("sy")
    column, row, core = lax.axis_index("gx"), lax.axis_index("gy"), lax.axis_index("core")
    shot_row = lax.axis_index("sy")
    total_x, total_y = block_x * nx, block_y * ny
    now, prev = field_now[0], field_prev[0]
    x_perms = [pairs(nx, 0), pairs(nx, 1)]
    y_perms = [pairs(ny, f) for f in range(2 if ny > 2 else 1)]
    places = jnp.stack([column, row, jnp.int32(nx), core]).astype(jnp.int32)

    now_x = [lax.ppermute(now, "gx", perm) for perm in x_perms]
    spread = lax.all_to_all(model_tiles, ("sy", "gx"), 0, 0, tiled=True)
    other = lax.ppermute(spread, "core", [(0, 1), (1, 0)])
    prev_x = [lax.ppermute(prev, "gx", perm) for perm in x_perms]
    sides = jnp.stack(
        [lax.ppermute(pack_sides(f, places, now, prev), "gy", perm) for f, perm in enumerate(y_perms)]
    )
    corners = [
        jnp.stack(
            [lax.ppermute(pack_corners(f, places, blocks), "gy", perm) for f, perm in enumerate(y_perms)]
        )
        for blocks in (now_x, prev_x)
    ]

    shifts = jnp.zeros((groups,), jnp.int32)
    for turn in range(groups):
        came = offsets if turn == 0 else lax.ppermute(
            offsets, "sy", [(i, (i + turn) % groups) for i in range(groups)]
        )
        at = (shot_row - turn) % groups
        shifts = jnp.where(jnp.arange(groups) == at, came, shifts)
    columns = (shifts[:, None] + jnp.arange(nx, dtype=jnp.int32)[None, :]).reshape(-1)
    stored_in, local_list = prepare(block_x, block_y, places, owner_map, columns, receivers[0].T)
    targets = groups * nx
    slice_shape = (targets, block_x // targets, block_y, depth)
    picked = pick(stored_in, places, spread.reshape(slice_shape), other.reshape(slice_shape))
    speed = lax.all_to_all(picked.reshape(model_tiles.shape), ("sy", "gx"), 0, 0, tiled=True)
    speed_x = [lax.ppermute(speed, "gx", perm) for perm in x_perms]
    speed_y, speed_xy = [], []
    for f, perm in enumerate(y_perms):
        start = jnp.where(row % 2 == f, block_y - HALO, 0)
        part = lax.dynamic_slice_in_dim(speed, start, HALO, axis=1)
        speed_y.append(lax.ppermute(part, "gy", perm))
        speed_xy.append(
            jnp.stack([lax.ppermute(part, ("gx", "gy"), joint(x_perm, perm, ny)) for x_perm in x_perms])
        )

    out_now, out_prev, partial = window(
        (block_x, block_y, total_x, total_y, ny),
        places, sources[0], wavelet[0], local_list, receivers.shape[1],
        now, prev, now_x, prev_x, sides, corners,
        speed, speed_x, jnp.stack(speed_y), jnp.stack(speed_xy), nx * ny,
    )
    gathered = lax.all_to_all(partial, ("gx", "gy"), 0, 0, tiled=True)
    shots = now.shape[0]
    traces = jnp.sum(gathered, axis=0).reshape(shots, STEPS, -1).transpose(0, 2, 1)
    return (out_now[None], out_prev[None], traces[None])


def solution(mesh):
    shape = dict(zip(mesh.axis_names, mesh.devices.shape))
    cores = 2 if shape["shot"] % 2 == 0 else 1
    fine = Mesh(
        mesh.devices.reshape(shape["shot"] // cores, cores, shape["gx"], shape["gy"]),
        ("sy", "core", "gx", "gy"),
    )
    shot = ("sy", "core")
    field = P(shot, None, "gx", "gy", None)
    return jax.shard_map(
        local,
        mesh=fine,
        in_specs=(
            P(("sy", "core", "gx"), "gy", None),
            P(),
            P(shot),
            field,
            field,
            P(shot, None, None),
            P(shot, None, None),
            P(shot, None, None),
        ),
        out_specs=(field, field, P(shot, None, None, None)),
        check_vma=False,
    )
```

time: 142 us -> 113 us (0.80)
  Pallas kernels: 52 us -> 34.4 us
  other arithmetic: 9.95 us -> 2.05 us
  local copies, waits for them, and re-layouts: 16.3 us -> 8.47 us
  starting transfers between devices: 32.4 us -> 36.8 us
  waiting for transfers between devices: 16.7 us -> 12.6 us
  blocking collectives: 12.9 us -> 15.8 us
    pallas_call x1, Pallas kernels: 37.5 us -> 20.5 us  [window(): pl.pallas_call(kernel, out_shape=(jax.ShapeDtypeStruct(now.shape, now.dty...]
    ppermute x5 -> x6, waiting for transfers between devices: 0.01 us -> 12.6 us  [the longest x2 10.5 us: local(): lax.ppermute(pack_corners(f, places, blocks), 'gy', perm)]
    all_to_all x1, waiting for transfers between devices: 11.3 us -> 0.01 us  [local(): spread = lax.all_to_all(model_tiles, ('sy', 'gx'), 0, 0, tiled=True)]
    pallas_call x1, Pallas kernels: 9.81 us -> 2.41 us  [pick(): pl.pallas_call(pick_kernel, out_shape=jax.ShapeDtypeStruct(stored.shape,...]
    pallas_call x1 -> x4, Pallas kernels: 4.67 us -> 11.5 us  [the longest x2 5.09 us: pack_corners(): pl.pallas_call(functools.partial(corner_kernel, block_y, parity_y), out_s...]
    all_to_all x1, waiting for transfers between devices: 5.36 us -> 0.01 us  [local(): lax.all_to_all(picked.reshape(model_tiles.shape), ('sy', 'gx'), 0, 0, til...]
    another operation x7 -> x1, other arithmetic: 4.86 us -> 0.66 us  [local(): places = jnp.stack([column, row, jnp.int32(nx), core]).astype(jnp.int32)]
    dynamic_slice x11 -> x1, local copies, waits for them, and re-layouts: 3.59 us -> 0.01 us  [local(): part = lax.dynamic_slice_in_dim(speed, start, HALO, axis=1)]
  transfers between devices with their start and end apart: 15 -> 16, of which waited for: 2 -> 3; matrix products, arithmetic and copies ran while one was open for 14% -> 2% of each run, Pallas kernels for 10% -> 12%
where the time goes in v2:
time: 113 us; the launch traced here: 112 us
  starting transfers between devices  36.8 us (33%)
  Pallas kernels  34.4 us (30%)
  blocking collectives  15.8 us (14%)
  waiting for transfers between devices  12.6 us (11%)
  local copies, waits for them, and re-layouts  8.47 us (7%)
  other arithmetic  2.05 us (2%)
  between operations  1.57 us (1%)
    pallas_call x1, Pallas kernels, window(): pl.pallas_call(kernel, out_shape=(jax.ShapeDtypeStruct(now.shape, now.dty...  20.5 us
    all_to_all x1, blocking collectives, local(): gathered = lax.all_to_all(partial, ('gx', 'gy'), 0, 0, tiled=True)  15.8 us
    ppermute x2, waiting for transfers between devices, local(): lax.ppermute(pack_corners(f, places, blocks), 'gy', perm)  10.5 us
    unnamed x37, local copies, waits for them, and re-layouts  7.87 us
    all_to_all x1, starting transfers between devices, local(): spread = lax.all_to_all(model_tiles, ('sy', 'gx'), 0, 0, tiled=True)  7.42 us
    ppermute x2, starting transfers between devices, local(): lax.ppermute(part, ('gx', 'gy'), joint(x_perm, perm, ny))  6.36 us
    ppermute x2, starting transfers between devices, local(): now_x = [lax.ppermute(now, 'gx', perm) for perm in x_perms]  5.44 us
    ppermute x2, starting transfers between devices, local(): speed_x = [lax.ppermute(speed, 'gx', perm) for perm in x_perms]  5.13 us
  transfers between devices with their start and end apart: 16, of which 3 were waited for; matrix products, arithmetic and copies ran while one was open for 2% of the time, Pallas kernels for 12%

profile of v2, /device:TPU:0, one launch (start us, length us, event | category | flops | bytes accessed | tf_op | source)
XLA Modules:
  0.0 111.6 jit_solution(16961506024976024807)
XLA Ops:
  0.6 7.4 %all-to-all-start = ((f32[16,32,128]{2,1,0:T(8,128)}), f32[16,32,128]{2,1,0:T(8,128)S(1)}, u32[]{:S(2)}, u32[]{:S(2)}) async-start(f32[16,32,128]{2,1,0:T(8,128)} %param.8), calls=%async_computation | async-start | bytes 524288 | tf_op jit(solution)/shard_map/all_to_all | solution.py:475
  8.1 0.7 collective-permute-start.2
  8.8 4.7 %collective-permute-start.1 = (f32[2,16,32,128]{3,2,1,0:T(8,128)S(1)}, f32[2,16,32,128]{3,2,1,0:T(8,128)S(1)}, u32[]{:S(2)}, u32[]{:S(2)}) collective-permute-start(f32[2,16,32,128]{3,2,1,0:T(8,128)S(1)} %bitcast.35), channel_id=1, source_target_pairs={{0,2},{2,0},{4,6},{6,4},{1,3},{3,1},{5,7},{7,5},{8,10},{10,8},{12,... | collective-permute-start | bytes 1572872 | tf_op jit(solution)/shard_map/ppermute | solution.py:474
  13.5 0.7 collective-permute-start.4
  14.2 1.9 %collective-permute-start.3 = (f32[2,16,32,128]{3,2,1,0:T(8,128)}, f32[2,16,32,128]{3,2,1,0:T(8,128)S(1)}, u32[]{:S(2)}, u32[]{:S(2)}) collective-permute-start(f32[2,16,32,128]{3,2,1,0:T(8,128)} %bitcast.38), channel_id=1, source_target_pairs={{0,2},{2,0},{4,6},{6,4},{1,3},{3,1},{5,7},{7,5},{8,10},{10,8},{12,... | collective-permute-start | bytes 1572872 | tf_op jit(solution)/shard_map/ppermute | solution.py:477
  16.1 1.5 %collective-permute-start = (s32[1]{0:T(128)}, s32[1]{0:T(128)}, u32[]{:S(2)}, u32[]{:S(2)}) collective-permute-start(s32[1]{0:T(128)} %param.10), channel_id=1, source_target_pairs={{0,16},{16,0},{1,17},{17,1},{2,18},{18,2},{3,19},{19,3},{4,20},{20... | collective-permute-start | bytes 20 | tf_op jit(solution)/shard_map/ppermute | solution.py:490
  18.2 0.7 copy-done.17
  20.3 0.7 compare_select_fusion.1
  21.6 3.9 %prepare_lists.1 = (s32[8]{0:T(128)}, s32[788]{0:T(1024)}) custom-call(s32[4]{0:T(128)} %pad_add_fusion.places.starts, s32[16]{0:T(128)} %owner_map.1, s32[8]{0:T(128)} %add.34.shifts, s32[3,256]{1,0:T(4,128)} %bitcast.51), custom_call_target="tpu_custom_call" | custom-call | tf_op jit(solution)/shard_map/prepare_lists/pallas_call | solution.py:70
  25.6 0.7 copy-done.16
  26.2 2.4 %pick_slices.1 = f32[8,2,32,128]{3,2,1,0:T(8,128)} custom-call(s32[8]{0:T(128)} %get-tuple-element.9.stored_in, s32[4]{0:T(128)} %pad_add_fusion.places.starts, f32[8,2,32,128]{3,2,1,0:T(8,128)} %bitcast.45, f32[8,2,32,128]{3,2,1,0:T(8,128)} %bitcast.47), custom_call_target="tpu_custom_call" | custom-call | tf_op jit(solution)/shard_map/pick_slices/pallas_call | solution.py:101
  28.7 4.0 %all-to-all-start.1 = ((f32[16,32,128]{2,1,0:T(8,128)}), f32[16,32,128]{2,1,0:T(8,128)S(1)}, u32[]{:S(2)}, u32[]{:S(2)}) async-start(f32[16,32,128]{2,1,0:T(8,128)} %bitcast.46), calls=%async_computation.1 | async-start | bytes 524288 | tf_op jit(solution)/shard_map/all_to_all | solution.py:500
  32.7 2.5 %pack_sides.1 = f32[2,2,16,16,128]{4,3,2,1,0:T(8,128)} custom-call(s32[4]{0:T(128)} %pad_add_fusion.places.starts, f32[2,16,32,128]{3,2,1,0:T(8,128)} %bitcast.33, f32[2,16,32,128]{3,2,1,0:T(8,128)} %bitcast.39), custom_call_target="tpu_custom_call" | custom-call | tf_op jit(solution)/shard_map/pack_sides/pallas_call | solution.py:167
  35.2 1.6 %collective-permute-start.5 = (f32[2,2,16,16,128]{4,3,2,1,0:T(8,128)}, f32[2,2,16,16,128]{4,3,2,1,0:T(8,128)}, u32[]{:S(2)}, u32[]{:S(2)}) collective-permute-start(f32[2,2,16,16,128]{4,3,2,1,0:T(8,128)} %pack_sides.1), channel_id=1, source_target_pairs={{0,1},{1,0},{2,3},{3,2},{4,5},{5,4},{6,7},{7,6},{8,9},{9,8},{10,11... | collective-permute-start | bytes 1572872 | tf_op jit(solution)/shard_map/ppermute | solution.py:479
  36.8 0.8 copy-done.3
  37.5 0.8 copy-done.5
  38.3 2.5 %pack_corners.2 = f32[2,2,8,24,128]{4,3,2,1,0:T(8,128)} custom-call(s32[4]{0:T(128)} %pad_add_fusion.places.starts, f32[2,16,32,128]{3,2,1,0:T(8,128)} %copy-done.5, f32[2,16,32,128]{3,2,1,0:T(8,128)} %copy-done.3), custom_call_target="tpu_custom_call" | custom-call | tf_op jit(solution)/shard_map/pack_corners/pallas_call | solution.py:143
  41.4 0.8 copy-done.7
  42.2 0.8 copy-done.9
  43.0 2.6 %pack_corners.3 = f32[2,2,8,24,128]{4,3,2,1,0:T(8,128)} custom-call(s32[4]{0:T(128)} %pad_add_fusion.places.starts, f32[2,16,32,128]{3,2,1,0:T(8,128)} %copy-done.9, f32[2,16,32,128]{3,2,1,0:T(8,128)} %copy-done.7), custom_call_target="tpu_custom_call" | custom-call | tf_op jit(solution)/shard_map/pack_corners/pallas_call | solution.py:143
  45.7 1.6 %collective-permute-start.7 = (f32[2,2,8,24,128]{4,3,2,1,0:T(8,128)}, f32[2,2,8,24,128]{4,3,2,1,0:T(8,128)S(1)}, u32[]{:S(2)}, u32[]{:S(2)}) collective-permute-start(f32[2,2,8,24,128]{4,3,2,1,0:T(8,128)} %pack_corners.3), channel_id=1, source_target_pairs={{0,1},{1,0},{2,3},{3,2},{4,5},{5,4},{6,7},{7,6},{8,9},{9,8},{10,11... | collective-permute-start | bytes 1179656 | tf_op jit(solution)/shard_map/ppermute | solution.py:483
  47.2 0.7 collective-permute-start.13
  47.9 5.7 %collective-permute-start.12 = (f32[16,16,128]{2,1,0:T(8,128)S(1)}, f32[16,16,128]{2,1,0:T(8,128)S(1)}, u32[]{:S(2)}, u32[]{:S(2)}) collective-permute-start(f32[16,16,128]{2,1,0:T(8,128)S(1)} %constant_dynamic-slice_fusion), channel_id=1, source_target_pairs={{0,3},{1,2},{2,1},{3,0},{4,7},{5,6},{6,5},{7,4},{8,11},{9,10},{10,... | collective-permute-start | bytes 393224 | tf_op jit(solution)/shard_map/ppermute | solution.py:508
  53.6 0.7 collective-permute-start.10
  54.3 4.5 %collective-permute-start.9 = (f32[16,32,128]{2,1,0:T(8,128)S(1)}, f32[16,32,128]{2,1,0:T(8,128)S(1)}, u32[]{:S(2)}, u32[]{:S(2)}) collective-permute-start(f32[16,32,128]{2,1,0:T(8,128)S(1)} %all-to-all-done.1.speed), channel_id=1, source_target_pairs={{0,2},{2,0},{4,6},{6,4},{1,3},{3,1},{5,7},{7,5},{8,10},{10,8},{12,... | collective-permute-start | bytes 786440 | tf_op jit(solution)/shard_map/ppermute | solution.py:501
  59.4 2.1 %collective-permute-done.6 = f32[2,2,8,24,128]{4,3,2,1,0:T(8,128)} collective-permute-done((f32[2,2,8,24,128]{4,3,2,1,0:T(8,128)}, f32[2,2,8,24,128]{4,3,2,1,0:T(8,128)}, u32[]{:S(2)}, u32[]{:S(2)}) %collective-permute-start.6) | collective-permute-done | bytes 393248 | tf_op jit(solution)/shard_map/ppermute | solution.py:483
  61.6 8.3 %collective-permute-done.7 = f32[2,2,8,24,128]{4,3,2,1,0:T(8,128)S(1)} collective-permute-done((f32[2,2,8,24,128]{4,3,2,1,0:T(8,128)}, f32[2,2,8,24,128]{4,3,2,1,0:T(8,128)S(1)}, u32[]{:S(2)}, u32[]{:S(2)}) %collective-permute-start.7) | collective-permute-done | bytes 393248 | tf_op jit(solution)/shard_map/ppermute | solution.py:483
  69.9 2.1 %collective-permute-done.11 = f32[16,16,128]{2,1,0:T(8,128)S(1)} collective-permute-done((f32[16,16,128]{2,1,0:T(8,128)S(1)}, f32[16,16,128]{2,1,0:T(8,128)S(1)}, u32[]{:S(2)}, u32[]{:S(2)}) %collective-permute-start.11) | collective-permute-done | bytes 131104 | tf_op jit(solution)/shard_map/ppermute | solution.py:506
  72.7 1.0 copy-done.8
  73.7 1.0 copy-done.10
  74.8 20.5 %wave_window.1 = (f32[2,16,32,128]{3,2,1,0:T(8,128)}, f32[2,16,32,128]{3,2,1,0:T(8,128)}, f32[8,16,256]{2,1,0:T(8,128)S(1)}) custom-call(s32[4]{0:T(128)S(1)} %copy-done.11, s32[2,3]{1,0:T(2,128)S(1)} %bitcast.43, f32[2,8]{1,0:T(2,128)S(1)} %bitcast.44, s32[788]{0:T(1024)S(1)} %copy-done.12, f32[2,16,32,128]{3,2,1,0:T(8,128)S(1)} %bitcast.36, ...), custom_call_target="tpu_custom_call" | custom-call | tf_op jit(solution)/shard_map/wave_window/pallas_call | solution.py:440
  95.3 15.8 %all_to_all.15 = f32[8,16,256]{2,1,0:T(8,128)S(1)} all-to-all(f32[8,16,256]{2,1,0:T(8,128)S(1)} %get-tuple-element.12), channel_id=1, replica_groups=mesh['sy'=2,'core'=2,'gx'=4,'gy'=2] {'gx','gy'}, dimensions={0} | all-to-all | bytes 262144 | tf_op jit(solution)/shard_map/all_to_all | solution.py:517
  (51 shorter events, 4.6 us)
Async XLA Ops:
  0.6 7.4 %copy-start = (f32[1,2,16,32,128]{4,3,2,1,0:T(8,128)S(1)}, f32[1,2,16,32,128]{4,3,2,1,0:T(8,128)}, u32[]{:S(2)}) copy-start(f32[1,2,16,32,128]{4,3,2,1,0:T(8,128)} %param.11) | copy-start | bytes 1572868
  0.6 19.5 %all-to-all-start = ((f32[16,32,128]{2,1,0:T(8,128)}), f32[16,32,128]{2,1,0:T(8,128)S(1)}, u32[]{:S(2)}, u32[]{:S(2)}) async-start(f32[16,32,128]{2,1,0:T(8,128)} %param.8), calls=%async_computation | async-start | bytes 524288 | tf_op jit(solution)/shard_map/all_to_all | solution.py:475
  8.1 28.7 %collective-permute-start.2 = (f32[2,16,32,128]{3,2,1,0:T(8,128)S(1)}, f32[2,16,32,128]{3,2,1,0:T(8,128)S(1)}, u32[]{:S(2)}, u32[]{:S(2)}) collective-permute-start(f32[2,16,32,128]{3,2,1,0:T(8,128)S(1)} %bitcast.34), channel_id=1, source_target_pairs={{2,4},{4,2},{3,5},{5,3},{10,12},{12,10},{11,13},{13,11},{18,20},{2... | collective-permute-start | bytes 1572872 | tf_op jit(solution)/shard_map/ppermute | solution.py:474
  8.8 28.0 %collective-permute-start.1 = (f32[2,16,32,128]{3,2,1,0:T(8,128)S(1)}, f32[2,16,32,128]{3,2,1,0:T(8,128)S(1)}, u32[]{:S(2)}, u32[]{:S(2)}) collective-permute-start(f32[2,16,32,128]{3,2,1,0:T(8,128)S(1)} %bitcast.35), channel_id=1, source_target_pairs={{0,2},{2,0},{4,6},{6,4},{1,3},{3,1},{5,7},{7,5},{8,10},{10,8},{12,... | collective-permute-start | bytes 1572872 | tf_op jit(solution)/shard_map/ppermute | solution.py:474
  13.5 27.9 %collective-permute-start.4 = (f32[2,16,32,128]{3,2,1,0:T(8,128)}, f32[2,16,32,128]{3,2,1,0:T(8,128)S(1)}, u32[]{:S(2)}, u32[]{:S(2)}) collective-permute-start(f32[2,16,32,128]{3,2,1,0:T(8,128)} %bitcast.37), channel_id=1, source_target_pairs={{2,4},{4,2},{3,5},{5,3},{10,12},{12,10},{11,13},{13,11},{18,20},{2... | collective-permute-start | bytes 1572872 | tf_op jit(solution)/shard_map/ppermute | solution.py:477
  14.2 27.2 %collective-permute-start.3 = (f32[2,16,32,128]{3,2,1,0:T(8,128)}, f32[2,16,32,128]{3,2,1,0:T(8,128)S(1)}, u32[]{:S(2)}, u32[]{:S(2)}) collective-permute-start(f32[2,16,32,128]{3,2,1,0:T(8,128)} %bitcast.38), channel_id=1, source_target_pairs={{0,2},{2,0},{4,6},{6,4},{1,3},{3,1},{5,7},{7,5},{8,10},{10,8},{12,... | collective-permute-start | bytes 1572872 | tf_op jit(solution)/shard_map/ppermute | solution.py:477
  16.1 4.1 %collective-permute-start = (s32[1]{0:T(128)}, s32[1]{0:T(128)}, u32[]{:S(2)}, u32[]{:S(2)}) collective-permute-start(s32[1]{0:T(128)} %param.10), channel_id=1, source_target_pairs={{0,16},{16,0},{1,17},{17,1},{2,18},{18,2},{3,19},{19,3},{4,20},{20... | collective-permute-start | bytes 20 | tf_op jit(solution)/shard_map/ppermute | solution.py:490
  18.2 0.7 copy-start.17
  20.2 5.4 %copy-start.15 = (f32[16,32,128]{2,1,0:T(8,128)}, f32[16,32,128]{2,1,0:T(8,128)S(1)}, u32[]{:S(2)}) copy-start(f32[16,32,128]{2,1,0:T(8,128)S(1)} %all-to-all-done) | copy-start | bytes 786436
  20.2 5.3 %collective-permute-start.8 = (f32[16,32,128]{2,1,0:T(8,128)S(1)}, f32[16,32,128]{2,1,0:T(8,128)S(1)}, u32[]{:S(2)}, u32[]{:S(2)}) collective-permute-start(f32[16,32,128]{2,1,0:T(8,128)S(1)} %all-to-all-done), channel_id=1, source_target_pairs={{0,8},{8,0},{1,9},{9,1},{2,10},{10,2},{3,11},{11,3},{4,12},{12,4},... | collective-permute-start | bytes 786440 | tf_op jit(solution)/shard_map/ppermute | solution.py:476
  25.5 0.7 copy-start.16
  28.7 18.5 %all-to-all-start.1 = ((f32[16,32,128]{2,1,0:T(8,128)}), f32[16,32,128]{2,1,0:T(8,128)S(1)}, u32[]{:S(2)}, u32[]{:S(2)}) async-start(f32[16,32,128]{2,1,0:T(8,128)} %bitcast.46), calls=%async_computation.1 | async-start | bytes 524288 | tf_op jit(solution)/shard_map/all_to_all | solution.py:500
  35.2 18.4 %collective-permute-start.5 = (f32[2,2,16,16,128]{4,3,2,1,0:T(8,128)}, f32[2,2,16,16,128]{4,3,2,1,0:T(8,128)}, u32[]{:S(2)}, u32[]{:S(2)}) collective-permute-start(f32[2,2,16,16,128]{4,3,2,1,0:T(8,128)} %pack_sides.1), channel_id=1, source_target_pairs={{0,1},{1,0},{2,3},{3,2},{4,5},{5,4},{6,7},{7,6},{8,9},{9,8},{10,11... | collective-permute-start | bytes 1572872 | tf_op jit(solution)/shard_map/ppermute | solution.py:479
  36.7 0.8 copy-start.3
  37.5 0.8 copy-start.5
  40.8 20.7 %collective-permute-start.6 = (f32[2,2,8,24,128]{4,3,2,1,0:T(8,128)}, f32[2,2,8,24,128]{4,3,2,1,0:T(8,128)}, u32[]{:S(2)}, u32[]{:S(2)}) collective-permute-start(f32[2,2,8,24,128]{4,3,2,1,0:T(8,128)} %pack_corners.2), channel_id=1, source_target_pairs={{0,1},{1,0},{2,3},{3,2},{4,5},{5,4},{6,7},{7,6},{8,9},{9,8},{10,11... | collective-permute-start | bytes 1179656 | tf_op jit(solution)/shard_map/ppermute | solution.py:483
  41.4 0.8 copy-start.7
  42.2 0.8 copy-start.9
  43.0 29.0 %copy-start.2 = (f32[1,2,16,32,128]{4,3,2,1,0:T(8,128)S(1)}, f32[1,2,16,32,128]{4,3,2,1,0:T(8,128)}, u32[]{:S(2)}) copy-start(f32[1,2,16,32,128]{4,3,2,1,0:T(8,128)} %param.12) | copy-start | bytes 1572868
  43.0 29.0 %copy-start.4 = (f32[2,16,32,128]{3,2,1,0:T(8,128)S(1)}, f32[2,16,32,128]{3,2,1,0:T(8,128)}, u32[]{:S(2)}) copy-start(f32[2,16,32,128]{3,2,1,0:T(8,128)} %copy-done.3) | copy-start | bytes 1572868
  43.0 29.0 %copy-start.6 = (f32[2,16,32,128]{3,2,1,0:T(8,128)S(1)}, f32[2,16,32,128]{3,2,1,0:T(8,128)}, u32[]{:S(2)}) copy-start(f32[2,16,32,128]{3,2,1,0:T(8,128)} %copy-done.5) | copy-start | bytes 1572868
  45.6 26.4 %copy-start.1 = (f32[1,2,16,32,128]{4,3,2,1,0:T(8,128)S(1)}, f32[1,2,16,32,128]{4,3,2,1,0:T(8,128)}, u32[]{:S(2)}) copy-start(f32[1,2,16,32,128]{4,3,2,1,0:T(8,128)} %param.11) | copy-start | bytes 1572868
  45.7 24.2 %collective-permute-start.7 = (f32[2,2,8,24,128]{4,3,2,1,0:T(8,128)}, f32[2,2,8,24,128]{4,3,2,1,0:T(8,128)S(1)}, u32[]{:S(2)}, u32[]{:S(2)}) collective-permute-start(f32[2,2,8,24,128]{4,3,2,1,0:T(8,128)} %pack_corners.3), channel_id=1, source_target_pairs={{0,1},{1,0},{2,3},{3,2},{4,5},{5,4},{6,7},{7,6},{8,9},{9,8},{10,11... | collective-permute-start | bytes 1179656 | tf_op jit(solution)/shard_map/ppermute | solution.py:483
  47.2 7.0 %collective-permute-start.13 = (f32[16,16,128]{2,1,0:T(8,128)S(1)}, f32[16,16,128]{2,1,0:T(8,128)S(1)}, u32[]{:S(2)}, u32[]{:S(2)}) collective-permute-start(f32[16,16,128]{2,1,0:T(8,128)S(1)} %constant_dynamic-slice_fusion), channel_id=1, source_target_pairs={{2,5},{3,4},{4,3},{5,2},{10,13},{11,12},{12,11},{13,10},{18,21},{1... | collective-permute-start | bytes 393224 | tf_op jit(solution)/shard_map/ppermute | solution.py:508
  47.9 10.8 %collective-permute-start.12 = (f32[16,16,128]{2,1,0:T(8,128)S(1)}, f32[16,16,128]{2,1,0:T(8,128)S(1)}, u32[]{:S(2)}, u32[]{:S(2)}) collective-permute-start(f32[16,16,128]{2,1,0:T(8,128)S(1)} %constant_dynamic-slice_fusion), channel_id=1, source_target_pairs={{0,3},{1,2},{2,1},{3,0},{4,7},{5,6},{6,5},{7,4},{8,11},{9,10},{10,... | collective-permute-start | bytes 393224 | tf_op jit(solution)/shard_map/ppermute | solution.py:508
  53.6 18.4 %collective-permute-start.10 = (f32[16,32,128]{2,1,0:T(8,128)S(1)}, f32[16,32,128]{2,1,0:T(8,128)S(1)}, u32[]{:S(2)}, u32[]{:S(2)}) collective-permute-start(f32[16,32,128]{2,1,0:T(8,128)S(1)} %all-to-all-done.1.speed), channel_id=1, source_target_pairs={{2,4},{4,2},{3,5},{5,3},{10,12},{12,10},{11,13},{13,11},{18,20},{2... | collective-permute-start | bytes 786440 | tf_op jit(solution)/shard_map/ppermute | solution.py:501
  54.3 17.7 %collective-permute-start.9 = (f32[16,32,128]{2,1,0:T(8,128)S(1)}, f32[16,32,128]{2,1,0:T(8,128)S(1)}, u32[]{:S(2)}, u32[]{:S(2)}) collective-permute-start(f32[16,32,128]{2,1,0:T(8,128)S(1)} %all-to-all-done.1.speed), channel_id=1, source_target_pairs={{0,2},{2,0},{4,6},{6,4},{1,3},{3,1},{5,7},{7,5},{8,10},{10,8},{12,... | collective-permute-start | bytes 786440 | tf_op jit(solution)/shard_map/ppermute | solution.py:501
  58.7 13.2 %collective-permute-start.11 = (f32[16,16,128]{2,1,0:T(8,128)S(1)}, f32[16,16,128]{2,1,0:T(8,128)S(1)}, u32[]{:S(2)}, u32[]{:S(2)}) collective-permute-start(f32[16,16,128]{2,1,0:T(8,128)S(1)} %constant_dynamic-slice_fusion), channel_id=1, source_target_pairs={{0,1},{1,0},{2,3},{3,2},{4,5},{5,4},{6,7},{7,6},{8,9},{9,8},{10,11... | collective-permute-start | bytes 393224 | tf_op jit(solution)/shard_map/ppermute | solution.py:506
  59.4 12.7 %copy-start.14 = (f32[1,2,8]{2,1,0:T(2,128)S(1)}, f32[1,2,8]{2,1,0:T(2,128)}, u32[]{:S(2)}) copy-start(f32[1,2,8]{2,1,0:T(2,128)} %param.14) | copy-start | bytes 196
  72.0 0.7 copy-start.13
  72.7 1.0 copy-start.8
  73.7 1.0 copy-start.10
  (2 other events, 1.4 us)

commit v3 on v2

--- a/solution.py
+++ b/solution.py
@@ -11,6 +11,9 @@
 STEPS = 8
 HALO = 2 * STEPS
 PAD = 8
+HALF = HALO // 2
+REACH_NOW = (HALF - 1, HALF)
+REACH_PREV = (HALF - 3, HALF)
 GROUP = 4
 BATCH = 4
 
@@ -36,12 +39,8 @@
     return [(a * count + b, c * count + d) for a, c in first for b, d in second]
 
 
-def prepare_kernel(block_x, block_y, places, owner_map, shifts, receivers, stored_in, local_list):
-    column, row, across = places[0], places[1], places[2]
-    targets = stored_in.shape[0]
-    for t in range(targets):
-        stored_in[t] = owner_map[shifts[t]]
-    x_first, y_first = column * block_x, row * block_y
+def list_kernel(block_x, block_y, receivers, local_list):
+    x_first, y_first = lax.axis_index("gx") * block_x, lax.axis_index("gy") * block_y
     total = receivers.shape[1]
     batch = 8
 
@@ -65,93 +64,97 @@
         local_list[3 + 3 * (count + i)] = 0
 
 
-def prepare(block_x, block_y, places, owner_map, shifts, receivers):
+def list_receivers(block_x, block_y, receivers):
     total = receivers.shape[1]
     return pl.pallas_call(
-        functools.partial(prepare_kernel, block_x, block_y),
-        out_shape=(
-            jax.ShapeDtypeStruct(shifts.shape, jnp.int32),
-            jax.ShapeDtypeStruct((3 * (total + BATCH) + 8,), jnp.int32),
-        ),
-        in_specs=[SMEM] * 4,
-        out_specs=(SMEM, SMEM),
-        name="prepare_lists",
-    )(places, owner_map, shifts, receivers)
-
-
-def pick_kernel(stored_in, places, stored, other, out, sems):
-    targets = out.shape[0]
-    across, core = places[2], places[3]
+        functools.partial(list_kernel, block_x, block_y),
+        out_shape=jax.ShapeDtypeStruct((3 * (total + BATCH) + 8,), jnp.int32),
+        in_specs=[SMEM],
+        out_specs=SMEM,
+        name="list_receivers",
+    )(receivers)
+
+
+def pick_kernel(across, groups, owner_map, *refs):
+    shifts, (stored, other, out, sems) = refs[:groups], refs[groups:]
+    core, mine = lax.axis_index("core"), lax.axis_index("sy")
     copies = []
-    for t in range(targets):
-        block = stored_in[t]
-        owner_core = (block // across) % 2
-        row = (block // (2 * across)) * across + block % across
-        here = pltpu.make_async_copy(stored.at[row], out.at[t], sems.at[t])
-        there = pltpu.make_async_copy(other.at[row], out.at[t], sems.at[t])
-        pl.when(owner_core == core)(here.start)
-        pl.when(owner_core != core)(there.start)
-        copies.append(here)
+    for turn in range(groups):
+        group = lax.rem(mine + groups - turn, groups)
+        for z in range(across):
+            block = owner_map[shifts[turn][0] + z]
+            owner_core = lax.rem(block // across, 2)
+            row = (block // (2 * across)) * across + lax.rem(block, across)
+            t = group * across + z
+            here = pltpu.make_async_copy(stored.at[row], out.at[t], sems.at[len(copies)])
+            there = pltpu.make_async_copy(other.at[row], out.at[t], sems.at[len(copies)])
+            pl.when(owner_core == core)(here.start)
+            pl.when(owner_core != core)(there.start)
+            copies.append(here)
     for copy in copies:
         copy.wait()
 
 
-def pick(stored_in, places, stored, other):
+def pick(across, shifts, owner_map, stored, other):
     targets = stored.shape[0]
     return pl.pallas_call(
-        pick_kernel,
+        functools.partial(pick_kernel, across, len(shifts)),
         out_shape=jax.ShapeDtypeStruct(stored.shape, stored.dtype),
-        in_specs=[SMEM, SMEM, ANY, ANY],
+        in_specs=[SMEM] * (1 + len(shifts)) + [ANY, ANY],
         out_specs=VMEM,
         scratch_shapes=[pltpu.SemaphoreType.DMA((targets,))],
         name="pick_slices",
-    )(stored_in, places, stored, other)
-
-
-def corner_kernel(block_y, parity_y, places, first, second, out, sems):
-    half = HALO // 2
-    odd_x, odd_y = places[0] % 2, places[1] % 2
+    )(owner_map, *shifts, stored, other)
+
+
+def corner_kernel(block_y, parity_y, reach, first, second, out, sems):
+    near, far = reach
+    block_x = first.shape[1]
+    odd_x, odd_y = lax.rem(lax.axis_index("gx"), 2), lax.rem(lax.axis_index("gy"), 2)
     above = odd_y == parity_y
     start = pl.multiple_of(jnp.where(above, block_y - HALO, 0), 8)
-    near_start = pl.multiple_of(jnp.where(above, block_y - half, 0), 8)
+    near_start = pl.multiple_of(jnp.where(above, block_y - HALF, 0), 8)
     copies = []
     for e, block in enumerate((first, second)):
-        near = jnp.where(odd_x == e, 0, half)
+        high = odd_x == e
         copies.append(
             pltpu.make_async_copy(
-                block.at[:, pl.ds(near, half), pl.ds(start, HALO)],
-                out.at[e, :, :, pl.ds(0, HALO)],
+                block.at[:, pl.ds(jnp.where(high, 0, block_x - near), near), pl.ds(start, HALO)],
+                out.at[e, :, pl.ds(0, near)],
                 sems.at[2 * e],
             )
         )
-        copies.append(
-            pltpu.make_async_copy(
-                block.at[:, pl.ds(half - near, half), pl.ds(near_start, half)],
-                out.at[e, :, :, pl.ds(HALO, half)],
-                sems.at[2 * e + 1],
+        for k in range(2):
+            first_plane = jnp.where(high, near, block_x - near - far) + k * (far // 2)
+            copies.append(
+                pltpu.make_async_copy(
+                    block.at[:, pl.ds(first_plane, far // 2), pl.ds(near_start, HALF)],
+                    out.at[e, :, pl.ds(near, far // 2), pl.ds(k * HALF, HALF)],
+                    sems.at[4 + 2 * e + k],
+                )
             )
-        )
     for copy in copies:
         copy.start()
     for copy in copies:
         copy.wait()
 
 
-def pack_corners(parity_y, places, blocks):
+def pack_corners(parity_y, reach, blocks):
     shots, _, block_y, depth = blocks[0].shape
-    half = HALO // 2
+    near, far = reach
     return pl.pallas_call(
-        functools.partial(corner_kernel, block_y, parity_y),
-        out_shape=jax.ShapeDtypeStruct((2, shots, half, HALO + half, depth), jnp.float32),
-        in_specs=[SMEM, ANY, ANY],
+        functools.partial(corner_kernel, block_y, parity_y, reach),
+        out_shape=jax.ShapeDtypeStruct((2, shots, near + far // 2, HALO, depth), jnp.float32),
+        in_specs=[ANY, ANY],
         out_specs=VMEM,
-        scratch_shapes=[pltpu.SemaphoreType.DMA((4,))],
+        scratch_shapes=[pltpu.SemaphoreType.DMA((8,))],
         name="pack_corners",
-    )(places, *blocks)
-
-
-def side_kernel(block_y, parity_y, places, now, prev, out, sems):
-    start = pl.multiple_of(jnp.where(places[1] % 2 == parity_y, block_y - HALO, 0), 8)
+    )(*blocks)
+
+
+def side_kernel(block_y, parity_y, now, prev, out, sems):
+    above = lax.rem(lax.axis_index("gy"), 2) == parity_y
+    start = pl.multiple_of(jnp.where(above, block_y - HALO, 0), 8)
     copies = [
         pltpu.make_async_copy(block.at[:, :, pl.ds(start, HALO)], out.at[k], sems.at[k])
         for k, block in enumerate((now, prev))
@@ -162,21 +165,20 @@
         copy.wait()
 
 
-def pack_sides(parity_y, places, now, prev):
+def pack_sides(parity_y, now, prev):
     shots, block_x, block_y, depth = now.shape
     return pl.pallas_call(
         functools.partial(side_kernel, block_y, parity_y),
         out_shape=jax.ShapeDtypeStruct((2, shots, block_x, HALO, depth), jnp.float32),
-        in_specs=[SMEM, ANY, ANY],
+        in_specs=[ANY, ANY],
         out_specs=VMEM,
         scratch_shapes=[pltpu.SemaphoreType.DMA((2,))],
         name="pack_sides",
-    )(places, now, prev)
+    )(now, prev)
 
 
 def window_kernel(
     sizes,
-    starts,
     sources,
     amplitudes,
     local_list,
@@ -206,8 +208,8 @@
     rows = now_ext.shape[2]
     planes = now_ext.shape[1]
     shots = now_ext.shape[0]
-    column, row = starts[0], starts[1]
-    odd_x, odd_y = column % 2, row % 2
+    column, row = lax.axis_index("gx"), lax.axis_index("gy")
+    odd_x, odd_y = lax.rem(column, 2), lax.rem(row, 2)
     own = pl.multiple_of(PAD + (HALO * odd_y if ny == 2 else HALO), 8)
     high_x = [odd_x == 0, odd_x == 1]
     high_y = [odd_y == 0, odd_y == 1]
@@ -215,15 +217,30 @@
     y_at = [
         pl.multiple_of(jnp.where(h, own + block_y, own - HALO), 8) for h in high_y
     ]
-    near_x = [jnp.where(h, 0, HALO // 2) for h in high_x]
     near_y = [
-        pl.multiple_of(jnp.where(h, own + block_y, own - HALO // 2), 8) for h in high_y
+        pl.multiple_of(jnp.where(h, own + block_y, own - HALF), 8) for h in high_y
     ]
-    far_y = [
-        pl.multiple_of(jnp.where(h, own + block_y + HALO // 2, own - HALO), 8)
-        for h in high_y
-    ]
-    half = HALO // 2
+    y_count = len(speed_y)
+    blank = jnp.zeros((PAD, now_ext.shape[3]), jnp.float32)
+
+    def clear(x, _):
+        for s in range(2 * shots):
+            ext_all[s, x, pl.ds(0, PAD)] = blank
+            ext_all[s, x, pl.ds(rows - PAD, PAD)] = blank
+        return 0
+
+    lax.fori_loop(0, planes, clear, 0)
+    for f in range(y_count):
+        for e in range(2):
+
+            def clear_corner(x, _):
+                for s in range(2 * shots + 1):
+                    for k in range(HALO // PAD):
+                        ext_all[s, x_at[e] + x, pl.ds(y_at[f] + PAD * k, PAD)] = blank
+                return 0
+
+            lax.fori_loop(0, HALO, clear_corner, 0)
+
     copies = []
 
     def fetch(src, dst):
@@ -231,17 +248,27 @@
         copy.start()
         copies.append(copy)
 
-    y_count = speed_y.shape[0]
-    corners = (corners_now, corners_prev)
+
+    def place_corner(ext, packed, reach, e, f):
+        near, far = reach
+        lead = pl.ds(jnp.where(high_x[e], HALO + block_x, HALO - near), near)
+        fetch(packed.at[:, pl.ds(0, near)], ext.at[:, lead, pl.ds(y_at[f], HALO)])
+        for k in range(2):
+            first_plane = jnp.where(high_x[e], HALO + block_x + near, HALO - near - far)
+            fetch(
+                packed.at[:, pl.ds(near, far // 2), pl.ds(k * HALF, HALF)],
+                ext.at[:, pl.ds(first_plane + k * (far // 2), far // 2), pl.ds(near_y[f], HALF)],
+            )
+
     own_rows = pl.ds(own, block_y)
     fetch(speed, near.at[pl.ds(HALO, block_x), own_rows])
     for e in range(2):
         fetch(speed_x[e], near.at[pl.ds(x_at[e], block_x), own_rows])
     for f in range(y_count):
         at = pl.ds(y_at[f], HALO)
-        fetch(speed_y.at[f], near.at[pl.ds(HALO, block_x), at])
+        fetch(speed_y[f], near.at[pl.ds(HALO, block_x), at])
         for e in range(2):
-            fetch(speed_xy.at[f, e], near.at[pl.ds(x_at[e], block_x), at])
+            fetch(speed_xy[2 * f + e], near.at[pl.ds(x_at[e], block_x), at])
     speed_copies = len(copies)
     fetch(now, now_ext.at[:, pl.ds(HALO, block_x), own_rows])
     fetch(prev, prev_ext.at[:, pl.ds(HALO, block_x), own_rows])
@@ -251,39 +278,14 @@
         fetch(prev_x[e], prev_ext.at[:, at, own_rows])
     for f in range(y_count):
         at = pl.ds(y_at[f], HALO)
-        fetch(sides.at[f, 0], now_ext.at[:, pl.ds(HALO, block_x), at])
-        fetch(sides.at[f, 1], prev_ext.at[:, pl.ds(HALO, block_x), at])
+        fetch(sides[f].at[0], now_ext.at[:, pl.ds(HALO, block_x), at])
+        fetch(sides[f].at[1], prev_ext.at[:, pl.ds(HALO, block_x), at])
         for e in range(2):
-            at_near = pl.ds(x_at[e] + near_x[e], half)
-            at_far = pl.ds(x_at[e] + half - near_x[e], half)
-            for k, ext in enumerate((now_ext, prev_ext)):
-                fetch(
-                    corners[k].at[f, e, :, :, pl.ds(0, HALO)],
-                    ext.at[:, at_near, at],
-                )
-                fetch(
-                    corners[k].at[f, e, :, :, pl.ds(HALO, half)],
-                    ext.at[:, at_far, pl.ds(near_y[f], half)],
-                )
-
-    blank = jnp.zeros((PAD, now_ext.shape[3]), jnp.float32)
-    for ext in (now_ext, prev_ext):
-        for s in range(shots):
-
-            def clear(x, _):
-                ext[s, x, pl.ds(0, PAD)] = blank
-                ext[s, x, pl.ds(rows - PAD, PAD)] = blank
-                return 0
-
-            lax.fori_loop(0, planes, clear, 0)
-            for f in range(y_count):
-                for e in range(2):
-
-                    def clear_far(x, _):
-                        ext[s, x_at[e] + half - near_x[e] + x, pl.ds(far_y[f], half)] = blank
-                        return 0
-
-                    lax.fori_loop(0, half, clear_far, 0)
+            for ext, packed, reach in (
+                (now_ext, corners_now, REACH_NOW),
+                (prev_ext, corners_prev, REACH_PREV),
+            ):
+                place_corner(ext, packed[f].at[e], reach, e, f)
 
     def depth_in(cell, total):
         inside = (cell >= 0) & (cell < total)
@@ -425,17 +427,21 @@
     last_out.wait()
 
 
-def window(sizes, starts, sources, amplitudes, local_list, recs, now, prev, now_x, prev_x, sides, corners, speed, speed_x, speed_y, speed_xy, copies):
+def window(sizes, sources, amplitudes, local_list, recs, now, prev, now_x, prev_x, sides, corners, speed, speed_x, speed_y, speed_xy, copies):
     block_x, block_y, total_x, total_y, ny = sizes
     shots, _, _, depth = now.shape
     planes = block_x + 2 * HALO
     rows = block_y + (HALO if ny == 2 else 2 * HALO) + 2 * PAD
 
-    def kernel(starts, sources, amplitudes, local_list, now, prev, n0, n1, p0, p1, sides, corners_now, corners_prev, speed, v0, v1, *rest):
-        window_kernel(
-            sizes, starts, sources, amplitudes, local_list, now, prev,
-            (n0, n1), (p0, p1), sides, corners_now, corners_prev, speed, (v0, v1), *rest,
-        )
+    count = len(speed_y)
+    parts = [now, prev, *now_x, *prev_x, *sides, *corners[0], *corners[1], speed, *speed_x, *speed_y, *speed_xy]
+
+    def kernel(sources, amplitudes, local_list, *refs):
+        groups = []
+        for size in (1, 1, 2, 2, count, count, count, 1, 2, count, 2 * count):
+            groups.append(refs[0] if size == 1 and len(groups) in (0, 1, 7) else refs[:size])
+            refs = refs[size:]
+        window_kernel(sizes, sources, amplitudes, local_list, *groups, *refs)
 
     return pl.pallas_call(
         kernel,
@@ -444,75 +450,71 @@
             jax.ShapeDtypeStruct(now.shape, now.dtype),
             jax.ShapeDtypeStruct((copies, shots * STEPS, recs), now.dtype),
         ),
-        in_specs=[SMEM] * 4 + [ANY] * 14,
+        in_specs=[SMEM] * 3 + [ANY] * len(parts),
         out_specs=(ANY, ANY, VMEM),
         scratch_shapes=[
             pltpu.VMEM((2 * shots + 2, planes, rows, depth), jnp.float32),
             pltpu.VMEM((shots * STEPS, recs + 8, depth), jnp.float32),
-            pltpu.SemaphoreType.DMA((48,)),
+            pltpu.SemaphoreType.DMA((64,)),
             pltpu.SemaphoreType.DMA((2,)),
         ],
         compiler_params=pltpu.CompilerParams(vmem_limit_bytes=40 * 2**20),
         name="wave_window",
     )(
-        starts, sources, amplitudes, local_list, now, prev, *now_x, *prev_x,
-        sides, *corners, speed, *speed_x, speed_y, speed_xy,
+        sources, amplitudes, local_list, *parts
     )
 
 
 def local(model_tiles, owner_map, offsets, field_now, field_prev, sources, wavelet, receivers):
     block_x, block_y, depth = model_tiles.shape
     nx, ny, groups = lax.axis_size("gx"), lax.axis_size("gy"), lax.axis_size("sy")
-    column, row, core = lax.axis_index("gx"), lax.axis_index("gy"), lax.axis_index("core")
-    shot_row = lax.axis_index("sy")
+    row = lax.axis_index("gy")
     total_x, total_y = block_x * nx, block_y * ny
     now, prev = field_now[0], field_prev[0]
     x_perms = [pairs(nx, 0), pairs(nx, 1)]
     y_perms = [pairs(ny, f) for f in range(2 if ny > 2 else 1)]
-    places = jnp.stack([column, row, jnp.int32(nx), core]).astype(jnp.int32)
-
+    spread = lax.all_to_all(model_tiles, ("sy", "gx"), 0, 0, tiled=True)
     now_x = [lax.ppermute(now, "gx", perm) for perm in x_perms]
-    spread = lax.all_to_all(model_tiles, ("sy", "gx"), 0, 0, tiled=True)
+    packed = [pack_sides(f, now, prev) for f in range(len(y_perms))]
+    shifts = [offsets] + [
+        lax.ppermute(offsets, "sy", [(i, (i + turn) % groups) for i in range(groups)])
+        for turn in range(1, groups)
+    ]
+    sides = [lax.ppermute(part, "gy", perm) for part, perm in zip(packed, y_perms)]
+    spread, packed, shifts, later = lax.optimization_barrier((spread, packed, shifts, prev))
     other = lax.ppermute(spread, "core", [(0, 1), (1, 0)])
-    prev_x = [lax.ppermute(prev, "gx", perm) for perm in x_perms]
-    sides = jnp.stack(
-        [lax.ppermute(pack_sides(f, places, now, prev), "gy", perm) for f, perm in enumerate(y_perms)]
-    )
-    corners = [
-        jnp.stack(
-            [lax.ppermute(pack_corners(f, places, blocks), "gy", perm) for f, perm in enumerate(y_perms)]
-        )
-        for blocks in (now_x, prev_x)
-    ]
-
-    shifts = jnp.zeros((groups,), jnp.int32)
-    for turn in range(groups):
-        came = offsets if turn == 0 else lax.ppermute(
-            offsets, "sy", [(i, (i + turn) % groups) for i in range(groups)]
-        )
-        at = (shot_row - turn) % groups
-        shifts = jnp.where(jnp.arange(groups) == at, came, shifts)
-    columns = (shifts[:, None] + jnp.arange(nx, dtype=jnp.int32)[None, :]).reshape(-1)
-    stored_in, local_list = prepare(block_x, block_y, places, owner_map, columns, receivers[0].T)
+    prev_x = [lax.ppermute(later, "gx", perm) for perm in x_perms]
+    local_list = list_receivers(block_x, block_y, receivers[0].T)
+
+    def cut_corners(blocks, reach):
+        return [pack_corners(f, reach, blocks) for f in range(len(y_perms))]
+
+    def swap_corners(packed):
+        return [lax.ppermute(part, "gy", perm) for part, perm in zip(packed, y_perms)]
+
+
     targets = groups * nx
     slice_shape = (targets, block_x // targets, block_y, depth)
-    picked = pick(stored_in, places, spread.reshape(slice_shape), other.reshape(slice_shape))
+    picked = pick(nx, shifts, owner_map, spread.reshape(slice_shape), other.reshape(slice_shape))
+    picked, now_x, sides = lax.optimization_barrier((picked, now_x, sides))
+    cut_now = cut_corners(now_x, REACH_NOW)
+    corners_now = swap_corners(cut_now)
     speed = lax.all_to_all(picked.reshape(model_tiles.shape), ("sy", "gx"), 0, 0, tiled=True)
+    speed, prev_x, corners_now, local_list = lax.optimization_barrier((speed, prev_x, corners_now, local_list))
+    corners = (corners_now, swap_corners(cut_corners(prev_x, REACH_PREV)))
     speed_x = [lax.ppermute(speed, "gx", perm) for perm in x_perms]
     speed_y, speed_xy = [], []
     for f, perm in enumerate(y_perms):
         start = jnp.where(row % 2 == f, block_y - HALO, 0)
         part = lax.dynamic_slice_in_dim(speed, start, HALO, axis=1)
         speed_y.append(lax.ppermute(part, "gy", perm))
-        speed_xy.append(
-            jnp.stack([lax.ppermute(part, ("gx", "gy"), joint(x_perm, perm, ny)) for x_perm in x_perms])
-        )
+        speed_xy += [lax.ppermute(part, ("gx", "gy"), joint(x_perm, perm, ny)) for x_perm in x_perms]
 
     out_now, out_prev, partial = window(
         (block_x, block_y, total_x, total_y, ny),
-        places, sources[0], wavelet[0], local_list, receivers.shape[1],
+        sources[0], wavelet[0], local_list, receivers.shape[1],
         now, prev, now_x, prev_x, sides, corners,
-        speed, speed_x, jnp.stack(speed_y), jnp.stack(speed_xy), nx * ny,
+        speed, speed_x, speed_y, speed_xy, nx * ny,
     )
     gathered = lax.all_to_all(partial, ("gx", "gy"), 0, 0, tiled=True)
     shots = now.shape[0]

time: 113 us -> 98.8 us (0.87)
  starting transfers between devices: 36.8 us -> 31.6 us
  blocking collectives: 15.8 us -> 11.8 us
  local copies, waits for them, and re-layouts: 8.47 us -> 4.76 us
  waiting for transfers between devices: 12.6 us -> 14.7 us
  Pallas kernels: 34.4 us -> 32.7 us
  other arithmetic: 2.05 us -> 0.62 us
    ppermute x5, waiting for transfers between devices: 10.5 us -> 2.82 us  [the longest x2 2.81 us: swap_corners(): lax.ppermute(part, 'gy', perm)]
    ppermute x2, starting transfers between devices: 6.36 us -> 1.09 us  [local(): lax.ppermute(part, ('gx', 'gy'), joint(x_perm, perm, ny))]
    ppermute x2, waiting for transfers between devices: 0.01 us -> 4.66 us  [local(): lax.ppermute(part, ('gx', 'gy'), joint(x_perm, perm, ny))]
    all_to_all x1, blocking collectives: 15.8 us -> 11.8 us  [local(): gathered = lax.all_to_all(partial, ('gx', 'gy'), 0, 0, tiled=True)]
    unnamed x37 -> x33, local copies, waits for them, and re-layouts: 7.87 us -> 4.75 us
    ppermute x1, waiting for transfers between devices: 0.01 us -> 2.31 us  [local(): lax.ppermute(offsets, 'sy', [(i, (i + turn) % groups) for i in range(grou...]
    ppermute x2, waiting for transfers between devices: 0.01 us -> 2.09 us  [local(): now_x = [lax.ppermute(now, 'gx', perm) for perm in x_perms]]
    ppermute x1, waiting for transfers between devices: 2.11 us -> 0.59 us  [local(): speed_y.append(lax.ppermute(part, 'gy', perm))]
  transfers between devices with their start and end apart: 16 -> 16, of which waited for: 3 -> 7; matrix products, arithmetic and copies ran while one was open for 2% -> 1% of each run, Pallas kernels for 12% -> 11%
where the time goes in v3:
time: 98.8 us; the launch traced here: 97.7 us
  Pallas kernels  32.7 us (33%)
  starting transfers between devices  31.6 us (32%)
  waiting for transfers between devices  14.7 us (15%)
  blocking collectives  11.8 us (12%)
  local copies, waits for them, and re-layouts  4.76 us (5%)
  between operations  1.54 us (2%)
    pallas_call x1, Pallas kernels, window(): pl.pallas_call(kernel, out_shape=(jax.ShapeDtypeStruct(now.shape, now.dty...  20.3 us
    all_to_all x1, blocking collectives, local(): gathered = lax.all_to_all(partial, ('gx', 'gy'), 0, 0, tiled=True)  11.8 us
    all_to_all x1, starting transfers between devices, local(): spread = lax.all_to_all(model_tiles, ('sy', 'gx'), 0, 0, tiled=True)  7.29 us
    ppermute x2, starting transfers between devices, local(): speed_x = [lax.ppermute(speed, 'gx', perm) for perm in x_perms]  5.59 us
    ppermute x2, starting transfers between devices, local(): now_x = [lax.ppermute(now, 'gx', perm) for perm in x_perms]  5.43 us
    unnamed x33, local copies, waits for them, and re-layouts  4.75 us
    ppermute x2, waiting for transfers between devices, local(): lax.ppermute(part, ('gx', 'gy'), joint(x_perm, perm, ny))  4.66 us
    all_to_all x1, starting transfers between devices, local(): lax.all_to_all(picked.reshape(model_tiles.shape), ('sy', 'gx'), 0, 0, til...  4.2 us
  transfers between devices with their start and end apart: 16, of which 7 were waited for; matrix products, arithmetic and copies ran while one was open for 1% of the time, Pallas kernels for 11%

profile of v3, /device:TPU:0, one launch (start us, length us, event | category | flops | bytes accessed | tf_op | source)
XLA Modules:
  0.0 97.7 jit_solution(4016362767632581529)
XLA Ops:
  0.6 7.3 %all-to-all-start = ((f32[16,32,128]{2,1,0:T(8,128)}), f32[16,32,128]{2,1,0:T(8,128)S(1)}, u32[]{:S(2)}, u32[]{:S(2)}) async-start(f32[16,32,128]{2,1,0:T(8,128)} %param.8), calls=%async_computation | async-start | bytes 524288 | tf_op jit(solution)/shard_map/all_to_all | solution.py:476
  7.9 1.9 %pack_sides.1 = f32[2,2,16,16,128]{4,3,2,1,0:T(8,128)} custom-call(f32[2,16,32,128]{3,2,1,0:T(8,128)} %bitcast.19, f32[2,16,32,128]{3,2,1,0:T(8,128)} %bitcast.23), custom_call_target="tpu_custom_call" | custom-call | tf_op jit(solution)/shard_map/pack_sides/pallas_call | solution.py:170
  9.9 1.6 %collective-permute-start.4 = (f32[2,2,16,16,128]{4,3,2,1,0:T(8,128)}, f32[2,2,16,16,128]{4,3,2,1,0:T(8,128)}, u32[]{:S(2)}, u32[]{:S(2)}) collective-permute-start(f32[2,2,16,16,128]{4,3,2,1,0:T(8,128)} %pack_sides.1), channel_id=1, source_target_pairs={{0,1},{1,0},{2,3},{3,2},{4,5},{5,4},{6,7},{7,6},{8,9},{9,8},{10,11... | collective-permute-start | bytes 1572872 | tf_op jit(solution)/shard_map/ppermute | solution.py:483
  11.4 0.7 collective-permute-start.3
  12.1 4.7 %collective-permute-start.2 = (f32[2,16,32,128]{3,2,1,0:T(8,128)S(1)}, f32[2,16,32,128]{3,2,1,0:T(8,128)S(1)}, u32[]{:S(2)}, u32[]{:S(2)}) collective-permute-start(f32[2,16,32,128]{3,2,1,0:T(8,128)S(1)} %bitcast.21), channel_id=1, source_target_pairs={{0,2},{2,0},{4,6},{6,4},{1,3},{3,1},{5,7},{7,5},{8,10},{10,8},{12,... | collective-permute-start | bytes 1572872 | tf_op jit(solution)/shard_map/ppermute | solution.py:477
  16.9 1.5 %collective-permute-start = (s32[1]{0:T(128)}, s32[1]{0:T(128)}, u32[]{:S(2)}, u32[]{:S(2)}) collective-permute-start(s32[1]{0:T(128)} %param.10), channel_id=1, source_target_pairs={{0,16},{16,0},{1,17},{17,1},{2,18},{18,2},{3,19},{19,3},{4,20},{20... | collective-permute-start | bytes 20 | tf_op jit(solution)/shard_map/ppermute | solution.py:480
  18.3 2.3 %collective-permute-done.refs_1_ = s32[1]{0:T(128)} collective-permute-done((s32[1]{0:T(128)}, s32[1]{0:T(128)}, u32[]{:S(2)}, u32[]{:S(2)}) %collective-permute-start) | collective-permute-done | bytes 36 | tf_op jit(solution)/shard_map/ppermute | solution.py:480
  20.7 0.7 collective-permute-start.6
  21.4 0.8 collective-permute-done.1
  22.2 0.7 copy-done.14
  22.9 1.0 %collective-permute-start.5 = (f32[2,16,32,128]{3,2,1,0:T(8,128)S(1)}, f32[2,16,32,128]{3,2,1,0:T(8,128)S(1)}, u32[]{:S(2)}, u32[]{:S(2)}) collective-permute-start(f32[2,16,32,128]{3,2,1,0:T(8,128)S(1)} %bitcast.25), channel_id=1, source_target_pairs={{0,2},{2,0},{4,6},{6,4},{1,3},{3,1},{5,7},{7,5},{8,10},{10,8},{12,... | collective-permute-start | bytes 1572872 | tf_op jit(solution)/shard_map/ppermute | solution.py:486
  24.6 3.0 %pick_slices.1 = f32[8,2,32,128]{3,2,1,0:T(8,128)} custom-call(s32[16]{0:T(128)} %owner_map.1, s32[1]{0:T(128)S(6)} %copy.14.refs_0_, s32[1]{0:T(128)} %collective-permute-done.refs_1_, f32[8,2,32,128]{3,2,1,0:T(8,128)} %bitcast.30, f32[8,2,32,128]{3,2,1,0:T(8,128)} %bitcast.31), custom_call_target="tpu_custom_call" | custom-call | tf_op jit(solution)/shard_map/pick_slices/pallas_call | solution.py:100
  27.6 2.1 %collective-permute-done.2.first.refs_2_ = f32[2,16,32,128]{3,2,1,0:T(8,128)S(1)} collective-permute-done((f32[2,16,32,128]{3,2,1,0:T(8,128)S(1)}, f32[2,16,32,128]{3,2,1,0:T(8,128)S(1)}, u32[]{:S(2)}, u32[]{:S(2)}) %collective-permute-start.2) | collective-permute-done | bytes 524320 | tf_op jit(solution)/shard_map/ppermute | solution.py:477
  29.7 4.2 %all-to-all-start.1 = ((f32[16,32,128]{2,1,0:T(8,128)}), f32[16,32,128]{2,1,0:T(8,128)S(1)}, u32[]{:S(2)}, u32[]{:S(2)}) async-start(f32[16,32,128]{2,1,0:T(8,128)} %bitcast.29), calls=%async_computation.1 | async-start | bytes 524288 | tf_op jit(solution)/shard_map/all_to_all | solution.py:502
  33.9 1.8 %pack_corners.2 = f32[2,2,11,16,128]{4,3,2,1,0:T(8,128)} custom-call(f32[2,16,32,128]{3,2,1,0:T(8,128)} %copy-done.4, f32[2,16,32,128]{3,2,1,0:T(8,128)} %copy-done.2), custom_call_target="tpu_custom_call" | custom-call | tf_op jit(solution)/shard_map/pack_corners/pallas_call | solution.py:145
  36.4 0.7 copy-done.15
  37.7 3.9 %list_receivers.1.local_list = s32[788]{0:T(1024)} custom-call(s32[3,256]{1,0:T(4,128)} %bitcast.33), custom_call_target="tpu_custom_call" | custom-call | tf_op jit(solution)/shard_map/list_receivers/pallas_call | solution.py:69
  41.6 2.8 %collective-permute-done.7.refs_7_ = f32[2,2,11,16,128]{4,3,2,1,0:T(8,128)} collective-permute-done((f32[2,2,11,16,128]{4,3,2,1,0:T(8,128)}, f32[2,2,11,16,128]{4,3,2,1,0:T(8,128)}, u32[]{:S(2)}, u32[]{:S(2)}) %collective-permute-start.7) | collective-permute-done | bytes 360480 | tf_op jit(solution)/shard_map/ppermute | solution.py:493
  44.4 1.4 %all-to-all-done.1.refs_9_ = f32[16,32,128]{2,1,0:T(8,128)S(1)} async-done(((f32[16,32,128]{2,1,0:T(8,128)}), f32[16,32,128]{2,1,0:T(8,128)S(1)}, u32[]{:S(2)}, u32[]{:S(2)}) %all-to-all-start.1) | async-done | bytes 262176 | tf_op jit(solution)/shard_map/all_to_all | solution.py:502
  45.8 1.8 %pack_corners.3 = f32[2,2,9,16,128]{4,3,2,1,0:T(8,128)} custom-call(f32[2,16,32,128]{3,2,1,0:T(8,128)} %copy-done.8, f32[2,16,32,128]{3,2,1,0:T(8,128)} %copy-done.6), custom_call_target="tpu_custom_call" | custom-call | tf_op jit(solution)/shard_map/pack_corners/pallas_call | solution.py:145
  47.6 1.6 %collective-permute-start.8 = (f32[2,2,9,16,128]{4,3,2,1,0:T(8,128)}, f32[2,2,9,16,128]{4,3,2,1,0:T(8,128)S(1)}, u32[]{:S(2)}, u32[]{:S(2)}) collective-permute-start(f32[2,2,9,16,128]{4,3,2,1,0:T(8,128)} %pack_corners.3), channel_id=1, source_target_pairs={{0,1},{1,0},{2,3},{3,2},{4,5},{5,4},{6,7},{7,6},{8,9},{9,8},{10,11... | collective-permute-start | bytes 884744 | tf_op jit(solution)/shard_map/ppermute | solution.py:493
  49.1 0.7 collective-permute-start.13
  49.8 0.7 collective-permute-start.10
  50.5 4.9 %collective-permute-start.9 = (f32[16,32,128]{2,1,0:T(8,128)S(1)}, f32[16,32,128]{2,1,0:T(8,128)S(1)}, u32[]{:S(2)}, u32[]{:S(2)}) collective-permute-start(f32[16,32,128]{2,1,0:T(8,128)S(1)} %all-to-all-done.1.refs_9_), channel_id=1, source_target_pairs={{0,2},{2,0},{4,6},{6,4},{1,3},{3,1},{5,7},{7,5},{8,10},{10,8},{12,... | collective-permute-start | bytes 786440 | tf_op jit(solution)/shard_map/ppermute | solution.py:505
  55.8 1.1 %collective-permute-start.11 = (f32[16,16,128]{2,1,0:T(8,128)S(1)}, f32[16,16,128]{2,1,0:T(8,128)S(1)}, u32[]{:S(2)}, u32[]{:S(2)}) collective-permute-start(f32[16,16,128]{2,1,0:T(8,128)S(1)} %constant_dynamic-slice_fusion), channel_id=1, source_target_pairs={{0,1},{1,0},{2,3},{3,2},{4,5},{5,4},{6,7},{7,6},{8,9},{9,8},{10,11... | collective-permute-start | bytes 393224 | tf_op jit(solution)/shard_map/ppermute | solution.py:510
  57.0 4.7 %collective-permute-done.12.refs_13_ = f32[16,16,128]{2,1,0:T(8,128)S(1)} collective-permute-done((f32[16,16,128]{2,1,0:T(8,128)S(1)}, f32[16,16,128]{2,1,0:T(8,128)S(1)}, u32[]{:S(2)}, u32[]{:S(2)}) %collective-permute-start.12) | collective-permute-done | bytes 131104 | tf_op jit(solution)/shard_map/ppermute | solution.py:511
  62.3 0.6 copy-done.11
  62.9 1.0 %copy-done.7 = f32[2,16,32,128]{3,2,1,0:T(8,128)S(1)} copy-done((f32[2,16,32,128]{3,2,1,0:T(8,128)S(1)}, f32[2,16,32,128]{3,2,1,0:T(8,128)}, u32[]{:S(2)}) %copy-start.7) | copy-done | bytes 524312
  63.9 1.0 %copy-done.9 = f32[2,16,32,128]{3,2,1,0:T(8,128)S(1)} copy-done((f32[2,16,32,128]{3,2,1,0:T(8,128)S(1)}, f32[2,16,32,128]{3,2,1,0:T(8,128)}, u32[]{:S(2)}) %copy-start.9) | copy-done | bytes 524312
  65.0 20.3 %wave_window.1 = (f32[2,16,32,128]{3,2,1,0:T(8,128)}, f32[2,16,32,128]{3,2,1,0:T(8,128)}, f32[8,16,256]{2,1,0:T(8,128)S(1)}) custom-call(s32[2,3]{1,0:T(2,128)S(1)} %bitcast.27, f32[2,8]{1,0:T(2,128)S(1)} %bitcast.28, s32[788]{0:T(1024)S(1)} %copy-done.10, f32[2,16,32,128]{3,2,1,0:T(8,128)S(1)} %bitcast.22, f32[2,16,32,128]{3,2,1,0:T(8,128)S(1)} %bitcast.26, ...), custom_call_target="tpu_custom_call" | custom-call | tf_op jit(solution)/shard_map/wave_window/pallas_call | solution.py:446
  85.3 11.8 %all_to_all.15 = f32[8,16,256]{2,1,0:T(8,128)S(1)} all-to-all(f32[8,16,256]{2,1,0:T(8,128)S(1)} %get-tuple-element.34), channel_id=1, replica_groups=mesh['sy'=2,'core'=2,'gx'=4,'gy'=2] {'gx','gy'}, dimensions={0} | all-to-all | bytes 262144 | tf_op jit(solution)/shard_map/all_to_all | solution.py:519
  97.1 0.6 reduce_sum.9
  (42 shorter events, 2.3 us)
Async XLA Ops:
  0.6 20.0 %all-to-all-start = ((f32[16,32,128]{2,1,0:T(8,128)}), f32[16,32,128]{2,1,0:T(8,128)S(1)}, u32[]{:S(2)}, u32[]{:S(2)}) async-start(f32[16,32,128]{2,1,0:T(8,128)} %param.8), calls=%async_computation | async-start | bytes 524288 | tf_op jit(solution)/shard_map/all_to_all | solution.py:476
  7.9 3.5 %copy-start = (f32[1,2,16,32,128]{4,3,2,1,0:T(8,128)S(1)}, f32[1,2,16,32,128]{4,3,2,1,0:T(8,128)}, u32[]{:S(2)}) copy-start(f32[1,2,16,32,128]{4,3,2,1,0:T(8,128)} %param.11) | copy-start | bytes 1572868
  7.9 12.7 %copy-start.1 = (f32[1,2,16,32,128]{4,3,2,1,0:T(8,128)S(1)}, f32[1,2,16,32,128]{4,3,2,1,0:T(8,128)}, u32[]{:S(2)}) copy-start(f32[1,2,16,32,128]{4,3,2,1,0:T(8,128)} %param.12) | copy-start | bytes 1572868
  9.9 17.7 %collective-permute-start.4 = (f32[2,2,16,16,128]{4,3,2,1,0:T(8,128)}, f32[2,2,16,16,128]{4,3,2,1,0:T(8,128)}, u32[]{:S(2)}, u32[]{:S(2)}) collective-permute-start(f32[2,2,16,16,128]{4,3,2,1,0:T(8,128)} %pack_sides.1), channel_id=1, source_target_pairs={{0,1},{1,0},{2,3},{3,2},{4,5},{5,4},{6,7},{7,6},{8,9},{9,8},{10,11... | collective-permute-start | bytes 1572872 | tf_op jit(solution)/shard_map/ppermute | solution.py:483
  11.4 16.2 %collective-permute-start.3 = (f32[2,16,32,128]{3,2,1,0:T(8,128)S(1)}, f32[2,16,32,128]{3,2,1,0:T(8,128)S(1)}, u32[]{:S(2)}, u32[]{:S(2)}) collective-permute-start(f32[2,16,32,128]{3,2,1,0:T(8,128)S(1)} %bitcast.20), channel_id=1, source_target_pairs={{2,4},{4,2},{3,5},{5,3},{10,12},{12,10},{11,13},{13,11},{18,20},{2... | collective-permute-start | bytes 1572872 | tf_op jit(solution)/shard_map/ppermute | solution.py:477
  12.1 17.6 %collective-permute-start.2 = (f32[2,16,32,128]{3,2,1,0:T(8,128)S(1)}, f32[2,16,32,128]{3,2,1,0:T(8,128)S(1)}, u32[]{:S(2)}, u32[]{:S(2)}) collective-permute-start(f32[2,16,32,128]{3,2,1,0:T(8,128)S(1)} %bitcast.21), channel_id=1, source_target_pairs={{0,2},{2,0},{4,6},{6,4},{1,3},{3,1},{5,7},{7,5},{8,10},{10,8},{12,... | collective-permute-start | bytes 1572872 | tf_op jit(solution)/shard_map/ppermute | solution.py:477
  16.9 3.8 %collective-permute-start = (s32[1]{0:T(128)}, s32[1]{0:T(128)}, u32[]{:S(2)}, u32[]{:S(2)}) collective-permute-start(s32[1]{0:T(128)} %param.10), channel_id=1, source_target_pairs={{0,16},{16,0},{1,17},{17,1},{2,18},{18,2},{3,19},{19,3},{4,20},{20... | collective-permute-start | bytes 20 | tf_op jit(solution)/shard_map/ppermute | solution.py:480
  20.7 3.9 %copy-start.13 = (f32[16,32,128]{2,1,0:T(8,128)}, f32[16,32,128]{2,1,0:T(8,128)S(1)}, u32[]{:S(2)}) copy-start(f32[16,32,128]{2,1,0:T(8,128)S(1)} %all-to-all-done) | copy-start | bytes 786436
  20.7 1.5 %collective-permute-start.1 = (f32[16,32,128]{2,1,0:T(8,128)S(1)}, f32[16,32,128]{2,1,0:T(8,128)S(1)}, u32[]{:S(2)}, u32[]{:S(2)}) collective-permute-start(f32[16,32,128]{2,1,0:T(8,128)S(1)} %all-to-all-done), channel_id=1, source_target_pairs={{0,8},{8,0},{1,9},{9,1},{2,10},{10,2},{3,11},{11,3},{4,12},{12,4},... | collective-permute-start | bytes 786440 | tf_op jit(solution)/shard_map/ppermute | solution.py:485
  20.7 20.9 %collective-permute-start.6 = (f32[2,16,32,128]{3,2,1,0:T(8,128)S(1)}, f32[2,16,32,128]{3,2,1,0:T(8,128)S(1)}, u32[]{:S(2)}, u32[]{:S(2)}) collective-permute-start(f32[2,16,32,128]{3,2,1,0:T(8,128)S(1)} %bitcast.24), channel_id=1, source_target_pairs={{2,4},{4,2},{3,5},{5,3},{10,12},{12,10},{11,13},{13,11},{18,20},{2... | collective-permute-start | bytes 1572872 | tf_op jit(solution)/shard_map/ppermute | solution.py:486
  22.2 0.7 copy-start.14
  22.9 18.7 %collective-permute-start.5 = (f32[2,16,32,128]{3,2,1,0:T(8,128)S(1)}, f32[2,16,32,128]{3,2,1,0:T(8,128)S(1)}, u32[]{:S(2)}, u32[]{:S(2)}) collective-permute-start(f32[2,16,32,128]{3,2,1,0:T(8,128)S(1)} %bitcast.25), channel_id=1, source_target_pairs={{0,2},{2,0},{4,6},{6,4},{1,3},{3,1},{5,7},{7,5},{8,10},{10,8},{12,... | collective-permute-start | bytes 1572872 | tf_op jit(solution)/shard_map/ppermute | solution.py:486
  27.6 6.3 %copy-start.2 = (f32[2,16,32,128]{3,2,1,0:T(8,128)}, f32[2,16,32,128]{3,2,1,0:T(8,128)S(1)}, u32[]{:S(2)}) copy-start(f32[2,16,32,128]{3,2,1,0:T(8,128)S(1)} %collective-permute-done.3.second.refs_3_) | copy-start | bytes 1572868
  29.7 4.2 %copy-start.4 = (f32[2,16,32,128]{3,2,1,0:T(8,128)}, f32[2,16,32,128]{3,2,1,0:T(8,128)S(1)}, u32[]{:S(2)}) copy-start(f32[2,16,32,128]{3,2,1,0:T(8,128)S(1)} %collective-permute-done.2.first.refs_2_) | copy-start | bytes 1572868
  29.7 16.1 %all-to-all-start.1 = ((f32[16,32,128]{2,1,0:T(8,128)}), f32[16,32,128]{2,1,0:T(8,128)S(1)}, u32[]{:S(2)}, u32[]{:S(2)}) async-start(f32[16,32,128]{2,1,0:T(8,128)} %bitcast.29), calls=%async_computation.1 | async-start | bytes 524288 | tf_op jit(solution)/shard_map/all_to_all | solution.py:502
  35.8 8.6 %collective-permute-start.7 = (f32[2,2,11,16,128]{4,3,2,1,0:T(8,128)}, f32[2,2,11,16,128]{4,3,2,1,0:T(8,128)}, u32[]{:S(2)}, u32[]{:S(2)}) collective-permute-start(f32[2,2,11,16,128]{4,3,2,1,0:T(8,128)} %pack_corners.2), channel_id=1, source_target_pairs={{0,1},{1,0},{2,3},{3,2},{4,5},{5,4},{6,7},{7,6},{8,9},{9,8},{10,11... | collective-permute-start | bytes 1081352 | tf_op jit(solution)/shard_map/ppermute | solution.py:493
  36.4 0.7 copy-start.15
  41.5 20.7 %copy-start.3 = (f32[2,16,32,128]{3,2,1,0:T(8,128)S(1)}, f32[2,16,32,128]{3,2,1,0:T(8,128)}, u32[]{:S(2)}) copy-start(f32[2,16,32,128]{3,2,1,0:T(8,128)} %copy-done.2) | copy-start | bytes 1572868
  41.6 20.7 %copy-start.5 = (f32[2,16,32,128]{3,2,1,0:T(8,128)S(1)}, f32[2,16,32,128]{3,2,1,0:T(8,128)}, u32[]{:S(2)}) copy-start(f32[2,16,32,128]{3,2,1,0:T(8,128)} %copy-done.4) | copy-start | bytes 1572868
  41.6 4.2 %copy-start.6 = (f32[2,16,32,128]{3,2,1,0:T(8,128)}, f32[2,16,32,128]{3,2,1,0:T(8,128)S(1)}, u32[]{:S(2)}) copy-start(f32[2,16,32,128]{3,2,1,0:T(8,128)S(1)} %collective-permute-done.6.second.refs_5_) | copy-start | bytes 1572868
  41.6 4.2 %copy-start.8 = (f32[2,16,32,128]{3,2,1,0:T(8,128)}, f32[2,16,32,128]{3,2,1,0:T(8,128)S(1)}, u32[]{:S(2)}) copy-start(f32[2,16,32,128]{3,2,1,0:T(8,128)S(1)} %collective-permute-done.5.first.refs_4_) | copy-start | bytes 1572868
  47.6 14.7 %collective-permute-start.8 = (f32[2,2,9,16,128]{4,3,2,1,0:T(8,128)}, f32[2,2,9,16,128]{4,3,2,1,0:T(8,128)S(1)}, u32[]{:S(2)}, u32[]{:S(2)}) collective-permute-start(f32[2,2,9,16,128]{4,3,2,1,0:T(8,128)} %pack_corners.3), channel_id=1, source_target_pairs={{0,1},{1,0},{2,3},{3,2},{4,5},{5,4},{6,7},{7,6},{8,9},{9,8},{10,11... | collective-permute-start | bytes 884744 | tf_op jit(solution)/shard_map/ppermute | solution.py:493
  49.1 13.1 %copy-start.10 = (s32[788]{0:T(1024)S(1)}, s32[788]{0:T(1024)}, u32[]{:S(2)}) copy-start(s32[788]{0:T(1024)} %list_receivers.1.local_list) | copy-start | bytes 9460
  49.1 13.1 %copy-start.12 = (f32[1,2,8]{2,1,0:T(2,128)S(1)}, f32[1,2,8]{2,1,0:T(2,128)}, u32[]{:S(2)}) copy-start(f32[1,2,8]{2,1,0:T(2,128)} %param.14) | copy-start | bytes 196
  49.1 6.7 %collective-permute-start.13 = (f32[16,16,128]{2,1,0:T(8,128)S(1)}, f32[16,16,128]{2,1,0:T(8,128)S(1)}, u32[]{:S(2)}, u32[]{:S(2)}) collective-permute-start(f32[16,16,128]{2,1,0:T(8,128)S(1)} %constant_dynamic-slice_fusion), channel_id=1, source_target_pairs={{2,5},{3,4},{4,3},{5,2},{10,13},{11,12},{12,11},{13,10},{18,21},{1... | collective-permute-start | bytes 393224 | tf_op jit(solution)/shard_map/ppermute | solution.py:511
  49.8 12.4 %collective-permute-start.10 = (f32[16,32,128]{2,1,0:T(8,128)S(1)}, f32[16,32,128]{2,1,0:T(8,128)S(1)}, u32[]{:S(2)}, u32[]{:S(2)}) collective-permute-start(f32[16,32,128]{2,1,0:T(8,128)S(1)} %all-to-all-done.1.refs_9_), channel_id=1, source_target_pairs={{2,4},{4,2},{3,5},{5,3},{10,12},{12,10},{11,13},{13,11},{18,20},{2... | collective-permute-start | bytes 786440 | tf_op jit(solution)/shard_map/ppermute | solution.py:505
  50.5 11.7 %collective-permute-start.9 = (f32[16,32,128]{2,1,0:T(8,128)S(1)}, f32[16,32,128]{2,1,0:T(8,128)S(1)}, u32[]{:S(2)}, u32[]{:S(2)}) collective-permute-start(f32[16,32,128]{2,1,0:T(8,128)S(1)} %all-to-all-done.1.refs_9_), channel_id=1, source_target_pairs={{0,2},{2,0},{4,6},{6,4},{1,3},{3,1},{5,7},{7,5},{8,10},{10,8},{12,... | collective-permute-start | bytes 786440 | tf_op jit(solution)/shard_map/ppermute | solution.py:505
  55.4 6.2 %collective-permute-start.12 = (f32[16,16,128]{2,1,0:T(8,128)S(1)}, f32[16,16,128]{2,1,0:T(8,128)S(1)}, u32[]{:S(2)}, u32[]{:S(2)}) collective-permute-start(f32[16,16,128]{2,1,0:T(8,128)S(1)} %constant_dynamic-slice_fusion), channel_id=1, source_target_pairs={{0,3},{1,2},{2,1},{3,0},{4,7},{5,6},{6,5},{7,4},{8,11},{9,10},{10,... | collective-permute-start | bytes 393224 | tf_op jit(solution)/shard_map/ppermute | solution.py:511
  55.8 6.4 %collective-permute-start.11 = (f32[16,16,128]{2,1,0:T(8,128)S(1)}, f32[16,16,128]{2,1,0:T(8,128)S(1)}, u32[]{:S(2)}, u32[]{:S(2)}) collective-permute-start(f32[16,16,128]{2,1,0:T(8,128)S(1)} %constant_dynamic-slice_fusion), channel_id=1, source_target_pairs={{0,1},{1,0},{2,3},{3,2},{4,5},{5,4},{6,7},{7,6},{8,9},{9,8},{10,11... | collective-permute-start | bytes 393224 | tf_op jit(solution)/shard_map/ppermute | solution.py:510
  62.2 0.7 copy-start.11
  62.9 1.0 %copy-start.7 = (f32[2,16,32,128]{3,2,1,0:T(8,128)S(1)}, f32[2,16,32,128]{3,2,1,0:T(8,128)}, u32[]{:S(2)}) copy-start(f32[2,16,32,128]{3,2,1,0:T(8,128)} %copy-done.6) | copy-start | bytes 1572868
  63.9 1.0 %copy-start.9 = (f32[2,16,32,128]{3,2,1,0:T(8,128)S(1)}, f32[2,16,32,128]{3,2,1,0:T(8,128)}, u32[]{:S(2)}) copy-start(f32[2,16,32,128]{3,2,1,0:T(8,128)} %copy-done.8) | copy-start | bytes 1572868

commit v4 on v3

--- a/solution.py
+++ b/solution.py
@@ -24,6 +24,7 @@
 
 SMEM = pl.BlockSpec(memory_space=pltpu.SMEM)
 ANY = pl.BlockSpec(memory_space=pl.ANY)
+SMALL = 4 * 2**20
 VMEM = pl.BlockSpec(memory_space=pltpu.VMEM)
 
 
@@ -71,6 +72,7 @@
         out_shape=jax.ShapeDtypeStruct((3 * (total + BATCH) + 8,), jnp.int32),
         in_specs=[SMEM],
         out_specs=SMEM,
+        compiler_params=pltpu.CompilerParams(vmem_limit_bytes=SMALL),
         name="list_receivers",
     )(receivers)
 
@@ -103,6 +105,7 @@
         in_specs=[SMEM] * (1 + len(shifts)) + [ANY, ANY],
         out_specs=VMEM,
         scratch_shapes=[pltpu.SemaphoreType.DMA((targets,))],
+        compiler_params=pltpu.CompilerParams(vmem_limit_bytes=SMALL),
         name="pick_slices",
     )(owner_map, *shifts, stored, other)
 
@@ -148,6 +151,7 @@
         in_specs=[ANY, ANY],
         out_specs=VMEM,
         scratch_shapes=[pltpu.SemaphoreType.DMA((8,))],
+        compiler_params=pltpu.CompilerParams(vmem_limit_bytes=SMALL),
         name="pack_corners",
     )(*blocks)
 
@@ -173,8 +177,137 @@
         in_specs=[ANY, ANY],
         out_specs=VMEM,
         scratch_shapes=[pltpu.SemaphoreType.DMA((2,))],
+        compiler_params=pltpu.CompilerParams(vmem_limit_bytes=SMALL),
         name="pack_sides",
     )(now, prev)
+
+
+def layout(sizes):
+    block_x, block_y, _, _, ny = sizes
+    odd_x, odd_y = lax.rem(lax.axis_index("gx"), 2), lax.rem(lax.axis_index("gy"), 2)
+    own = pl.multiple_of(PAD + (HALO * odd_y if ny == 2 else HALO), 8)
+    high_x = [odd_x == 0, odd_x == 1]
+    high_y = [odd_y == 0, odd_y == 1]
+    x_at = [jnp.where(h, HALO + block_x, 0) for h in high_x]
+    y_at = [pl.multiple_of(jnp.where(h, own + block_y, own - HALO), 8) for h in high_y]
+    near_y = [pl.multiple_of(jnp.where(h, own + block_y, own - HALF), 8) for h in high_y]
+    return own, odd_y, high_x, x_at, y_at, near_y
+
+
+def depth_in(cell, total, width):
+    inside = (cell >= 0) & (cell < total)
+    depth = jnp.maximum(width - jnp.minimum(cell + 1, total - cell), 0)
+    return inside, depth.astype(jnp.float32) / width
+
+
+def assemble_kernel(sizes, now, prev, now_x, prev_x, sides, corners_now, corners_prev, ext_all, sems):
+    block_x, block_y, total_x, total_y, ny = sizes
+    shots = now.shape[0]
+    planes, rows, depth = ext_all.shape[1:]
+    now_ext, prev_ext = ext_all.at[pl.ds(0, shots)], ext_all.at[pl.ds(shots, shots)]
+    twice = ext_all.at[2 * shots + 1]
+    own, _, high_x, x_at, y_at, near_y = layout(sizes)
+    blank = jnp.zeros((PAD, depth), jnp.float32)
+
+    def clear(x, _):
+        for s in range(2 * shots):
+            ext_all[s, x, pl.ds(0, PAD)] = blank
+            ext_all[s, x, pl.ds(rows - PAD, PAD)] = blank
+        return 0
+
+    lax.fori_loop(0, planes, clear, 0)
+    for f in range(len(sides)):
+        for e in range(2):
+
+            def clear_corner(x, _):
+                for s in range(2 * shots):
+                    for k in range(HALO // PAD):
+                        ext_all[s, x_at[e] + x, pl.ds(y_at[f] + PAD * k, PAD)] = blank
+                return 0
+
+            lax.fori_loop(0, HALO, clear_corner, 0)
+
+    copies = []
+
+    def fetch(src, dst):
+        copy = pltpu.make_async_copy(src, dst, sems.at[len(copies)])
+        copy.start()
+        copies.append(copy)
+
+    def place_corner(ext, packed, reach, e, f):
+        near, far = reach
+        lead = pl.ds(jnp.where(high_x[e], HALO + block_x, HALO - near), near)
+        fetch(packed.at[:, pl.ds(0, near)], ext.at[:, lead, pl.ds(y_at[f], HALO)])
+        for k in range(2):
+            first_plane = jnp.where(high_x[e], HALO + block_x + near, HALO - near - far)
+            fetch(
+                packed.at[:, pl.ds(near, far // 2), pl.ds(k * HALF, HALF)],
+                ext.at[:, pl.ds(first_plane + k * (far // 2), far // 2), pl.ds(near_y[f], HALF)],
+            )
+
+    own_rows = pl.ds(own, block_y)
+    fetch(now, now_ext.at[:, pl.ds(HALO, block_x), own_rows])
+    fetch(prev, prev_ext.at[:, pl.ds(HALO, block_x), own_rows])
+    for e in range(2):
+        at = pl.ds(x_at[e], block_x)
+        fetch(now_x[e], now_ext.at[:, at, own_rows])
+        fetch(prev_x[e], prev_ext.at[:, at, own_rows])
+    for f in range(len(sides)):
+        at = pl.ds(y_at[f], HALO)
+        fetch(sides[f].at[0], now_ext.at[:, pl.ds(HALO, block_x), at])
+        fetch(sides[f].at[1], prev_ext.at[:, pl.ds(HALO, block_x), at])
+        for e in range(2):
+            for ext, packed, reach in (
+                (now_ext, corners_now, REACH_NOW),
+                (prev_ext, corners_prev, REACH_PREV),
+            ):
+                place_corner(ext, packed[f].at[e], reach, e, f)
+
+    x_first = lax.axis_index("gx") * block_x - HALO
+    y_first = lax.axis_index("gy") * block_y - own
+    shape = (rows, depth)
+    y_in, y_depth = depth_in(lax.broadcasted_iota(jnp.int32, shape, 0) + y_first, total_y, block_x)
+    y_part = y_depth * y_depth
+
+    def weigh(x, _):
+        x_in, x_depth = depth_in(jnp.full(shape, x + x_first, jnp.int32), total_x, block_x)
+        twice[x] = jnp.where(
+            x_in & y_in, 2.0 / (1.0 + damp_peak * (x_depth * x_depth + y_part)), 0.0
+        )
+        return 0
+
+    lax.fori_loop(2, planes - 2, weigh, 0)
+    for copy in copies:
+        copy.wait()
+
+
+def call_with_groups(kernel, sizes, counts):
+    def called(*refs):
+        groups = []
+        for count in counts:
+            groups.append(refs[0] if count is None else refs[:count])
+            refs = refs[1 if count is None else count:]
+        kernel(sizes, *groups, *refs)
+
+    return called
+
+
+def assemble(sizes, now, prev, now_x, prev_x, sides, corners):
+    block_x, block_y, _, _, ny = sizes
+    shots, _, _, depth = now.shape
+    planes = block_x + 2 * HALO
+    rows = block_y + (HALO if ny == 2 else 2 * HALO) + 2 * PAD
+    count = len(sides)
+    parts = [now, prev, *now_x, *prev_x, *sides, *corners[0], *corners[1]]
+    return pl.pallas_call(
+        call_with_groups(assemble_kernel, sizes, (None, None, 2, 2, count, count, count)),
+        out_shape=pltpu.VMEM((2 * shots + 2, planes, rows, depth), jnp.float32),
+        in_specs=[ANY] * len(parts),
+        out_specs=VMEM,
+        scratch_shapes=[pltpu.SemaphoreType.DMA((64,))],
+        compiler_params=pltpu.CompilerParams(vmem_limit_bytes=SMALL),
+        name="assemble_fields",
+    )(*parts)
 
 
 def window_kernel(
@@ -182,13 +315,7 @@
     sources,
     amplitudes,
     local_list,
-    now,
-    prev,
-    now_x,
-    prev_x,
-    sides,
-    corners_now,
-    corners_prev,
+    _,
     speed,
     speed_x,
     speed_y,
@@ -202,45 +329,14 @@
     out_sems,
 ):
     block_x, block_y, total_x, total_y, ny = sizes
-    half_way = (ext_all.shape[0] - 2) // 2
-    now_ext, prev_ext = ext_all.at[pl.ds(0, half_way)], ext_all.at[pl.ds(half_way, half_way)]
-    near, twice = ext_all.at[2 * half_way], ext_all.at[2 * half_way + 1]
-    rows = now_ext.shape[2]
-    planes = now_ext.shape[1]
-    shots = now_ext.shape[0]
-    column, row = lax.axis_index("gx"), lax.axis_index("gy")
-    odd_x, odd_y = lax.rem(column, 2), lax.rem(row, 2)
-    own = pl.multiple_of(PAD + (HALO * odd_y if ny == 2 else HALO), 8)
-    high_x = [odd_x == 0, odd_x == 1]
-    high_y = [odd_y == 0, odd_y == 1]
-    x_at = [jnp.where(h, HALO + block_x, 0) for h in high_x]
-    y_at = [
-        pl.multiple_of(jnp.where(h, own + block_y, own - HALO), 8) for h in high_y
-    ]
-    near_y = [
-        pl.multiple_of(jnp.where(h, own + block_y, own - HALF), 8) for h in high_y
-    ]
-    y_count = len(speed_y)
-    blank = jnp.zeros((PAD, now_ext.shape[3]), jnp.float32)
-
-    def clear(x, _):
-        for s in range(2 * shots):
-            ext_all[s, x, pl.ds(0, PAD)] = blank
-            ext_all[s, x, pl.ds(rows - PAD, PAD)] = blank
-        return 0
-
-    lax.fori_loop(0, planes, clear, 0)
-    for f in range(y_count):
-        for e in range(2):
-
-            def clear_corner(x, _):
-                for s in range(2 * shots + 1):
-                    for k in range(HALO // PAD):
-                        ext_all[s, x_at[e] + x, pl.ds(y_at[f] + PAD * k, PAD)] = blank
-                return 0
-
-            lax.fori_loop(0, HALO, clear_corner, 0)
-
+    shots = (ext_all.shape[0] - 2) // 2
+    now_ext, prev_ext = ext_all.at[pl.ds(0, shots)], ext_all.at[pl.ds(shots, shots)]
+    near, twice = ext_all.at[2 * shots], ext_all.at[2 * shots + 1]
+    planes, rows = ext_all.shape[1:3]
+    own, odd_y, high_x, x_at, y_at, near_y = layout(sizes)
+    own_rows = pl.ds(own, block_y)
+    x_first = lax.axis_index("gx") * block_x - HALO
+    y_first = lax.axis_index("gy") * block_y - own
     copies = []
 
     def fetch(src, dst):
@@ -248,75 +344,26 @@
         copy.start()
         copies.append(copy)
 
-
-    def place_corner(ext, packed, reach, e, f):
-        near, far = reach
-        lead = pl.ds(jnp.where(high_x[e], HALO + block_x, HALO - near), near)
-        fetch(packed.at[:, pl.ds(0, near)], ext.at[:, lead, pl.ds(y_at[f], HALO)])
-        for k in range(2):
-            first_plane = jnp.where(high_x[e], HALO + block_x + near, HALO - near - far)
-            fetch(
-                packed.at[:, pl.ds(near, far // 2), pl.ds(k * HALF, HALF)],
-                ext.at[:, pl.ds(first_plane + k * (far // 2), far // 2), pl.ds(near_y[f], HALF)],
-            )
-
-    own_rows = pl.ds(own, block_y)
     fetch(speed, near.at[pl.ds(HALO, block_x), own_rows])
     for e in range(2):
         fetch(speed_x[e], near.at[pl.ds(x_at[e], block_x), own_rows])
-    for f in range(y_count):
+    for f in range(len(speed_y)):
         at = pl.ds(y_at[f], HALO)
         fetch(speed_y[f], near.at[pl.ds(HALO, block_x), at])
         for e in range(2):
             fetch(speed_xy[2 * f + e], near.at[pl.ds(x_at[e], block_x), at])
-    speed_copies = len(copies)
-    fetch(now, now_ext.at[:, pl.ds(HALO, block_x), own_rows])
-    fetch(prev, prev_ext.at[:, pl.ds(HALO, block_x), own_rows])
-    for e in range(2):
-        at = pl.ds(x_at[e], block_x)
-        fetch(now_x[e], now_ext.at[:, at, own_rows])
-        fetch(prev_x[e], prev_ext.at[:, at, own_rows])
-    for f in range(y_count):
-        at = pl.ds(y_at[f], HALO)
-        fetch(sides[f].at[0], now_ext.at[:, pl.ds(HALO, block_x), at])
-        fetch(sides[f].at[1], prev_ext.at[:, pl.ds(HALO, block_x), at])
-        for e in range(2):
-            for ext, packed, reach in (
-                (now_ext, corners_now, REACH_NOW),
-                (prev_ext, corners_prev, REACH_PREV),
-            ):
-                place_corner(ext, packed[f].at[e], reach, e, f)
-
-    def depth_in(cell, total):
-        inside = (cell >= 0) & (cell < total)
-        depth = jnp.maximum(
-            block_x - jnp.minimum(cell + 1, total - cell), 0
-        ).astype(jnp.float32) / block_x
-        return inside, depth
-
-    x_first = column * block_x - HALO
-    y_first = row * block_y - own
-    shape = (rows, now_ext.shape[3])
-    y_in, y_depth = depth_in(lax.broadcasted_iota(jnp.int32, shape, 0) + y_first, total_y)
-    y_part = y_depth * y_depth
-
     for k in range(shots * STEPS):
         samples[k] = jnp.zeros(samples.shape[1:], jnp.float32)
-    for copy in copies[:speed_copies]:
+    for copy in copies:
         copy.wait()
 
     def prepare(x, _):
-        x_in, x_depth = depth_in(jnp.full(shape, x + x_first, jnp.int32), total_x)
-        inverse = 1.0 / (1.0 + damp_peak * (x_depth * x_depth + y_part))
-        inverse = jnp.where(x_in & y_in, inverse, 0.0)
-        v = near[x]
-        near[x] = jnp.where(x_in & y_in, inverse * (v * v) * near_weight, 0.0)
-        twice[x] = 2.0 * inverse
+        at = pl.ds(PAD, rows - 2 * PAD)
+        v = near[x, at]
+        near[x, at] = (0.5 * near_weight) * twice[x, at] * (v * v)
         return 0
 
     lax.fori_loop(2, planes - 2, prepare, 0, unroll=2)
-    for copy in copies[speed_copies:]:
-        copy.wait()
 
     depth = now_ext.shape[3]
     gap = lax.broadcasted_iota(jnp.int32, (depth, depth), 0) - lax.broadcasted_iota(jnp.int32, (depth, depth), 1)
@@ -339,36 +386,50 @@
 
         size = 8 * tiles
 
-        def plane(g, _, cur=cur, old=old, first=first, tiles=tiles, size=size, step=step):
+        def plane(g, _, cur=cur, old=old, first=first, tiles=tiles, step=step):
             x = 2 * step + GROUP * g
-            along = []
-            for s in range(shots):
-                c = cur[s, pl.ds(x, GROUP), pl.ds(first, size)].reshape(GROUP * size, depth)
-                head = c.astype(jnp.bfloat16)
-                rest = (c - head.astype(jnp.float32)).astype(jnp.bfloat16)
-                parts = jnp.concatenate([head, rest], axis=1)
-                out = jnp.dot(parts, band, preferred_element_type=jnp.float32)
-                along.append(out.reshape(GROUP, size, depth))
-            for s in range(shots):
-                for j in range(tiles):
-                    base = first + 8 * j
+            for j0 in range(0, tiles, 3):
+                sub = min(3, tiles - j0)
+                size = 8 * sub
+                start = pl.multiple_of(first + 8 * j0, 8)
+                along = []
+                for s in range(shots):
+                    c = cur[s, pl.ds(x, GROUP), pl.ds(start, size)].reshape(GROUP * size, depth)
+                    head = c.astype(jnp.bfloat16)
+                    rest = (c - head.astype(jnp.float32)).astype(jnp.bfloat16)
+                    parts = jnp.concatenate([head, rest], axis=1)
+                    out = jnp.dot(parts, band, preferred_element_type=jnp.float32)
+                    along.append(out.reshape(GROUP, size, depth))
+                for j in range(sub):
+                    base = start + 8 * j
                     at = pl.ds(pl.multiple_of(base, 8), 8)
                     n = [near[x + i, at] for i in range(GROUP)]
                     a = [twice[x + i, at] for i in range(GROUP)]
-                    c = [cur[s, x + i - 2, at] for i in range(GROUP + 4)]
-                    out = []
-                    for i in range(GROUP):
-                        m = c[i + 2]
-                        close = (c[i + 1] + c[i + 3]) + (cur[s, x + i, pl.ds(base - 1, 8)] + cur[s, x + i, pl.ds(base + 1, 8)])
-                        wide = (c[i] + c[i + 4]) + (cur[s, x + i, pl.ds(base - 2, 8)] + cur[s, x + i, pl.ds(base + 2, 8)])
-                        p = old[s, x + i, at]
-                        lap = along[s][i, 8 * j : 8 * j + 8] + close + far_part * wide
-                        out.append(p + a[i] * (m - p) + n[i] * lap)
-                    for i in range(GROUP):
-                        old[s, x + i, at] = out[i]
+                    for s in range(shots):
+                        c = [cur[s, x + i - 2, at] for i in range(GROUP + 4)]
+                        out = []
+                        for i in range(GROUP):
+                            m = c[i + 2]
+                            close = (c[i + 1] + c[i + 3]) + (cur[s, x + i, pl.ds(base - 1, 8)] + cur[s, x + i, pl.ds(base + 1, 8)])
+                            wide = (c[i] + c[i + 4]) + (cur[s, x + i, pl.ds(base - 2, 8)] + cur[s, x + i, pl.ds(base + 2, 8)])
+                            p = old[s, x + i, at]
+                            lap = along[s][i, 8 * j : 8 * j + 8] + close + far_part * wide
+                            out.append(p + a[i] * (m - p) + n[i] * lap)
+                        for i in range(GROUP):
+                            old[s, x + i, at] = out[i]
             return 0
 
-        lax.fori_loop(0, (planes - 4 * step) // GROUP, plane, 0)
+        count = (planes - 4 * step) // GROUP
+        edge = 2 if side == 2 else 0
+        if edge:
+            cut = functools.partial(
+                plane,
+                first=pl.multiple_of(own - 8 * (odd_y if ny == 2 else 1), 8),
+                tiles=tiles - (1 if ny == 2 else 2),
+            )
+            lax.fori_loop(0, edge, cut, 0)
+            lax.fori_loop(count - edge, count, cut, 0)
+        lax.fori_loop(edge, count - edge, plane, 0)
 
         for s in range(shots):
             sx = sources[s, 0] - x_first
@@ -427,42 +488,32 @@
     last_out.wait()
 
 
-def window(sizes, sources, amplitudes, local_list, recs, now, prev, now_x, prev_x, sides, corners, speed, speed_x, speed_y, speed_xy, copies):
-    block_x, block_y, total_x, total_y, ny = sizes
-    shots, _, _, depth = now.shape
-    planes = block_x + 2 * HALO
-    rows = block_y + (HALO if ny == 2 else 2 * HALO) + 2 * PAD
-
+def window(sizes, sources, amplitudes, local_list, recs, ext_all, speed, speed_x, speed_y, speed_xy, copies):
+    block_x, block_y, _, _, _ = sizes
+    shots = (ext_all.shape[0] - 2) // 2
+    depth = ext_all.shape[3]
+    field = jax.ShapeDtypeStruct((shots, block_x, block_y, depth), jnp.float32)
     count = len(speed_y)
-    parts = [now, prev, *now_x, *prev_x, *sides, *corners[0], *corners[1], speed, *speed_x, *speed_y, *speed_xy]
-
-    def kernel(sources, amplitudes, local_list, *refs):
-        groups = []
-        for size in (1, 1, 2, 2, count, count, count, 1, 2, count, 2 * count):
-            groups.append(refs[0] if size == 1 and len(groups) in (0, 1, 7) else refs[:size])
-            refs = refs[size:]
-        window_kernel(sizes, sources, amplitudes, local_list, *groups, *refs)
-
+    parts = [speed, *speed_x, *speed_y, *speed_xy]
     return pl.pallas_call(
-        kernel,
+        call_with_groups(window_kernel, sizes, (None, None, None, None, None, 2, count, 2 * count)),
         out_shape=(
-            jax.ShapeDtypeStruct(now.shape, now.dtype),
-            jax.ShapeDtypeStruct(now.shape, now.dtype),
-            jax.ShapeDtypeStruct((copies, shots * STEPS, recs), now.dtype),
+            field,
+            field,
+            jax.ShapeDtypeStruct((copies, shots * STEPS, recs), jnp.float32),
+            pltpu.VMEM(ext_all.shape, jnp.float32),
         ),
-        in_specs=[SMEM] * 3 + [ANY] * len(parts),
-        out_specs=(ANY, ANY, VMEM),
+        in_specs=[SMEM] * 3 + [VMEM] + [ANY] * len(parts),
+        out_specs=(ANY, ANY, VMEM, VMEM),
+        input_output_aliases={3: 3},
         scratch_shapes=[
-            pltpu.VMEM((2 * shots + 2, planes, rows, depth), jnp.float32),
             pltpu.VMEM((shots * STEPS, recs + 8, depth), jnp.float32),
-            pltpu.SemaphoreType.DMA((64,)),
+            pltpu.SemaphoreType.DMA((16,)),
             pltpu.SemaphoreType.DMA((2,)),
         ],
-        compiler_params=pltpu.CompilerParams(vmem_limit_bytes=40 * 2**20),
+        compiler_params=pltpu.CompilerParams(vmem_limit_bytes=16 * 2**20),
         name="wave_window",
-    )(
-        sources, amplitudes, local_list, *parts
-    )
+    )(sources, amplitudes, local_list, ext_all, *parts)
 
 
 def local(model_tiles, owner_map, offsets, field_now, field_prev, sources, wavelet, receivers):
@@ -510,11 +561,11 @@
         speed_y.append(lax.ppermute(part, "gy", perm))
         speed_xy += [lax.ppermute(part, ("gx", "gy"), joint(x_perm, perm, ny)) for x_perm in x_perms]
 
-    out_now, out_prev, partial = window(
-        (block_x, block_y, total_x, total_y, ny),
-        sources[0], wavelet[0], local_list, receivers.shape[1],
-        now, prev, now_x, prev_x, sides, corners,
-        speed, speed_x, speed_y, speed_xy, nx * ny,
+    sizes = (block_x, block_y, total_x, total_y, ny)
+    ext_all = assemble(sizes, now, prev, now_x, prev_x, sides, corners)
+    out_now, out_prev, partial, _ = window(
+        sizes, sources[0], wavelet[0], local_list, receivers.shape[1],
+        ext_all, speed, speed_x, speed_y, speed_xy, nx * ny,
     )
     gathered = lax.all_to_all(partial, ("gx", "gy"), 0, 0, tiled=True)
     shots = now.shape[0]

time: 98.8 us -> 91.4 us (0.925)
  Pallas kernels: 32.7 us -> 27.6 us
  waiting for transfers between devices: 14.7 us -> 11.9 us
    ppermute x2, waiting for transfers between devices: 4.66 us -> 0.01 us  [local(): lax.ppermute(part, ('gx', 'gy'), joint(x_perm, perm, ny))]
    pallas_call x2, Pallas kernels: 3.59 us -> 0.27 us  [pack_corners(): pl.pallas_call(functools.partial(corner_kernel, block_y, parity_y, reach)...]
    ppermute x2, starting transfers between devices: 1.09 us -> 3.99 us  [local(): lax.ppermute(part, ('gx', 'gy'), joint(x_perm, perm, ny))]
    ppermute x2, starting transfers between devices: 5.59 us -> 2.78 us  [local(): speed_x = [lax.ppermute(speed, 'gx', perm) for perm in x_perms]]
    all_to_all x1, waiting for transfers between devices: 1.38 us -> 3.19 us  [local(): lax.all_to_all(picked.reshape(model_tiles.shape), ('sy', 'gx'), 0, 0, til...]
    ppermute x2, waiting for transfers between devices: 2.81 us -> 1.54 us  [swap_corners(): lax.ppermute(part, 'gy', perm)]
    ppermute x2, waiting for transfers between devices: 0.01 us -> 1.22 us  [local(): prev_x = [lax.ppermute(later, 'gx', perm) for perm in x_perms]]
    unnamed x33 -> x15, local copies, waits for them, and re-layouts: 4.75 us -> 5.15 us
where the time goes in v4:
time: 91.4 us; the launch traced here: 91.2 us
  starting transfers between devices  32 us (35%)
  Pallas kernels  27.6 us (30%)
  blocking collectives  12.4 us (14%)
  waiting for transfers between devices  11.9 us (13%)
  local copies, waits for them, and re-layouts  5.16 us (6%)
  between operations  1.48 us (2%)
    pallas_call x1, Pallas kernels, window(): pl.pallas_call(call_with_groups(window_kernel, sizes, (None, None, None,...  17.6 us
    all_to_all x1, blocking collectives, local(): gathered = lax.all_to_all(partial, ('gx', 'gy'), 0, 0, tiled=True)  12.4 us
    all_to_all x1, starting transfers between devices, local(): spread = lax.all_to_all(model_tiles, ('sy', 'gx'), 0, 0, tiled=True)  7.29 us
    ppermute x2, starting transfers between devices, local(): now_x = [lax.ppermute(now, 'gx', perm) for perm in x_perms]  5.45 us
    unnamed x15, local copies, waits for them, and re-layouts  5.15 us
    all_to_all x1, starting transfers between devices, local(): lax.all_to_all(picked.reshape(model_tiles.shape), ('sy', 'gx'), 0, 0, til...  4.2 us
    ppermute x2, starting transfers between devices, local(): lax.ppermute(part, ('gx', 'gy'), joint(x_perm, perm, ny))  3.99 us
    pallas_call x1, Pallas kernels, list_receivers(): pl.pallas_call(functools.partial(list_kernel, block_x, block_y), out_shap...  3.8 us
  transfers between devices with their start and end apart: 16, of which 7 were waited for; matrix products, arithmetic and copies ran while one was open for 1% of the time, Pallas kernels for 11%

profile of v4, /device:TPU:0, one launch (start us, length us, event | category | flops | bytes accessed | tf_op | source)
XLA Modules:
  0.0 91.2 jit_solution(13291088268292010559)
XLA Ops:
  0.6 7.3 %all-to-all-start = ((f32[16,32,128]{2,1,0:T(8,128)}), f32[16,32,128]{2,1,0:T(8,128)S(1)}, u32[]{:S(2)}, u32[]{:S(2)}) async-start(f32[16,32,128]{2,1,0:T(8,128)} %param.8), calls=%async_computation | async-start | bytes 524288 | tf_op jit(solution)/shard_map/all_to_all | solution.py:527
  7.9 1.0 %copy-done = f32[1,2,16,32,128]{4,3,2,1,0:T(8,128)S(1)} copy-done((f32[1,2,16,32,128]{4,3,2,1,0:T(8,128)S(1)}, f32[1,2,16,32,128]{4,3,2,1,0:T(8,128)}, u32[]{:S(2)}) %copy-start) | copy-done | bytes 524312
  9.0 1.0 %pack_sides.1 = f32[2,2,16,16,128]{4,3,2,1,0:T(8,128)S(1)} custom-call(f32[2,16,32,128]{3,2,1,0:T(8,128)} %bitcast.2.now.refs_0_, f32[2,16,32,128]{3,2,1,0:T(8,128)S(1)} %bitcast.21), custom_call_target="tpu_custom_call" | custom-call | tf_op jit(solution)/shard_map/pack_sides/pallas_call | solution.py:174
  10.0 1.6 %collective-permute-start.4 = (f32[2,2,16,16,128]{4,3,2,1,0:T(8,128)S(1)}, f32[2,2,16,16,128]{4,3,2,1,0:T(8,128)S(1)}, u32[]{:S(2)}, u32[]{:S(2)}) collective-permute-start(f32[2,2,16,16,128]{4,3,2,1,0:T(8,128)S(1)} %pack_sides.1), channel_id=1, source_target_pairs={{0,1},{1,0},{2,3},{3,2},{4,5},{5,4},{6,7},{7,6},{8,9},{9,8},{10,11... | collective-permute-start | bytes 1572872 | tf_op jit(solution)/shard_map/ppermute | solution.py:534
  11.5 0.7 collective-permute-start.3
  12.2 4.8 %collective-permute-start.2 = (f32[2,16,32,128]{3,2,1,0:T(8,128)}, f32[2,16,32,128]{3,2,1,0:T(8,128)S(1)}, u32[]{:S(2)}, u32[]{:S(2)}) collective-permute-start(f32[2,16,32,128]{3,2,1,0:T(8,128)} %bitcast.2.now.refs_0_), channel_id=1, source_target_pairs={{0,2},{2,0},{4,6},{6,4},{1,3},{3,1},{5,7},{7,5},{8,10},{10,8},{12,... | collective-permute-start | bytes 1572872 | tf_op jit(solution)/shard_map/ppermute | solution.py:528
  17.0 1.5 %collective-permute-start = (s32[1]{0:T(128)}, s32[1]{0:T(128)}, u32[]{:S(2)}, u32[]{:S(2)}) collective-permute-start(s32[1]{0:T(128)} %param.10), channel_id=1, source_target_pairs={{0,16},{16,0},{1,17},{17,1},{2,18},{18,2},{3,19},{19,3},{4,20},{20... | collective-permute-start | bytes 20 | tf_op jit(solution)/shard_map/ppermute | solution.py:531
  18.4 2.2 %collective-permute-done.refs_1_ = s32[1]{0:T(128)} collective-permute-done((s32[1]{0:T(128)}, s32[1]{0:T(128)}, u32[]{:S(2)}, u32[]{:S(2)}) %collective-permute-start) | collective-permute-done | bytes 36 | tf_op jit(solution)/shard_map/ppermute | solution.py:531
  20.6 0.7 collective-permute-start.6
  21.3 0.8 collective-permute-done.1
  22.1 1.1 %collective-permute-start.5 = (f32[2,16,32,128]{3,2,1,0:T(8,128)}, f32[2,16,32,128]{3,2,1,0:T(8,128)S(1)}, u32[]{:S(2)}, u32[]{:S(2)}) collective-permute-start(f32[2,16,32,128]{3,2,1,0:T(8,128)} %bitcast.20), channel_id=1, source_target_pairs={{0,2},{2,0},{4,6},{6,4},{1,3},{3,1},{5,7},{7,5},{8,10},{10,8},{12,... | collective-permute-start | bytes 1572872 | tf_op jit(solution)/shard_map/ppermute | solution.py:537
  23.9 0.6 copy-done.6
  24.6 2.5 %pick_slices.1 = f32[8,2,32,128]{3,2,1,0:T(8,128)} custom-call(s32[16]{0:T(128)S(1)} %copy-done.6, s32[1]{0:T(128)S(6)} %copy.16.refs_0_, s32[1]{0:T(128)} %collective-permute-done.refs_1_, f32[8,2,32,128]{3,2,1,0:T(8,128)S(1)} %bitcast.23, f32[8,2,32,128]{3,2,1,0:T(8,128)S(1)} %bitcast.24), custom_call_target="tpu_custom_call" | custom-call | tf_op jit(solution)/shard_map/pick_slices/pallas_call | solution.py:102
  27.1 3.0 %collective-permute-done.2.first.refs_2_ = f32[2,16,32,128]{3,2,1,0:T(8,128)S(1)} collective-permute-done((f32[2,16,32,128]{3,2,1,0:T(8,128)}, f32[2,16,32,128]{3,2,1,0:T(8,128)S(1)}, u32[]{:S(2)}, u32[]{:S(2)}) %collective-permute-start.2) | collective-permute-done | bytes 524320 | tf_op jit(solution)/shard_map/ppermute | solution.py:528
  30.0 4.2 %all-to-all-start.1 = ((f32[16,32,128]{2,1,0:T(8,128)}), f32[16,32,128]{2,1,0:T(8,128)S(1)}, u32[]{:S(2)}, u32[]{:S(2)}) async-start(f32[16,32,128]{2,1,0:T(8,128)} %bitcast.6), calls=%async_computation.1 | async-start | bytes 524288 | tf_op jit(solution)/shard_map/all_to_all | solution.py:553
  35.0 0.7 copy.14
  35.7 3.8 %list_receivers.1.refs_2_ = s32[788]{0:T(1024)S(1)} custom-call(s32[3,256]{1,0:T(4,128)S(1)} %bitcast.25), custom_call_target="tpu_custom_call" | custom-call | tf_op jit(solution)/shard_map/list_receivers/pallas_call | solution.py:70
  39.5 1.2 %collective-permute-done.5.first.refs_4_ = f32[2,16,32,128]{3,2,1,0:T(8,128)S(1)} collective-permute-done((f32[2,16,32,128]{3,2,1,0:T(8,128)}, f32[2,16,32,128]{3,2,1,0:T(8,128)S(1)}, u32[]{:S(2)}, u32[]{:S(2)}) %collective-permute-start.5) | collective-permute-done | bytes 524320 | tf_op jit(solution)/shard_map/ppermute | solution.py:537
  40.7 1.2 %collective-permute-done.7.refs_7_ = f32[2,2,11,16,128]{4,3,2,1,0:T(8,128)S(1)} collective-permute-done((f32[2,2,11,16,128]{4,3,2,1,0:T(8,128)S(1)}, f32[2,2,11,16,128]{4,3,2,1,0:T(8,128)S(1)}, u32[]{:S(2)}, u32[]{:S(2)}) %collective-permute-start.7) | collective-permute-done | bytes 360480 | tf_op jit(solution)/shard_map/ppermute | solution.py:544
  41.9 0.7 copy-done.2
  42.6 3.2 %all-to-all-done.1.refs_4_ = f32[16,32,128]{2,1,0:T(8,128)S(1)} async-done(((f32[16,32,128]{2,1,0:T(8,128)}), f32[16,32,128]{2,1,0:T(8,128)S(1)}, u32[]{:S(2)}, u32[]{:S(2)}) %all-to-all-start.1) | async-done | bytes 262176 | tf_op jit(solution)/shard_map/all_to_all | solution.py:553
  45.9 1.6 %collective-permute-start.8 = (f32[2,2,9,16,128]{4,3,2,1,0:T(8,128)S(1)}, f32[2,2,9,16,128]{4,3,2,1,0:T(8,128)}, u32[]{:S(2)}, u32[]{:S(2)}) collective-permute-start(f32[2,2,9,16,128]{4,3,2,1,0:T(8,128)S(1)} %pack_corners.3), channel_id=1, source_target_pairs={{0,1},{1,0},{2,3},{3,2},{4,5},{5,4},{6,7},{7,6},{8,9},{9,8},{10,11... | collective-permute-start | bytes 884744 | tf_op jit(solution)/shard_map/ppermute | solution.py:544
  47.5 1.3 %collective-permute-start.10 = (f32[16,32,128]{2,1,0:T(8,128)S(1)}, f32[16,32,128]{2,1,0:T(8,128)}, u32[]{:S(2)}, u32[]{:S(2)}) collective-permute-start(f32[16,32,128]{2,1,0:T(8,128)S(1)} %all-to-all-done.1.refs_4_), channel_id=1, source_target_pairs={{2,4},{4,2},{3,5},{5,3},{10,12},{12,10},{11,13},{13,11},{18,20},{2... | collective-permute-start | bytes 786440 | tf_op jit(solution)/shard_map/ppermute | solution.py:556
  48.8 1.4 %collective-permute-start.9 = (f32[16,32,128]{2,1,0:T(8,128)S(1)}, f32[16,32,128]{2,1,0:T(8,128)}, u32[]{:S(2)}, u32[]{:S(2)}) collective-permute-start(f32[16,32,128]{2,1,0:T(8,128)S(1)} %all-to-all-done.1.refs_4_), channel_id=1, source_target_pairs={{0,2},{2,0},{4,6},{6,4},{1,3},{3,1},{5,7},{7,5},{8,10},{10,8},{12,... | collective-permute-start | bytes 786440 | tf_op jit(solution)/shard_map/ppermute | solution.py:556
  50.3 0.7 collective-permute-start.13
  51.0 3.3 %collective-permute-start.12 = (f32[16,16,128]{2,1,0:T(8,128)S(1)}, f32[16,16,128]{2,1,0:T(8,128)S(1)}, u32[]{:S(2)}, u32[]{:S(2)}) collective-permute-start(f32[16,16,128]{2,1,0:T(8,128)S(1)} %constant_dynamic-slice_fusion), channel_id=1, source_target_pairs={{0,3},{1,2},{2,1},{3,0},{4,7},{5,6},{6,5},{7,4},{8,11},{9,10},{10,... | collective-permute-start | bytes 393224 | tf_op jit(solution)/shard_map/ppermute | solution.py:562
  54.6 1.3 %collective-permute-start.11 = (f32[16,16,128]{2,1,0:T(8,128)S(1)}, f32[16,16,128]{2,1,0:T(8,128)S(1)}, u32[]{:S(2)}, u32[]{:S(2)}) collective-permute-start(f32[16,16,128]{2,1,0:T(8,128)S(1)} %constant_dynamic-slice_fusion), channel_id=1, source_target_pairs={{0,1},{1,0},{2,3},{3,2},{4,5},{5,4},{6,7},{7,6},{8,9},{9,8},{10,11... | collective-permute-start | bytes 393224 | tf_op jit(solution)/shard_map/ppermute | solution.py:561
  56.0 1.0 %copy-done.1 = f32[1,2,16,32,128]{4,3,2,1,0:T(8,128)S(1)} copy-done((f32[1,2,16,32,128]{4,3,2,1,0:T(8,128)S(1)}, f32[1,2,16,32,128]{4,3,2,1,0:T(8,128)}, u32[]{:S(2)}) %copy-start.1) | copy-done | bytes 524312
  57.0 1.0 %copy-done.3 = f32[2,2,11,16,128]{4,3,2,1,0:T(8,128)S(1)} copy-done((f32[2,2,11,16,128]{4,3,2,1,0:T(8,128)S(1)}, f32[2,2,11,16,128]{4,3,2,1,0:T(8,128)}, u32[]{:S(2)}) %copy-start.3) | copy-done | bytes 360472
  58.0 2.4 %assemble_fields.1.refs_3_ = f32[6,48,64,128]{3,2,1,0:T(8,128)S(1)} custom-call(f32[2,16,32,128]{3,2,1,0:T(8,128)} %bitcast.2.now.refs_0_, f32[2,16,32,128]{3,2,1,0:T(8,128)S(1)} %bitcast.22, f32[2,16,32,128]{3,2,1,0:T(8,128)S(1)} %collective-permute-done.2.first.refs_2_, f32[2,16,32,128]{3,2,1,0:T(8,128)S(1)} %collective-permute-done.3.second.refs_3_, ...), custom_call_target="tpu_custom_call" | custom-call | tf_op jit(solution)/shard_map/assemble_fields/pallas_call | solution.py:302
  60.5 17.6 %wave_window.1 = (f32[2,16,32,128]{3,2,1,0:T(8,128)}, f32[2,16,32,128]{3,2,1,0:T(8,128)}, f32[8,16,256]{2,1,0:T(8,128)S(1)}, f32[6,48,64,128]{3,2,1,0:T(8,128)S(1)}) custom-call(s32[2,3]{1,0:T(2,128)S(1)} %bitcast.26, f32[2,8]{1,0:T(2,128)S(1)} %bitcast.27, s32[788]{0:T(1024)S(1)} %list_receivers.1.refs_2_, ...), custom_call_target="tpu_custom_call", output_to_operand_aliasing={{3}: (3, {})} | custom-call | tf_op jit(solution)/shard_map/wave_window/pallas_call | solution.py:498
  78.2 12.4 %all_to_all.15 = f32[8,16,256]{2,1,0:T(8,128)S(1)} all-to-all(f32[8,16,256]{2,1,0:T(8,128)S(1)} %get-tuple-element.34), channel_id=1, replica_groups=mesh['sy'=2,'core'=2,'gx'=4,'gy'=2] {'gx','gy'}, dimensions={0} | all-to-all | bytes 262144 | tf_op jit(solution)/shard_map/all_to_all | solution.py:570
  (25 shorter events, 1.9 us)
Async XLA Ops:
  0.6 20.0 %all-to-all-start = ((f32[16,32,128]{2,1,0:T(8,128)}), f32[16,32,128]{2,1,0:T(8,128)S(1)}, u32[]{:S(2)}, u32[]{:S(2)}) async-start(f32[16,32,128]{2,1,0:T(8,128)} %param.8), calls=%async_computation | async-start | bytes 524288 | tf_op jit(solution)/shard_map/all_to_all | solution.py:527
  7.9 1.0 %copy-start = (f32[1,2,16,32,128]{4,3,2,1,0:T(8,128)S(1)}, f32[1,2,16,32,128]{4,3,2,1,0:T(8,128)}, u32[]{:S(2)}) copy-start(f32[1,2,16,32,128]{4,3,2,1,0:T(8,128)} %param.12) | copy-start | bytes 1572868
  9.9 50.6 %copy-start.4 = (s32[1,2,3]{2,1,0:T(2,128)S(1)}, s32[1,2,3]{2,1,0:T(2,128)}, u32[]{:S(2)}) copy-start(s32[1,2,3]{2,1,0:T(2,128)} %param.13) | copy-start | bytes 76
  10.0 50.6 %copy-start.5 = (f32[1,2,8]{2,1,0:T(2,128)S(1)}, f32[1,2,8]{2,1,0:T(2,128)}, u32[]{:S(2)}) copy-start(f32[1,2,8]{2,1,0:T(2,128)} %param.14) | copy-start | bytes 196
  10.0 17.1 %collective-permute-start.4 = (f32[2,2,16,16,128]{4,3,2,1,0:T(8,128)S(1)}, f32[2,2,16,16,128]{4,3,2,1,0:T(8,128)S(1)}, u32[]{:S(2)}, u32[]{:S(2)}) collective-permute-start(f32[2,2,16,16,128]{4,3,2,1,0:T(8,128)S(1)} %pack_sides.1), channel_id=1, source_target_pairs={{0,1},{1,0},{2,3},{3,2},{4,5},{5,4},{6,7},{7,6},{8,9},{9,8},{10,11... | collective-permute-start | bytes 1572872 | tf_op jit(solution)/shard_map/ppermute | solution.py:534
  11.5 15.5 %collective-permute-start.3 = (f32[2,16,32,128]{3,2,1,0:T(8,128)}, f32[2,16,32,128]{3,2,1,0:T(8,128)S(1)}, u32[]{:S(2)}, u32[]{:S(2)}) collective-permute-start(f32[2,16,32,128]{3,2,1,0:T(8,128)} %bitcast.2.now.refs_0_), channel_id=1, source_target_pairs={{2,4},{4,2},{3,5},{5,3},{10,12},{12,10},{11,13},{13,11},{18,20},{2... | collective-permute-start | bytes 1572872 | tf_op jit(solution)/shard_map/ppermute | solution.py:528
  12.2 17.8 %collective-permute-start.2 = (f32[2,16,32,128]{3,2,1,0:T(8,128)}, f32[2,16,32,128]{3,2,1,0:T(8,128)S(1)}, u32[]{:S(2)}, u32[]{:S(2)}) collective-permute-start(f32[2,16,32,128]{3,2,1,0:T(8,128)} %bitcast.2.now.refs_0_), channel_id=1, source_target_pairs={{0,2},{2,0},{4,6},{6,4},{1,3},{3,1},{5,7},{7,5},{8,10},{10,8},{12,... | collective-permute-start | bytes 1572872 | tf_op jit(solution)/shard_map/ppermute | solution.py:528
  17.0 3.6 %collective-permute-start = (s32[1]{0:T(128)}, s32[1]{0:T(128)}, u32[]{:S(2)}, u32[]{:S(2)}) collective-permute-start(s32[1]{0:T(128)} %param.10), channel_id=1, source_target_pairs={{0,16},{16,0},{1,17},{17,1},{2,18},{18,2},{3,19},{19,3},{4,20},{20... | collective-permute-start | bytes 20 | tf_op jit(solution)/shard_map/ppermute | solution.py:531
  20.6 1.5 %collective-permute-start.1 = (f32[16,32,128]{2,1,0:T(8,128)S(1)}, f32[16,32,128]{2,1,0:T(8,128)S(1)}, u32[]{:S(2)}, u32[]{:S(2)}) collective-permute-start(f32[16,32,128]{2,1,0:T(8,128)S(1)} %all-to-all-done), channel_id=1, source_target_pairs={{0,8},{8,0},{1,9},{9,1},{2,10},{10,2},{3,11},{11,3},{4,12},{12,4},... | collective-permute-start | bytes 786440 | tf_op jit(solution)/shard_map/ppermute | solution.py:536
  20.6 18.9 %collective-permute-start.6 = (f32[2,16,32,128]{3,2,1,0:T(8,128)}, f32[2,16,32,128]{3,2,1,0:T(8,128)S(1)}, u32[]{:S(2)}, u32[]{:S(2)}) collective-permute-start(f32[2,16,32,128]{3,2,1,0:T(8,128)} %bitcast.19), channel_id=1, source_target_pairs={{2,4},{4,2},{3,5},{5,3},{10,12},{12,10},{11,13},{13,11},{18,20},{2... | collective-permute-start | bytes 1572872 | tf_op jit(solution)/shard_map/ppermute | solution.py:537
  22.1 18.6 %collective-permute-start.5 = (f32[2,16,32,128]{3,2,1,0:T(8,128)}, f32[2,16,32,128]{3,2,1,0:T(8,128)S(1)}, u32[]{:S(2)}, u32[]{:S(2)}) collective-permute-start(f32[2,16,32,128]{3,2,1,0:T(8,128)} %bitcast.20), channel_id=1, source_target_pairs={{0,2},{2,0},{4,6},{6,4},{1,3},{3,1},{5,7},{7,5},{8,10},{10,8},{12,... | collective-permute-start | bytes 1572872 | tf_op jit(solution)/shard_map/ppermute | solution.py:537
  23.9 0.7 copy-start.6
  30.0 15.8 %all-to-all-start.1 = ((f32[16,32,128]{2,1,0:T(8,128)}), f32[16,32,128]{2,1,0:T(8,128)S(1)}, u32[]{:S(2)}, u32[]{:S(2)}) async-start(f32[16,32,128]{2,1,0:T(8,128)} %bitcast.6), calls=%async_computation.1 | async-start | bytes 524288 | tf_op jit(solution)/shard_map/all_to_all | solution.py:553
  34.4 7.5 %collective-permute-start.7 = (f32[2,2,11,16,128]{4,3,2,1,0:T(8,128)S(1)}, f32[2,2,11,16,128]{4,3,2,1,0:T(8,128)S(1)}, u32[]{:S(2)}, u32[]{:S(2)}) collective-permute-start(f32[2,2,11,16,128]{4,3,2,1,0:T(8,128)S(1)} %pack_corners.2), channel_id=1, source_target_pairs={{0,1},{1,0},{2,3},{3,2},{4,5},{5,4},{6,7},{7,6},{8,9},{9,8},{10,11... | collective-permute-start | bytes 1081352 | tf_op jit(solution)/shard_map/ppermute | solution.py:544
  41.9 0.7 copy-start.2
  45.9 8.7 %collective-permute-start.8 = (f32[2,2,9,16,128]{4,3,2,1,0:T(8,128)S(1)}, f32[2,2,9,16,128]{4,3,2,1,0:T(8,128)}, u32[]{:S(2)}, u32[]{:S(2)}) collective-permute-start(f32[2,2,9,16,128]{4,3,2,1,0:T(8,128)S(1)} %pack_corners.3), channel_id=1, source_target_pairs={{0,1},{1,0},{2,3},{3,2},{4,5},{5,4},{6,7},{7,6},{8,9},{9,8},{10,11... | collective-permute-start | bytes 884744 | tf_op jit(solution)/shard_map/ppermute | solution.py:544
  47.5 13.0 %collective-permute-start.10 = (f32[16,32,128]{2,1,0:T(8,128)S(1)}, f32[16,32,128]{2,1,0:T(8,128)}, u32[]{:S(2)}, u32[]{:S(2)}) collective-permute-start(f32[16,32,128]{2,1,0:T(8,128)S(1)} %all-to-all-done.1.refs_4_), channel_id=1, source_target_pairs={{2,4},{4,2},{3,5},{5,3},{10,12},{12,10},{11,13},{13,11},{18,20},{2... | collective-permute-start | bytes 786440 | tf_op jit(solution)/shard_map/ppermute | solution.py:556
  48.8 11.7 %collective-permute-start.9 = (f32[16,32,128]{2,1,0:T(8,128)S(1)}, f32[16,32,128]{2,1,0:T(8,128)}, u32[]{:S(2)}, u32[]{:S(2)}) collective-permute-start(f32[16,32,128]{2,1,0:T(8,128)S(1)} %all-to-all-done.1.refs_4_), channel_id=1, source_target_pairs={{0,2},{2,0},{4,6},{6,4},{1,3},{3,1},{5,7},{7,5},{8,10},{10,8},{12,... | collective-permute-start | bytes 786440 | tf_op jit(solution)/shard_map/ppermute | solution.py:556
  50.3 10.2 %collective-permute-start.13 = (f32[16,16,128]{2,1,0:T(8,128)S(1)}, f32[16,16,128]{2,1,0:T(8,128)S(1)}, u32[]{:S(2)}, u32[]{:S(2)}) collective-permute-start(f32[16,16,128]{2,1,0:T(8,128)S(1)} %constant_dynamic-slice_fusion), channel_id=1, source_target_pairs={{2,5},{3,4},{4,3},{5,2},{10,13},{11,12},{12,11},{13,10},{18,21},{1... | collective-permute-start | bytes 393224 | tf_op jit(solution)/shard_map/ppermute | solution.py:562
  51.0 9.5 %collective-permute-start.12 = (f32[16,16,128]{2,1,0:T(8,128)S(1)}, f32[16,16,128]{2,1,0:T(8,128)S(1)}, u32[]{:S(2)}, u32[]{:S(2)}) collective-permute-start(f32[16,16,128]{2,1,0:T(8,128)S(1)} %constant_dynamic-slice_fusion), channel_id=1, source_target_pairs={{0,3},{1,2},{2,1},{3,0},{4,7},{5,6},{6,5},{7,4},{8,11},{9,10},{10,... | collective-permute-start | bytes 393224 | tf_op jit(solution)/shard_map/ppermute | solution.py:562
  54.6 5.8 %collective-permute-start.11 = (f32[16,16,128]{2,1,0:T(8,128)S(1)}, f32[16,16,128]{2,1,0:T(8,128)S(1)}, u32[]{:S(2)}, u32[]{:S(2)}) collective-permute-start(f32[16,16,128]{2,1,0:T(8,128)S(1)} %constant_dynamic-slice_fusion), channel_id=1, source_target_pairs={{0,1},{1,0},{2,3},{3,2},{4,5},{5,4},{6,7},{7,6},{8,9},{9,8},{10,11... | collective-permute-start | bytes 393224 | tf_op jit(solution)/shard_map/ppermute | solution.py:561
  56.0 1.0 %copy-start.1 = (f32[1,2,16,32,128]{4,3,2,1,0:T(8,128)S(1)}, f32[1,2,16,32,128]{4,3,2,1,0:T(8,128)}, u32[]{:S(2)}) copy-start(f32[1,2,16,32,128]{4,3,2,1,0:T(8,128)} %param.12) | copy-start | bytes 1572868
  57.0 1.0 %copy-start.3 = (f32[2,2,11,16,128]{4,3,2,1,0:T(8,128)S(1)}, f32[2,2,11,16,128]{4,3,2,1,0:T(8,128)}, u32[]{:S(2)}) copy-start(f32[2,2,11,16,128]{4,3,2,1,0:T(8,128)} %copy-done.2) | copy-start | bytes 1081348

commit v5 on v4

--- a/solution.py
+++ b/solution.py
@@ -14,7 +14,7 @@
 HALF = HALO // 2
 REACH_NOW = (HALF - 1, HALF)
 REACH_PREV = (HALF - 3, HALF)
-GROUP = 4
+WIDEST = 10
 BATCH = 4
 
 near_weight = 4.0 / 3.0
@@ -26,6 +26,10 @@
 ANY = pl.BlockSpec(memory_space=pl.ANY)
 SMALL = 4 * 2**20
 VMEM = pl.BlockSpec(memory_space=pltpu.VMEM)
+
+
+def in_hbm(array):
+    return pltpu.with_memory_space_constraint(array, pltpu.HBM)
 
 
 def pairs(count, parity):
@@ -171,6 +175,7 @@
 
 def pack_sides(parity_y, now, prev):
     shots, block_x, block_y, depth = now.shape
+    now, prev = in_hbm(now), in_hbm(prev)
     return pl.pallas_call(
         functools.partial(side_kernel, block_y, parity_y),
         out_shape=jax.ShapeDtypeStruct((2, shots, block_x, HALO, depth), jnp.float32),
@@ -298,7 +303,7 @@
     planes = block_x + 2 * HALO
     rows = block_y + (HALO if ny == 2 else 2 * HALO) + 2 * PAD
     count = len(sides)
-    parts = [now, prev, *now_x, *prev_x, *sides, *corners[0], *corners[1]]
+    parts = [in_hbm(now), in_hbm(prev), *now_x, *prev_x, *sides, *corners[0], *corners[1]]
     return pl.pallas_call(
         call_with_groups(assemble_kernel, sizes, (None, None, 2, 2, count, count, count)),
         out_shape=pltpu.VMEM((2 * shots + 2, planes, rows, depth), jnp.float32),
@@ -386,50 +391,51 @@
 
         size = 8 * tiles
 
-        def plane(g, _, cur=cur, old=old, first=first, tiles=tiles, step=step):
-            x = 2 * step + GROUP * g
+        def some(g, _, at_x, size_x, first, tiles, cur=cur, old=old):
+            x = at_x + size_x * g
             for j0 in range(0, tiles, 3):
                 sub = min(3, tiles - j0)
                 size = 8 * sub
                 start = pl.multiple_of(first + 8 * j0, 8)
                 along = []
                 for s in range(shots):
-                    c = cur[s, pl.ds(x, GROUP), pl.ds(start, size)].reshape(GROUP * size, depth)
+                    c = cur[s, pl.ds(x, size_x), pl.ds(start, size)].reshape(size_x * size, depth)
                     head = c.astype(jnp.bfloat16)
                     rest = (c - head.astype(jnp.float32)).astype(jnp.bfloat16)
                     parts = jnp.concatenate([head, rest], axis=1)
                     out = jnp.dot(parts, band, preferred_element_type=jnp.float32)
-                    along.append(out.reshape(GROUP, size, depth))
+                    along.append(out.reshape(size_x, size, depth))
                 for j in range(sub):
                     base = start + 8 * j
                     at = pl.ds(pl.multiple_of(base, 8), 8)
-                    n = [near[x + i, at] for i in range(GROUP)]
-                    a = [twice[x + i, at] for i in range(GROUP)]
+                    n = [near[x + i, at] for i in range(size_x)]
+                    a = [twice[x + i, at] for i in range(size_x)]
                     for s in range(shots):
-                        c = [cur[s, x + i - 2, at] for i in range(GROUP + 4)]
+                        c = [cur[s, x + i - 2, at] for i in range(size_x + 4)]
                         out = []
-                        for i in range(GROUP):
+                        for i in range(size_x):
                             m = c[i + 2]
                             close = (c[i + 1] + c[i + 3]) + (cur[s, x + i, pl.ds(base - 1, 8)] + cur[s, x + i, pl.ds(base + 1, 8)])
                             wide = (c[i] + c[i + 4]) + (cur[s, x + i, pl.ds(base - 2, 8)] + cur[s, x + i, pl.ds(base + 2, 8)])
                             p = old[s, x + i, at]
                             lap = along[s][i, 8 * j : 8 * j + 8] + close + far_part * wide
                             out.append(p + a[i] * (m - p) + n[i] * lap)
-                        for i in range(GROUP):
+                        for i in range(size_x):
                             old[s, x + i, at] = out[i]
             return 0
 
-        count = (planes - 4 * step) // GROUP
-        edge = 2 if side == 2 else 0
+        def sweep(at_x, count, first, tiles):
+            size_x = max(n for n in range(1, WIDEST + 1) if count % n == 0)
+            part = functools.partial(some, at_x=at_x, size_x=size_x, first=first, tiles=tiles)
+            lax.fori_loop(0, count // size_x, part, 0)
+
+        edge = 8 if side == 2 else 0
         if edge:
-            cut = functools.partial(
-                plane,
-                first=pl.multiple_of(own - 8 * (odd_y if ny == 2 else 1), 8),
-                tiles=tiles - (1 if ny == 2 else 2),
-            )
-            lax.fori_loop(0, edge, cut, 0)
-            lax.fori_loop(count - edge, count, cut, 0)
-        lax.fori_loop(edge, count - edge, plane, 0)
+            near_first = pl.multiple_of(own - 8 * (odd_y if ny == 2 else 1), 8)
+            near_tiles = tiles - (1 if ny == 2 else 2)
+            sweep(2 * step, edge, near_first, near_tiles)
+            sweep(planes - 2 * step - edge, edge, near_first, near_tiles)
+        sweep(2 * step + edge, planes - 4 * step - 2 * edge, first, tiles)
 
         for s in range(shots):
             sx = sources[s, 0] - x_first

time: 91.4 us -> 88.9 us (0.973)
  local copies, waits for them, and re-layouts: 5.16 us -> 3.08 us
  Pallas kernels: 27.6 us -> 26 us
  waiting for transfers between devices: 11.9 us -> 13.4 us
    unnamed x15 -> x11, local copies, waits for them, and re-layouts: 5.15 us -> 3.07 us
    pallas_call x1, Pallas kernels: 17.6 us -> 16 us  [window(): pl.pallas_call(call_with_groups(window_kernel, sizes, (None, None, None,...]
  transfers between devices with their start and end apart: 16 -> 16, of which waited for: 7 -> 8; matrix products, arithmetic and copies ran while one was open for 1% -> 1% of each run, Pallas kernels for 11% -> 11%
where the time goes in v5:
time: 88.9 us; the launch traced here: 88.1 us
  starting transfers between devices  32 us (36%)
  Pallas kernels  26 us (29%)
  waiting for transfers between devices  13.4 us (15%)
  blocking collectives  11.5 us (13%)
  local copies, waits for them, and re-layouts  3.08 us (3%)
  between operations  1.45 us (2%)
    pallas_call x1, Pallas kernels, window(): pl.pallas_call(call_with_groups(window_kernel, sizes, (None, None, None,...  16 us
    all_to_all x1, blocking collectives, local(): gathered = lax.all_to_all(partial, ('gx', 'gy'), 0, 0, tiled=True)  11.5 us
    all_to_all x1, starting transfers between devices, local(): spread = lax.all_to_all(model_tiles, ('sy', 'gx'), 0, 0, tiled=True)  7.29 us
    ppermute x2, starting transfers between devices, local(): now_x = [lax.ppermute(now, 'gx', perm) for perm in x_perms]  5.45 us
    all_to_all x1, starting transfers between devices, local(): lax.all_to_all(picked.reshape(model_tiles.shape), ('sy', 'gx'), 0, 0, til...  4.2 us
    all_to_all x1, waiting for transfers between devices, local(): lax.all_to_all(picked.reshape(model_tiles.shape), ('sy', 'gx'), 0, 0, til...  3.96 us
    ppermute x2, starting transfers between devices, local(): lax.ppermute(part, ('gx', 'gy'), joint(x_perm, perm, ny))  3.84 us
    pallas_call x1, Pallas kernels, list_receivers(): pl.pallas_call(functools.partial(list_kernel, block_x, block_y), out_shap...  3.8 us
  transfers between devices with their start and end apart: 16, of which 8 were waited for; matrix products, arithmetic and copies ran while one was open for 1% of the time, Pallas kernels for 11%

profile of v5, /device:TPU:0, one launch (start us, length us, event | category | flops | bytes accessed | tf_op | source)
XLA Modules:
  0.0 88.1 jit_solution(16391556445603178214)
XLA Ops:
  0.6 7.3 %all-to-all-start = ((f32[16,32,128]{2,1,0:T(8,128)}), f32[16,32,128]{2,1,0:T(8,128)S(1)}, u32[]{:S(2)}, u32[]{:S(2)}) async-start(f32[16,32,128]{2,1,0:T(8,128)} %param.8), calls=%async_computation | async-start | bytes 524288 | tf_op jit(solution)/shard_map/all_to_all | solution.py:533
  7.9 1.0 %pack_sides.1 = f32[2,2,16,16,128]{4,3,2,1,0:T(8,128)S(1)} custom-call(f32[2,16,32,128]{3,2,1,0:T(8,128)} %bitcast.24, f32[2,16,32,128]{3,2,1,0:T(8,128)} %bitcast.28), custom_call_target="tpu_custom_call" | custom-call | tf_op jit(solution)/shard_map/pack_sides/pallas_call | solution.py:179
  9.0 1.6 %collective-permute-start.4 = (f32[2,2,16,16,128]{4,3,2,1,0:T(8,128)S(1)}, f32[2,2,16,16,128]{4,3,2,1,0:T(8,128)S(1)}, u32[]{:S(2)}, u32[]{:S(2)}) collective-permute-start(f32[2,2,16,16,128]{4,3,2,1,0:T(8,128)S(1)} %pack_sides.1), channel_id=1, source_target_pairs={{0,1},{1,0},{2,3},{3,2},{4,5},{5,4},{6,7},{7,6},{8,9},{9,8},{10,11... | collective-permute-start | bytes 1572872 | tf_op jit(solution)/shard_map/ppermute | solution.py:540
  10.6 0.7 collective-permute-start.3
  11.2 4.8 %collective-permute-start.2 = (f32[2,16,32,128]{3,2,1,0:T(8,128)}, f32[2,16,32,128]{3,2,1,0:T(8,128)S(1)}, u32[]{:S(2)}, u32[]{:S(2)}) collective-permute-start(f32[2,16,32,128]{3,2,1,0:T(8,128)} %bitcast.26), channel_id=1, source_target_pairs={{0,2},{2,0},{4,6},{6,4},{1,3},{3,1},{5,7},{7,5},{8,10},{10,8},{12,... | collective-permute-start | bytes 1572872 | tf_op jit(solution)/shard_map/ppermute | solution.py:534
  16.0 1.5 %collective-permute-start = (s32[1]{0:T(128)}, s32[1]{0:T(128)}, u32[]{:S(2)}, u32[]{:S(2)}) collective-permute-start(s32[1]{0:T(128)} %param.10), channel_id=1, source_target_pairs={{0,16},{16,0},{1,17},{17,1},{2,18},{18,2},{3,19},{19,3},{4,20},{20... | collective-permute-start | bytes 20 | tf_op jit(solution)/shard_map/ppermute | solution.py:537
  17.5 2.3 %collective-permute-done.refs_1_ = s32[1]{0:T(128)} collective-permute-done((s32[1]{0:T(128)}, s32[1]{0:T(128)}, u32[]{:S(2)}, u32[]{:S(2)}) %collective-permute-start) | collective-permute-done | bytes 36 | tf_op jit(solution)/shard_map/ppermute | solution.py:537
  19.8 0.7 collective-permute-start.6
  20.5 0.8 collective-permute-done.1
  21.3 1.1 %collective-permute-start.5 = (f32[2,16,32,128]{3,2,1,0:T(8,128)}, f32[2,16,32,128]{3,2,1,0:T(8,128)S(1)}, u32[]{:S(2)}, u32[]{:S(2)}) collective-permute-start(f32[2,16,32,128]{3,2,1,0:T(8,128)} %bitcast.30), channel_id=1, source_target_pairs={{0,2},{2,0},{4,6},{6,4},{1,3},{3,1},{5,7},{7,5},{8,10},{10,8},{12,... | collective-permute-start | bytes 1572872 | tf_op jit(solution)/shard_map/ppermute | solution.py:543
  23.1 0.6 copy-done.4
  23.7 2.5 %pick_slices.1 = f32[8,2,32,128]{3,2,1,0:T(8,128)} custom-call(s32[16]{0:T(128)S(1)} %copy-done.4, s32[1]{0:T(128)S(6)} %copy.16.refs_0_, s32[1]{0:T(128)} %collective-permute-done.refs_1_, f32[8,2,32,128]{3,2,1,0:T(8,128)S(1)} %bitcast.19, f32[8,2,32,128]{3,2,1,0:T(8,128)S(1)} %bitcast.20), custom_call_target="tpu_custom_call" | custom-call | tf_op jit(solution)/shard_map/pick_slices/pallas_call | solution.py:106
  26.3 2.8 %collective-permute-done.2.first.refs_2_ = f32[2,16,32,128]{3,2,1,0:T(8,128)S(1)} collective-permute-done((f32[2,16,32,128]{3,2,1,0:T(8,128)}, f32[2,16,32,128]{3,2,1,0:T(8,128)S(1)}, u32[]{:S(2)}, u32[]{:S(2)}) %collective-permute-start.2) | collective-permute-done | bytes 524320 | tf_op jit(solution)/shard_map/ppermute | solution.py:534
  29.1 4.2 %all-to-all-start.1 = ((f32[16,32,128]{2,1,0:T(8,128)}), f32[16,32,128]{2,1,0:T(8,128)S(1)}, u32[]{:S(2)}, u32[]{:S(2)}) async-start(f32[16,32,128]{2,1,0:T(8,128)} %bitcast.6), calls=%async_computation.1 | async-start | bytes 524288 | tf_op jit(solution)/shard_map/all_to_all | solution.py:559
  33.4 0.6 collective-permute-start.7
  34.0 0.7 copy.14
  34.7 3.8 %list_receivers.1.refs_2_ = s32[788]{0:T(1024)S(1)} custom-call(s32[3,256]{1,0:T(4,128)S(1)} %bitcast.21), custom_call_target="tpu_custom_call" | custom-call | tf_op jit(solution)/shard_map/list_receivers/pallas_call | solution.py:74
  38.5 1.5 %collective-permute-done.5.first.refs_4_ = f32[2,16,32,128]{3,2,1,0:T(8,128)S(1)} collective-permute-done((f32[2,16,32,128]{3,2,1,0:T(8,128)}, f32[2,16,32,128]{3,2,1,0:T(8,128)S(1)}, u32[]{:S(2)}, u32[]{:S(2)}) %collective-permute-start.5) | collective-permute-done | bytes 524320 | tf_op jit(solution)/shard_map/ppermute | solution.py:543
  40.0 1.1 %collective-permute-done.7.refs_7_ = f32[2,2,11,16,128]{4,3,2,1,0:T(8,128)S(1)} collective-permute-done((f32[2,2,11,16,128]{4,3,2,1,0:T(8,128)S(1)}, f32[2,2,11,16,128]{4,3,2,1,0:T(8,128)S(1)}, u32[]{:S(2)}, u32[]{:S(2)}) %collective-permute-start.7) | collective-permute-done | bytes 360480 | tf_op jit(solution)/shard_map/ppermute | solution.py:550
  41.1 0.7 copy-done
  41.8 4.0 %all-to-all-done.1.refs_4_ = f32[16,32,128]{2,1,0:T(8,128)S(1)} async-done(((f32[16,32,128]{2,1,0:T(8,128)}), f32[16,32,128]{2,1,0:T(8,128)S(1)}, u32[]{:S(2)}, u32[]{:S(2)}) %all-to-all-start.1) | async-done | bytes 262176 | tf_op jit(solution)/shard_map/all_to_all | solution.py:559
  45.9 1.6 %collective-permute-start.8 = (f32[2,2,9,16,128]{4,3,2,1,0:T(8,128)S(1)}, f32[2,2,9,16,128]{4,3,2,1,0:T(8,128)}, u32[]{:S(2)}, u32[]{:S(2)}) collective-permute-start(f32[2,2,9,16,128]{4,3,2,1,0:T(8,128)S(1)} %pack_corners.3), channel_id=1, source_target_pairs={{0,1},{1,0},{2,3},{3,2},{4,5},{5,4},{6,7},{7,6},{8,9},{9,8},{10,11... | collective-permute-start | bytes 884744 | tf_op jit(solution)/shard_map/ppermute | solution.py:550
  47.5 1.4 %collective-permute-start.10 = (f32[16,32,128]{2,1,0:T(8,128)S(1)}, f32[16,32,128]{2,1,0:T(8,128)}, u32[]{:S(2)}, u32[]{:S(2)}) collective-permute-start(f32[16,32,128]{2,1,0:T(8,128)S(1)} %all-to-all-done.1.refs_4_), channel_id=1, source_target_pairs={{2,4},{4,2},{3,5},{5,3},{10,12},{12,10},{11,13},{13,11},{18,20},{2... | collective-permute-start | bytes 786440 | tf_op jit(solution)/shard_map/ppermute | solution.py:562
  48.8 1.4 %collective-permute-start.9 = (f32[16,32,128]{2,1,0:T(8,128)S(1)}, f32[16,32,128]{2,1,0:T(8,128)}, u32[]{:S(2)}, u32[]{:S(2)}) collective-permute-start(f32[16,32,128]{2,1,0:T(8,128)S(1)} %all-to-all-done.1.refs_4_), channel_id=1, source_target_pairs={{0,2},{2,0},{4,6},{6,4},{1,3},{3,1},{5,7},{7,5},{8,10},{10,8},{12,... | collective-permute-start | bytes 786440 | tf_op jit(solution)/shard_map/ppermute | solution.py:562
  50.3 0.7 collective-permute-start.13
  51.0 3.2 %collective-permute-start.12 = (f32[16,16,128]{2,1,0:T(8,128)S(1)}, f32[16,16,128]{2,1,0:T(8,128)S(1)}, u32[]{:S(2)}, u32[]{:S(2)}) collective-permute-start(f32[16,16,128]{2,1,0:T(8,128)S(1)} %constant_dynamic-slice_fusion), channel_id=1, source_target_pairs={{0,3},{1,2},{2,1},{3,0},{4,7},{5,6},{6,5},{7,4},{8,11},{9,10},{10,... | collective-permute-start | bytes 393224 | tf_op jit(solution)/shard_map/ppermute | solution.py:568
  54.5 1.5 %collective-permute-start.11 = (f32[16,16,128]{2,1,0:T(8,128)S(1)}, f32[16,16,128]{2,1,0:T(8,128)S(1)}, u32[]{:S(2)}, u32[]{:S(2)}) collective-permute-start(f32[16,16,128]{2,1,0:T(8,128)S(1)} %constant_dynamic-slice_fusion), channel_id=1, source_target_pairs={{0,1},{1,0},{2,3},{3,2},{4,5},{5,4},{6,7},{7,6},{8,9},{9,8},{10,11... | collective-permute-start | bytes 393224 | tf_op jit(solution)/shard_map/ppermute | solution.py:567
  56.0 1.0 %copy-done.1 = f32[2,2,11,16,128]{4,3,2,1,0:T(8,128)S(1)} copy-done((f32[2,2,11,16,128]{4,3,2,1,0:T(8,128)S(1)}, f32[2,2,11,16,128]{4,3,2,1,0:T(8,128)}, u32[]{:S(2)}) %copy-start.1) | copy-done | bytes 360472
  57.0 2.4 %assemble_fields.1.refs_3_ = f32[6,48,64,128]{3,2,1,0:T(8,128)S(1)} custom-call(f32[2,16,32,128]{3,2,1,0:T(8,128)} %bitcast.27, f32[2,16,32,128]{3,2,1,0:T(8,128)} %bitcast.31, f32[2,16,32,128]{3,2,1,0:T(8,128)S(1)} %collective-permute-done.2.first.refs_2_, f32[2,16,32,128]{3,2,1,0:T(8,128)S(1)} %collective-permute-done.3.second.refs_3_, ...), custom_call_target="tpu_custom_call" | custom-call | tf_op jit(solution)/shard_map/assemble_fields/pallas_call | solution.py:307
  60.0 16.0 %wave_window.1 = (f32[2,16,32,128]{3,2,1,0:T(8,128)}, f32[2,16,32,128]{3,2,1,0:T(8,128)}, f32[8,16,256]{2,1,0:T(8,128)S(1)}, f32[6,48,64,128]{3,2,1,0:T(8,128)S(1)}) custom-call(s32[2,3]{1,0:T(2,128)S(1)} %bitcast.22, f32[2,8]{1,0:T(2,128)S(1)} %bitcast.23, s32[788]{0:T(1024)S(1)} %list_receivers.1.refs_2_, ...), custom_call_target="tpu_custom_call", output_to_operand_aliasing={{3}: (3, {})} | custom-call | tf_op jit(solution)/shard_map/wave_window/pallas_call | solution.py:504
  76.0 11.5 %all_to_all.15 = f32[8,16,256]{2,1,0:T(8,128)S(1)} all-to-all(f32[8,16,256]{2,1,0:T(8,128)S(1)} %get-tuple-element.34), channel_id=1, replica_groups=mesh['sy'=2,'core'=2,'gx'=4,'gy'=2] {'gx','gy'}, dimensions={0} | all-to-all | bytes 262144 | tf_op jit(solution)/shard_map/all_to_all | solution.py:576
  87.5 0.6 reduce_sum.9
  (21 shorter events, 1.2 us)
Async XLA Ops:
  0.6 19.2 %all-to-all-start = ((f32[16,32,128]{2,1,0:T(8,128)}), f32[16,32,128]{2,1,0:T(8,128)S(1)}, u32[]{:S(2)}, u32[]{:S(2)}) async-start(f32[16,32,128]{2,1,0:T(8,128)} %param.8), calls=%async_computation | async-start | bytes 524288 | tf_op jit(solution)/shard_map/all_to_all | solution.py:533
  9.0 51.0 %copy-start.2 = (s32[1,2,3]{2,1,0:T(2,128)S(1)}, s32[1,2,3]{2,1,0:T(2,128)}, u32[]{:S(2)}) copy-start(s32[1,2,3]{2,1,0:T(2,128)} %param.13) | copy-start | bytes 76
  9.0 51.0 %copy-start.3 = (f32[1,2,8]{2,1,0:T(2,128)S(1)}, f32[1,2,8]{2,1,0:T(2,128)}, u32[]{:S(2)}) copy-start(f32[1,2,8]{2,1,0:T(2,128)} %param.14) | copy-start | bytes 196
  9.0 17.2 %collective-permute-start.4 = (f32[2,2,16,16,128]{4,3,2,1,0:T(8,128)S(1)}, f32[2,2,16,16,128]{4,3,2,1,0:T(8,128)S(1)}, u32[]{:S(2)}, u32[]{:S(2)}) collective-permute-start(f32[2,2,16,16,128]{4,3,2,1,0:T(8,128)S(1)} %pack_sides.1), channel_id=1, source_target_pairs={{0,1},{1,0},{2,3},{3,2},{4,5},{5,4},{6,7},{7,6},{8,9},{9,8},{10,11... | collective-permute-start | bytes 1572872 | tf_op jit(solution)/shard_map/ppermute | solution.py:540
  10.6 15.7 %collective-permute-start.3 = (f32[2,16,32,128]{3,2,1,0:T(8,128)}, f32[2,16,32,128]{3,2,1,0:T(8,128)S(1)}, u32[]{:S(2)}, u32[]{:S(2)}) collective-permute-start(f32[2,16,32,128]{3,2,1,0:T(8,128)} %bitcast.25), channel_id=1, source_target_pairs={{2,4},{4,2},{3,5},{5,3},{10,12},{12,10},{11,13},{13,11},{18,20},{2... | collective-permute-start | bytes 1572872 | tf_op jit(solution)/shard_map/ppermute | solution.py:534
  11.2 17.8 %collective-permute-start.2 = (f32[2,16,32,128]{3,2,1,0:T(8,128)}, f32[2,16,32,128]{3,2,1,0:T(8,128)S(1)}, u32[]{:S(2)}, u32[]{:S(2)}) collective-permute-start(f32[2,16,32,128]{3,2,1,0:T(8,128)} %bitcast.26), channel_id=1, source_target_pairs={{0,2},{2,0},{4,6},{6,4},{1,3},{3,1},{5,7},{7,5},{8,10},{10,8},{12,... | collective-permute-start | bytes 1572872 | tf_op jit(solution)/shard_map/ppermute | solution.py:534
  16.0 3.8 %collective-permute-start = (s32[1]{0:T(128)}, s32[1]{0:T(128)}, u32[]{:S(2)}, u32[]{:S(2)}) collective-permute-start(s32[1]{0:T(128)} %param.10), channel_id=1, source_target_pairs={{0,16},{16,0},{1,17},{17,1},{2,18},{18,2},{3,19},{19,3},{4,20},{20... | collective-permute-start | bytes 20 | tf_op jit(solution)/shard_map/ppermute | solution.py:537
  19.8 1.5 %collective-permute-start.1 = (f32[16,32,128]{2,1,0:T(8,128)S(1)}, f32[16,32,128]{2,1,0:T(8,128)S(1)}, u32[]{:S(2)}, u32[]{:S(2)}) collective-permute-start(f32[16,32,128]{2,1,0:T(8,128)S(1)} %all-to-all-done), channel_id=1, source_target_pairs={{0,8},{8,0},{1,9},{9,1},{2,10},{10,2},{3,11},{11,3},{4,12},{12,4},... | collective-permute-start | bytes 786440 | tf_op jit(solution)/shard_map/ppermute | solution.py:542
  19.8 18.7 %collective-permute-start.6 = (f32[2,16,32,128]{3,2,1,0:T(8,128)}, f32[2,16,32,128]{3,2,1,0:T(8,128)S(1)}, u32[]{:S(2)}, u32[]{:S(2)}) collective-permute-start(f32[2,16,32,128]{3,2,1,0:T(8,128)} %bitcast.29), channel_id=1, source_target_pairs={{2,4},{4,2},{3,5},{5,3},{10,12},{12,10},{11,13},{13,11},{18,20},{2... | collective-permute-start | bytes 1572872 | tf_op jit(solution)/shard_map/ppermute | solution.py:543
  21.3 18.7 %collective-permute-start.5 = (f32[2,16,32,128]{3,2,1,0:T(8,128)}, f32[2,16,32,128]{3,2,1,0:T(8,128)S(1)}, u32[]{:S(2)}, u32[]{:S(2)}) collective-permute-start(f32[2,16,32,128]{3,2,1,0:T(8,128)} %bitcast.30), channel_id=1, source_target_pairs={{0,2},{2,0},{4,6},{6,4},{1,3},{3,1},{5,7},{7,5},{8,10},{10,8},{12,... | collective-permute-start | bytes 1572872 | tf_op jit(solution)/shard_map/ppermute | solution.py:543
  23.1 0.7 copy-start.4
  29.1 16.7 %all-to-all-start.1 = ((f32[16,32,128]{2,1,0:T(8,128)}), f32[16,32,128]{2,1,0:T(8,128)S(1)}, u32[]{:S(2)}, u32[]{:S(2)}) async-start(f32[16,32,128]{2,1,0:T(8,128)} %bitcast.6), calls=%async_computation.1 | async-start | bytes 524288 | tf_op jit(solution)/shard_map/all_to_all | solution.py:559
  33.4 7.7 %collective-permute-start.7 = (f32[2,2,11,16,128]{4,3,2,1,0:T(8,128)S(1)}, f32[2,2,11,16,128]{4,3,2,1,0:T(8,128)S(1)}, u32[]{:S(2)}, u32[]{:S(2)}) collective-permute-start(f32[2,2,11,16,128]{4,3,2,1,0:T(8,128)S(1)} %pack_corners.2), channel_id=1, source_target_pairs={{0,1},{1,0},{2,3},{3,2},{4,5},{5,4},{6,7},{7,6},{8,9},{9,8},{10,11... | collective-permute-start | bytes 1081352 | tf_op jit(solution)/shard_map/ppermute | solution.py:550
  41.1 0.7 copy-start
  45.9 8.5 %collective-permute-start.8 = (f32[2,2,9,16,128]{4,3,2,1,0:T(8,128)S(1)}, f32[2,2,9,16,128]{4,3,2,1,0:T(8,128)}, u32[]{:S(2)}, u32[]{:S(2)}) collective-permute-start(f32[2,2,9,16,128]{4,3,2,1,0:T(8,128)S(1)} %pack_corners.3), channel_id=1, source_target_pairs={{0,1},{1,0},{2,3},{3,2},{4,5},{5,4},{6,7},{7,6},{8,9},{9,8},{10,11... | collective-permute-start | bytes 884744 | tf_op jit(solution)/shard_map/ppermute | solution.py:550
  47.5 12.5 %collective-permute-start.10 = (f32[16,32,128]{2,1,0:T(8,128)S(1)}, f32[16,32,128]{2,1,0:T(8,128)}, u32[]{:S(2)}, u32[]{:S(2)}) collective-permute-start(f32[16,32,128]{2,1,0:T(8,128)S(1)} %all-to-all-done.1.refs_4_), channel_id=1, source_target_pairs={{2,4},{4,2},{3,5},{5,3},{10,12},{12,10},{11,13},{13,11},{18,20},{2... | collective-permute-start | bytes 786440 | tf_op jit(solution)/shard_map/ppermute | solution.py:562
  48.8 11.2 %collective-permute-start.9 = (f32[16,32,128]{2,1,0:T(8,128)S(1)}, f32[16,32,128]{2,1,0:T(8,128)}, u32[]{:S(2)}, u32[]{:S(2)}) collective-permute-start(f32[16,32,128]{2,1,0:T(8,128)S(1)} %all-to-all-done.1.refs_4_), channel_id=1, source_target_pairs={{0,2},{2,0},{4,6},{6,4},{1,3},{3,1},{5,7},{7,5},{8,10},{10,8},{12,... | collective-permute-start | bytes 786440 | tf_op jit(solution)/shard_map/ppermute | solution.py:562
  50.3 9.1 %collective-permute-start.13 = (f32[16,16,128]{2,1,0:T(8,128)S(1)}, f32[16,16,128]{2,1,0:T(8,128)S(1)}, u32[]{:S(2)}, u32[]{:S(2)}) collective-permute-start(f32[16,16,128]{2,1,0:T(8,128)S(1)} %constant_dynamic-slice_fusion), channel_id=1, source_target_pairs={{2,5},{3,4},{4,3},{5,2},{10,13},{11,12},{12,11},{13,10},{18,21},{1... | collective-permute-start | bytes 393224 | tf_op jit(solution)/shard_map/ppermute | solution.py:568
  51.0 8.5 %collective-permute-start.12 = (f32[16,16,128]{2,1,0:T(8,128)S(1)}, f32[16,16,128]{2,1,0:T(8,128)S(1)}, u32[]{:S(2)}, u32[]{:S(2)}) collective-permute-start(f32[16,16,128]{2,1,0:T(8,128)S(1)} %constant_dynamic-slice_fusion), channel_id=1, source_target_pairs={{0,3},{1,2},{2,1},{3,0},{4,7},{5,6},{6,5},{7,4},{8,11},{9,10},{10,... | collective-permute-start | bytes 393224 | tf_op jit(solution)/shard_map/ppermute | solution.py:568
  54.5 5.5 %collective-permute-start.11 = (f32[16,16,128]{2,1,0:T(8,128)S(1)}, f32[16,16,128]{2,1,0:T(8,128)S(1)}, u32[]{:S(2)}, u32[]{:S(2)}) collective-permute-start(f32[16,16,128]{2,1,0:T(8,128)S(1)} %constant_dynamic-slice_fusion), channel_id=1, source_target_pairs={{0,1},{1,0},{2,3},{3,2},{4,5},{5,4},{6,7},{7,6},{8,9},{9,8},{10,11... | collective-permute-start | bytes 393224 | tf_op jit(solution)/shard_map/ppermute | solution.py:567
  56.0 1.0 %copy-start.1 = (f32[2,2,11,16,128]{4,3,2,1,0:T(8,128)S(1)}, f32[2,2,11,16,128]{4,3,2,1,0:T(8,128)}, u32[]{:S(2)}) copy-start(f32[2,2,11,16,128]{4,3,2,1,0:T(8,128)} %copy-done) | copy-start | bytes 1081348

commit v6 on v5

--- a/solution.py
+++ b/solution.py
@@ -486,10 +486,9 @@
                 last_out = copy
 
     total = partial.shape[2]
-    for k in range(shots * STEPS):
-        values = jnp.sum(samples[k, pl.ds(0, total)], axis=1)
-        for copy_to in range(partial.shape[0]):
-            partial[copy_to, k] = values
+    values = jnp.sum(samples[:, pl.ds(0, total)], axis=2)
+    for copy_to in range(partial.shape[0]):
+        partial[copy_to] = values
     first_out.wait()
     last_out.wait()
 

time: 88.9 us -> 88.7 us (level)
  no operation moved by 1% of the time
where the time goes in v6:
time: 88.7 us; the launch traced here: 88.1 us
  starting transfers between devices  32 us (36%)
  Pallas kernels  26 us (29%)
  waiting for transfers between devices  13.4 us (15%)
  blocking collectives  11.5 us (13%)
  local copies, waits for them, and re-layouts  3.08 us (3%)
  between operations  1.45 us (2%)
    pallas_call x1, Pallas kernels, window(): pl.pallas_call(call_with_groups(window_kernel, sizes, (None, None, None,...  16 us
    all_to_all x1, blocking collectives, local(): gathered = lax.all_to_all(partial, ('gx', 'gy'), 0, 0, tiled=True)  11.5 us
    all_to_all x1, starting transfers between devices, local(): spread = lax.all_to_all(model_tiles, ('sy', 'gx'), 0, 0, tiled=True)  7.29 us
    ppermute x2, starting transfers between devices, local(): now_x = [lax.ppermute(now, 'gx', perm) for perm in x_perms]  5.45 us
    all_to_all x1, starting transfers between devices, local(): lax.all_to_all(picked.reshape(model_tiles.shape), ('sy', 'gx'), 0, 0, til...  4.2 us
    all_to_all x1, waiting for transfers between devices, local(): lax.all_to_all(picked.reshape(model_tiles.shape), ('sy', 'gx'), 0, 0, til...  3.96 us
    ppermute x2, starting transfers between devices, local(): lax.ppermute(part, ('gx', 'gy'), joint(x_perm, perm, ny))  3.84 us
    pallas_call x1, Pallas kernels, list_receivers(): pl.pallas_call(functools.partial(list_kernel, block_x, block_y), out_shap...  3.8 us
  transfers between devices with their start and end apart: 16, of which 8 were waited for; matrix products, arithmetic and copies ran while one was open for 1% of the time, Pallas kernels for 11%

profile of v6, /device:TPU:0, one launch (start us, length us, event | category | flops | bytes accessed | tf_op | source)
XLA Modules:
  0.0 88.1 jit_solution(5554744597448496830)
XLA Ops:
  0.6 7.3 %all-to-all-start = ((f32[16,32,128]{2,1,0:T(8,128)}), f32[16,32,128]{2,1,0:T(8,128)S(1)}, u32[]{:S(2)}, u32[]{:S(2)}) async-start(f32[16,32,128]{2,1,0:T(8,128)} %param.8), calls=%async_computation | async-start | bytes 524288 | tf_op jit(solution)/shard_map/all_to_all | solution.py:532
  7.9 1.0 %pack_sides.1 = f32[2,2,16,16,128]{4,3,2,1,0:T(8,128)S(1)} custom-call(f32[2,16,32,128]{3,2,1,0:T(8,128)} %bitcast.24, f32[2,16,32,128]{3,2,1,0:T(8,128)} %bitcast.28), custom_call_target="tpu_custom_call" | custom-call | tf_op jit(solution)/shard_map/pack_sides/pallas_call | solution.py:179
  9.0 1.6 %collective-permute-start.4 = (f32[2,2,16,16,128]{4,3,2,1,0:T(8,128)S(1)}, f32[2,2,16,16,128]{4,3,2,1,0:T(8,128)S(1)}, u32[]{:S(2)}, u32[]{:S(2)}) collective-permute-start(f32[2,2,16,16,128]{4,3,2,1,0:T(8,128)S(1)} %pack_sides.1), channel_id=1, source_target_pairs={{0,1},{1,0},{2,3},{3,2},{4,5},{5,4},{6,7},{7,6},{8,9},{9,8},{10,11... | collective-permute-start | bytes 1572872 | tf_op jit(solution)/shard_map/ppermute | solution.py:539
  10.6 0.7 collective-permute-start.3
  11.2 4.8 %collective-permute-start.2 = (f32[2,16,32,128]{3,2,1,0:T(8,128)}, f32[2,16,32,128]{3,2,1,0:T(8,128)S(1)}, u32[]{:S(2)}, u32[]{:S(2)}) collective-permute-start(f32[2,16,32,128]{3,2,1,0:T(8,128)} %bitcast.26), channel_id=1, source_target_pairs={{0,2},{2,0},{4,6},{6,4},{1,3},{3,1},{5,7},{7,5},{8,10},{10,8},{12,... | collective-permute-start | bytes 1572872 | tf_op jit(solution)/shard_map/ppermute | solution.py:533
  16.0 1.5 %collective-permute-start = (s32[1]{0:T(128)}, s32[1]{0:T(128)}, u32[]{:S(2)}, u32[]{:S(2)}) collective-permute-start(s32[1]{0:T(128)} %param.10), channel_id=1, source_target_pairs={{0,16},{16,0},{1,17},{17,1},{2,18},{18,2},{3,19},{19,3},{4,20},{20... | collective-permute-start | bytes 20 | tf_op jit(solution)/shard_map/ppermute | solution.py:536
  17.5 2.3 %collective-permute-done.refs_1_ = s32[1]{0:T(128)} collective-permute-done((s32[1]{0:T(128)}, s32[1]{0:T(128)}, u32[]{:S(2)}, u32[]{:S(2)}) %collective-permute-start) | collective-permute-done | bytes 36 | tf_op jit(solution)/shard_map/ppermute | solution.py:536
  19.8 0.7 collective-permute-start.6
  20.5 0.8 collective-permute-done.1
  21.3 1.1 %collective-permute-start.5 = (f32[2,16,32,128]{3,2,1,0:T(8,128)}, f32[2,16,32,128]{3,2,1,0:T(8,128)S(1)}, u32[]{:S(2)}, u32[]{:S(2)}) collective-permute-start(f32[2,16,32,128]{3,2,1,0:T(8,128)} %bitcast.30), channel_id=1, source_target_pairs={{0,2},{2,0},{4,6},{6,4},{1,3},{3,1},{5,7},{7,5},{8,10},{10,8},{12,... | collective-permute-start | bytes 1572872 | tf_op jit(solution)/shard_map/ppermute | solution.py:542
  23.1 0.6 copy-done.4
  23.7 2.5 %pick_slices.1 = f32[8,2,32,128]{3,2,1,0:T(8,128)} custom-call(s32[16]{0:T(128)S(1)} %copy-done.4, s32[1]{0:T(128)S(6)} %copy.16.refs_0_, s32[1]{0:T(128)} %collective-permute-done.refs_1_, f32[8,2,32,128]{3,2,1,0:T(8,128)S(1)} %bitcast.19, f32[8,2,32,128]{3,2,1,0:T(8,128)S(1)} %bitcast.20), custom_call_target="tpu_custom_call" | custom-call | tf_op jit(solution)/shard_map/pick_slices/pallas_call | solution.py:106
  26.3 2.8 %collective-permute-done.2.first.refs_2_ = f32[2,16,32,128]{3,2,1,0:T(8,128)S(1)} collective-permute-done((f32[2,16,32,128]{3,2,1,0:T(8,128)}, f32[2,16,32,128]{3,2,1,0:T(8,128)S(1)}, u32[]{:S(2)}, u32[]{:S(2)}) %collective-permute-start.2) | collective-permute-done | bytes 524320 | tf_op jit(solution)/shard_map/ppermute | solution.py:533
  29.1 4.2 %all-to-all-start.1 = ((f32[16,32,128]{2,1,0:T(8,128)}), f32[16,32,128]{2,1,0:T(8,128)S(1)}, u32[]{:S(2)}, u32[]{:S(2)}) async-start(f32[16,32,128]{2,1,0:T(8,128)} %bitcast.6), calls=%async_computation.1 | async-start | bytes 524288 | tf_op jit(solution)/shard_map/all_to_all | solution.py:558
  33.4 0.6 collective-permute-start.7
  34.0 0.7 copy.14
  34.7 3.8 %list_receivers.1.refs_2_ = s32[788]{0:T(1024)S(1)} custom-call(s32[3,256]{1,0:T(4,128)S(1)} %bitcast.21), custom_call_target="tpu_custom_call" | custom-call | tf_op jit(solution)/shard_map/list_receivers/pallas_call | solution.py:74
  38.5 1.5 %collective-permute-done.5.first.refs_4_ = f32[2,16,32,128]{3,2,1,0:T(8,128)S(1)} collective-permute-done((f32[2,16,32,128]{3,2,1,0:T(8,128)}, f32[2,16,32,128]{3,2,1,0:T(8,128)S(1)}, u32[]{:S(2)}, u32[]{:S(2)}) %collective-permute-start.5) | collective-permute-done | bytes 524320 | tf_op jit(solution)/shard_map/ppermute | solution.py:542
  40.0 1.1 %collective-permute-done.7.refs_7_ = f32[2,2,11,16,128]{4,3,2,1,0:T(8,128)S(1)} collective-permute-done((f32[2,2,11,16,128]{4,3,2,1,0:T(8,128)S(1)}, f32[2,2,11,16,128]{4,3,2,1,0:T(8,128)S(1)}, u32[]{:S(2)}, u32[]{:S(2)}) %collective-permute-start.7) | collective-permute-done | bytes 360480 | tf_op jit(solution)/shard_map/ppermute | solution.py:549
  41.1 0.7 copy-done
  41.8 4.0 %all-to-all-done.1.refs_4_ = f32[16,32,128]{2,1,0:T(8,128)S(1)} async-done(((f32[16,32,128]{2,1,0:T(8,128)}), f32[16,32,128]{2,1,0:T(8,128)S(1)}, u32[]{:S(2)}, u32[]{:S(2)}) %all-to-all-start.1) | async-done | bytes 262176 | tf_op jit(solution)/shard_map/all_to_all | solution.py:558
  45.9 1.6 %collective-permute-start.8 = (f32[2,2,9,16,128]{4,3,2,1,0:T(8,128)S(1)}, f32[2,2,9,16,128]{4,3,2,1,0:T(8,128)}, u32[]{:S(2)}, u32[]{:S(2)}) collective-permute-start(f32[2,2,9,16,128]{4,3,2,1,0:T(8,128)S(1)} %pack_corners.3), channel_id=1, source_target_pairs={{0,1},{1,0},{2,3},{3,2},{4,5},{5,4},{6,7},{7,6},{8,9},{9,8},{10,11... | collective-permute-start | bytes 884744 | tf_op jit(solution)/shard_map/ppermute | solution.py:549
  47.5 1.4 %collective-permute-start.10 = (f32[16,32,128]{2,1,0:T(8,128)S(1)}, f32[16,32,128]{2,1,0:T(8,128)}, u32[]{:S(2)}, u32[]{:S(2)}) collective-permute-start(f32[16,32,128]{2,1,0:T(8,128)S(1)} %all-to-all-done.1.refs_4_), channel_id=1, source_target_pairs={{2,4},{4,2},{3,5},{5,3},{10,12},{12,10},{11,13},{13,11},{18,20},{2... | collective-permute-start | bytes 786440 | tf_op jit(solution)/shard_map/ppermute | solution.py:561
  48.8 1.4 %collective-permute-start.9 = (f32[16,32,128]{2,1,0:T(8,128)S(1)}, f32[16,32,128]{2,1,0:T(8,128)}, u32[]{:S(2)}, u32[]{:S(2)}) collective-permute-start(f32[16,32,128]{2,1,0:T(8,128)S(1)} %all-to-all-done.1.refs_4_), channel_id=1, source_target_pairs={{0,2},{2,0},{4,6},{6,4},{1,3},{3,1},{5,7},{7,5},{8,10},{10,8},{12,... | collective-permute-start | bytes 786440 | tf_op jit(solution)/shard_map/ppermute | solution.py:561
  50.3 0.7 collective-permute-start.13
  51.0 3.2 %collective-permute-start.12 = (f32[16,16,128]{2,1,0:T(8,128)S(1)}, f32[16,16,128]{2,1,0:T(8,128)S(1)}, u32[]{:S(2)}, u32[]{:S(2)}) collective-permute-start(f32[16,16,128]{2,1,0:T(8,128)S(1)} %constant_dynamic-slice_fusion), channel_id=1, source_target_pairs={{0,3},{1,2},{2,1},{3,0},{4,7},{5,6},{6,5},{7,4},{8,11},{9,10},{10,... | collective-permute-start | bytes 393224 | tf_op jit(solution)/shard_map/ppermute | solution.py:567
  54.5 1.5 %collective-permute-start.11 = (f32[16,16,128]{2,1,0:T(8,128)S(1)}, f32[16,16,128]{2,1,0:T(8,128)S(1)}, u32[]{:S(2)}, u32[]{:S(2)}) collective-permute-start(f32[16,16,128]{2,1,0:T(8,128)S(1)} %constant_dynamic-slice_fusion), channel_id=1, source_target_pairs={{0,1},{1,0},{2,3},{3,2},{4,5},{5,4},{6,7},{7,6},{8,9},{9,8},{10,11... | collective-permute-start | bytes 393224 | tf_op jit(solution)/shard_map/ppermute | solution.py:566
  56.0 1.0 %copy-done.1 = f32[2,2,11,16,128]{4,3,2,1,0:T(8,128)S(1)} copy-done((f32[2,2,11,16,128]{4,3,2,1,0:T(8,128)S(1)}, f32[2,2,11,16,128]{4,3,2,1,0:T(8,128)}, u32[]{:S(2)}) %copy-start.1) | copy-done | bytes 360472
  57.0 2.4 %assemble_fields.1.refs_3_ = f32[6,48,64,128]{3,2,1,0:T(8,128)S(1)} custom-call(f32[2,16,32,128]{3,2,1,0:T(8,128)} %bitcast.27, f32[2,16,32,128]{3,2,1,0:T(8,128)} %bitcast.31, f32[2,16,32,128]{3,2,1,0:T(8,128)S(1)} %collective-permute-done.2.first.refs_2_, f32[2,16,32,128]{3,2,1,0:T(8,128)S(1)} %collective-permute-done.3.second.refs_3_, ...), custom_call_target="tpu_custom_call" | custom-call | tf_op jit(solution)/shard_map/assemble_fields/pallas_call | solution.py:307
  60.0 16.0 %wave_window.1 = (f32[2,16,32,128]{3,2,1,0:T(8,128)}, f32[2,16,32,128]{3,2,1,0:T(8,128)}, f32[8,16,256]{2,1,0:T(8,128)S(1)}, f32[6,48,64,128]{3,2,1,0:T(8,128)S(1)}) custom-call(s32[2,3]{1,0:T(2,128)S(1)} %bitcast.22, f32[2,8]{1,0:T(2,128)S(1)} %bitcast.23, s32[788]{0:T(1024)S(1)} %list_receivers.1.refs_2_, ...), custom_call_target="tpu_custom_call", output_to_operand_aliasing={{3}: (3, {})} | custom-call | tf_op jit(solution)/shard_map/wave_window/pallas_call | solution.py:503
  76.0 11.5 %all_to_all.15 = f32[8,16,256]{2,1,0:T(8,128)S(1)} all-to-all(f32[8,16,256]{2,1,0:T(8,128)S(1)} %get-tuple-element.34), channel_id=1, replica_groups=mesh['sy'=2,'core'=2,'gx'=4,'gy'=2] {'gx','gy'}, dimensions={0} | all-to-all | bytes 262144 | tf_op jit(solution)/shard_map/all_to_all | solution.py:575
  87.5 0.6 reduce_sum.9
  (21 shorter events, 1.2 us)
Async XLA Ops:
  0.6 19.2 %all-to-all-start = ((f32[16,32,128]{2,1,0:T(8,128)}), f32[16,32,128]{2,1,0:T(8,128)S(1)}, u32[]{:S(2)}, u32[]{:S(2)}) async-start(f32[16,32,128]{2,1,0:T(8,128)} %param.8), calls=%async_computation | async-start | bytes 524288 | tf_op jit(solution)/shard_map/all_to_all | solution.py:532
  9.0 51.0 %copy-start.2 = (s32[1,2,3]{2,1,0:T(2,128)S(1)}, s32[1,2,3]{2,1,0:T(2,128)}, u32[]{:S(2)}) copy-start(s32[1,2,3]{2,1,0:T(2,128)} %param.13) | copy-start | bytes 76
  9.0 51.0 %copy-start.3 = (f32[1,2,8]{2,1,0:T(2,128)S(1)}, f32[1,2,8]{2,1,0:T(2,128)}, u32[]{:S(2)}) copy-start(f32[1,2,8]{2,1,0:T(2,128)} %param.14) | copy-start | bytes 196
  9.0 17.2 %collective-permute-start.4 = (f32[2,2,16,16,128]{4,3,2,1,0:T(8,128)S(1)}, f32[2,2,16,16,128]{4,3,2,1,0:T(8,128)S(1)}, u32[]{:S(2)}, u32[]{:S(2)}) collective-permute-start(f32[2,2,16,16,128]{4,3,2,1,0:T(8,128)S(1)} %pack_sides.1), channel_id=1, source_target_pairs={{0,1},{1,0},{2,3},{3,2},{4,5},{5,4},{6,7},{7,6},{8,9},{9,8},{10,11... | collective-permute-start | bytes 1572872 | tf_op jit(solution)/shard_map/ppermute | solution.py:539
  10.6 15.7 %collective-permute-start.3 = (f32[2,16,32,128]{3,2,1,0:T(8,128)}, f32[2,16,32,128]{3,2,1,0:T(8,128)S(1)}, u32[]{:S(2)}, u32[]{:S(2)}) collective-permute-start(f32[2,16,32,128]{3,2,1,0:T(8,128)} %bitcast.25), channel_id=1, source_target_pairs={{2,4},{4,2},{3,5},{5,3},{10,12},{12,10},{11,13},{13,11},{18,20},{2... | collective-permute-start | bytes 1572872 | tf_op jit(solution)/shard_map/ppermute | solution.py:533
  11.2 17.8 %collective-permute-start.2 = (f32[2,16,32,128]{3,2,1,0:T(8,128)}, f32[2,16,32,128]{3,2,1,0:T(8,128)S(1)}, u32[]{:S(2)}, u32[]{:S(2)}) collective-permute-start(f32[2,16,32,128]{3,2,1,0:T(8,128)} %bitcast.26), channel_id=1, source_target_pairs={{0,2},{2,0},{4,6},{6,4},{1,3},{3,1},{5,7},{7,5},{8,10},{10,8},{12,... | collective-permute-start | bytes 1572872 | tf_op jit(solution)/shard_map/ppermute | solution.py:533
  16.0 3.8 %collective-permute-start = (s32[1]{0:T(128)}, s32[1]{0:T(128)}, u32[]{:S(2)}, u32[]{:S(2)}) collective-permute-start(s32[1]{0:T(128)} %param.10), channel_id=1, source_target_pairs={{0,16},{16,0},{1,17},{17,1},{2,18},{18,2},{3,19},{19,3},{4,20},{20... | collective-permute-start | bytes 20 | tf_op jit(solution)/shard_map/ppermute | solution.py:536
  19.8 1.5 %collective-permute-start.1 = (f32[16,32,128]{2,1,0:T(8,128)S(1)}, f32[16,32,128]{2,1,0:T(8,128)S(1)}, u32[]{:S(2)}, u32[]{:S(2)}) collective-permute-start(f32[16,32,128]{2,1,0:T(8,128)S(1)} %all-to-all-done), channel_id=1, source_target_pairs={{0,8},{8,0},{1,9},{9,1},{2,10},{10,2},{3,11},{11,3},{4,12},{12,4},... | collective-permute-start | bytes 786440 | tf_op jit(solution)/shard_map/ppermute | solution.py:541
  19.8 18.7 %collective-permute-start.6 = (f32[2,16,32,128]{3,2,1,0:T(8,128)}, f32[2,16,32,128]{3,2,1,0:T(8,128)S(1)}, u32[]{:S(2)}, u32[]{:S(2)}) collective-permute-start(f32[2,16,32,128]{3,2,1,0:T(8,128)} %bitcast.29), channel_id=1, source_target_pairs={{2,4},{4,2},{3,5},{5,3},{10,12},{12,10},{11,13},{13,11},{18,20},{2... | collective-permute-start | bytes 1572872 | tf_op jit(solution)/shard_map/ppermute | solution.py:542
  21.3 18.7 %collective-permute-start.5 = (f32[2,16,32,128]{3,2,1,0:T(8,128)}, f32[2,16,32,128]{3,2,1,0:T(8,128)S(1)}, u32[]{:S(2)}, u32[]{:S(2)}) collective-permute-start(f32[2,16,32,128]{3,2,1,0:T(8,128)} %bitcast.30), channel_id=1, source_target_pairs={{0,2},{2,0},{4,6},{6,4},{1,3},{3,1},{5,7},{7,5},{8,10},{10,8},{12,... | collective-permute-start | bytes 1572872 | tf_op jit(solution)/shard_map/ppermute | solution.py:542
  23.1 0.7 copy-start.4
  29.1 16.7 %all-to-all-start.1 = ((f32[16,32,128]{2,1,0:T(8,128)}), f32[16,32,128]{2,1,0:T(8,128)S(1)}, u32[]{:S(2)}, u32[]{:S(2)}) async-start(f32[16,32,128]{2,1,0:T(8,128)} %bitcast.6), calls=%async_computation.1 | async-start | bytes 524288 | tf_op jit(solution)/shard_map/all_to_all | solution.py:558
  33.4 7.7 %collective-permute-start.7 = (f32[2,2,11,16,128]{4,3,2,1,0:T(8,128)S(1)}, f32[2,2,11,16,128]{4,3,2,1,0:T(8,128)S(1)}, u32[]{:S(2)}, u32[]{:S(2)}) collective-permute-start(f32[2,2,11,16,128]{4,3,2,1,0:T(8,128)S(1)} %pack_corners.2), channel_id=1, source_target_pairs={{0,1},{1,0},{2,3},{3,2},{4,5},{5,4},{6,7},{7,6},{8,9},{9,8},{10,11... | collective-permute-start | bytes 1081352 | tf_op jit(solution)/shard_map/ppermute | solution.py:549
  41.1 0.7 copy-start
  45.9 8.5 %collective-permute-start.8 = (f32[2,2,9,16,128]{4,3,2,1,0:T(8,128)S(1)}, f32[2,2,9,16,128]{4,3,2,1,0:T(8,128)}, u32[]{:S(2)}, u32[]{:S(2)}) collective-permute-start(f32[2,2,9,16,128]{4,3,2,1,0:T(8,128)S(1)} %pack_corners.3), channel_id=1, source_target_pairs={{0,1},{1,0},{2,3},{3,2},{4,5},{5,4},{6,7},{7,6},{8,9},{9,8},{10,11... | collective-permute-start | bytes 884744 | tf_op jit(solution)/shard_map/ppermute | solution.py:549
  47.5 12.5 %collective-permute-start.10 = (f32[16,32,128]{2,1,0:T(8,128)S(1)}, f32[16,32,128]{2,1,0:T(8,128)}, u32[]{:S(2)}, u32[]{:S(2)}) collective-permute-start(f32[16,32,128]{2,1,0:T(8,128)S(1)} %all-to-all-done.1.refs_4_), channel_id=1, source_target_pairs={{2,4},{4,2},{3,5},{5,3},{10,12},{12,10},{11,13},{13,11},{18,20},{2... | collective-permute-start | bytes 786440 | tf_op jit(solution)/shard_map/ppermute | solution.py:561
  48.8 11.2 %collective-permute-start.9 = (f32[16,32,128]{2,1,0:T(8,128)S(1)}, f32[16,32,128]{2,1,0:T(8,128)}, u32[]{:S(2)}, u32[]{:S(2)}) collective-permute-start(f32[16,32,128]{2,1,0:T(8,128)S(1)} %all-to-all-done.1.refs_4_), channel_id=1, source_target_pairs={{0,2},{2,0},{4,6},{6,4},{1,3},{3,1},{5,7},{7,5},{8,10},{10,8},{12,... | collective-permute-start | bytes 786440 | tf_op jit(solution)/shard_map/ppermute | solution.py:561
  50.3 9.1 %collective-permute-start.13 = (f32[16,16,128]{2,1,0:T(8,128)S(1)}, f32[16,16,128]{2,1,0:T(8,128)S(1)}, u32[]{:S(2)}, u32[]{:S(2)}) collective-permute-start(f32[16,16,128]{2,1,0:T(8,128)S(1)} %constant_dynamic-slice_fusion), channel_id=1, source_target_pairs={{2,5},{3,4},{4,3},{5,2},{10,13},{11,12},{12,11},{13,10},{18,21},{1... | collective-permute-start | bytes 393224 | tf_op jit(solution)/shard_map/ppermute | solution.py:567
  51.0 8.5 %collective-permute-start.12 = (f32[16,16,128]{2,1,0:T(8,128)S(1)}, f32[16,16,128]{2,1,0:T(8,128)S(1)}, u32[]{:S(2)}, u32[]{:S(2)}) collective-permute-start(f32[16,16,128]{2,1,0:T(8,128)S(1)} %constant_dynamic-slice_fusion), channel_id=1, source_target_pairs={{0,3},{1,2},{2,1},{3,0},{4,7},{5,6},{6,5},{7,4},{8,11},{9,10},{10,... | collective-permute-start | bytes 393224 | tf_op jit(solution)/shard_map/ppermute | solution.py:567
  54.5 5.5 %collective-permute-start.11 = (f32[16,16,128]{2,1,0:T(8,128)S(1)}, f32[16,16,128]{2,1,0:T(8,128)S(1)}, u32[]{:S(2)}, u32[]{:S(2)}) collective-permute-start(f32[16,16,128]{2,1,0:T(8,128)S(1)} %constant_dynamic-slice_fusion), channel_id=1, source_target_pairs={{0,1},{1,0},{2,3},{3,2},{4,5},{5,4},{6,7},{7,6},{8,9},{9,8},{10,11... | collective-permute-start | bytes 393224 | tf_op jit(solution)/shard_map/ppermute | solution.py:566
  56.0 1.0 %copy-start.1 = (f32[2,2,11,16,128]{4,3,2,1,0:T(8,128)S(1)}, f32[2,2,11,16,128]{4,3,2,1,0:T(8,128)}, u32[]{:S(2)}) copy-start(f32[2,2,11,16,128]{4,3,2,1,0:T(8,128)} %copy-done) | copy-start | bytes 1081348
